TPU v7x, 256 devices: a whole 4x4x8 slice. The times are simulated.
256 devices in a mesh: tm: 16 (over y, x), row: 2 (over core), col: 8 (over z).
Axes of the slice: x: 4, y: 4, z: 8, core: 2. Of those that a mesh axis runs over, the one named last changes fastest.
Arguments:
- latents: bfloat16 [64, 8, 256, 384], P('tm', 'row', 'col'), may hold values from -6 to 6
- norm_gain: float32 [384], replicated, may hold values from 0.1 to 1.9
- conv_weight: bfloat16 [3, 3, 3, 384, 384], replicated, may hold values from -0.0625 to 0.0625
- conv_bias: float32 [384], replicated, may hold values from -3 to 3
- time_weight: bfloat16 [3, 384, 768], replicated, may hold values from -0.1875 to 0.1875
- time_bias: float32 [768], replicated, may hold values from -3 to 3
- spatial_weight: bfloat16 [3, 3, 384, 192], replicated, may hold values from -0.109375 to 0.109375
- spatial_bias: float32 [192], replicated, may hold values from -3 to 3
Outputs:
- decoded: bfloat16 [128, 16, 512, 192], P('tm', 'row', 'col')
All inputs are finite; a program needn't handle non-finite values.
Results may differ from a plain program's by a relative error of at most 0.01.
Values may be sent and summed in bfloat16 or wider, within the bound.
No kernel may reach another device: no remote copies, remote signals or barrier semaphores. Data moves between devices by JAX's collectives and lax.ppermute only.
A program may use at most 128 MiB of HBM per device.

v0:
```python
import jax
import jax.numpy as jnp
from jax import lax
from jax.sharding import PartitionSpec as P


def from_behind(block, axis, distance):
    devices = range(lax.axis_size(axis))
    route = [(i - distance, i) for i in devices if i - distance in devices]
    return lax.ppermute(block, axis, route)


def with_halo(block, sides, width):
    for axis, dim in sides:
        count = lax.axis_size(axis)
        forward = [(i, i + 1) for i in range(count - 1)]
        backward = [(target, source) for source, target in forward]
        low = lax.ppermute(
            lax.slice_in_dim(block, block.shape[dim] - width, None, axis=dim), axis, forward
        )
        high = lax.ppermute(lax.slice_in_dim(block, 0, width, axis=dim), axis, backward)
        block = jnp.concatenate([low, block, high], axis=dim)
    return block


def normalize_silu(values, gain):
    scale = lax.rsqrt(jnp.mean(values * values, axis=-1, keepdims=True) + 1e-06)
    return jax.nn.silu(values * scale * gain)


def conv_cube(source, weight, frame_count, row_count, col_count):
    running = jnp.zeros((frame_count * row_count * col_count, weight.shape[-1]), jnp.float32)
    for step_time in range(3):
        for step_row in range(3):
            for step_col in range(3):
                slab_piece = source[
                    step_time : step_time + frame_count,
                    step_row : step_row + row_count,
                    step_col : step_col + col_count,
                ]
                running = running + jnp.dot(
                    slab_piece.reshape(-1, source.shape[-1]),
                    weight[step_time, step_row, step_col],
                    preferred_element_type=jnp.float32,
                )
    return running.reshape(frame_count, row_count, col_count, weight.shape[-1])


def conv_time(source, weight, frame_count):
    running = jnp.zeros(
        (frame_count * source.shape[1] * source.shape[2], weight.shape[-1]), jnp.float32
    )
    for step_time in range(3):
        slab_piece = source[step_time : step_time + frame_count].reshape(-1, source.shape[-1])
        running = running + jnp.dot(
            slab_piece, weight[step_time], preferred_element_type=jnp.float32
        )
    return running.reshape(frame_count, source.shape[1], source.shape[2], weight.shape[-1])


def split_halves(doubled):
    shape_in = doubled.shape
    halves = doubled.reshape(shape_in[0], shape_in[1], shape_in[2], 2, shape_in[3] // 2)
    return jnp.transpose(halves, (0, 3, 1, 2, 4)).reshape(
        2 * shape_in[0], shape_in[1], shape_in[2], shape_in[3] // 2
    )


def upsample_conv(framed, spatial_weight, spatial_bias, row_count, col_count):
    parity_taps = (((-1, (0,)), (0, (1, 2))), ((0, (0, 1)), (1, (2,))))
    kernel_full = spatial_weight.astype(jnp.float32)
    out_width = spatial_weight.shape[-1]
    frame_count = framed.shape[0]
    phases = []
    for parity_row in range(2):
        for parity_col in range(2):
            running = jnp.zeros((frame_count * row_count * col_count, out_width), jnp.float32)
            for offset_row, taps_row in parity_taps[parity_row]:
                for offset_col, taps_col in parity_taps[parity_col]:
                    summed = jnp.zeros(kernel_full.shape[2:], jnp.float32)
                    for tap_row in taps_row:
                        for tap_col in taps_col:
                            summed = summed + kernel_full[tap_row, tap_col]
                    high_part = summed.astype(jnp.bfloat16)
                    low_part = (summed - high_part.astype(jnp.float32)).astype(jnp.bfloat16)
                    paired = jnp.concatenate([high_part, low_part], axis=1)
                    slab_piece = framed[
                        :,
                        1 + offset_row : 1 + offset_row + row_count,
                        1 + offset_col : 1 + offset_col + col_count,
                    ]
                    product = jnp.dot(
                        slab_piece.reshape(-1, framed.shape[-1]),
                        paired,
                        preferred_element_type=jnp.float32,
                    )
                    running = running + product[:, :out_width] + product[:, out_width:]
            phases.append(running.reshape(frame_count, row_count, col_count, out_width))
    stacked = jnp.stack(phases, axis=0).reshape(2, 2, frame_count, row_count, col_count, out_width)
    woven = jnp.transpose(stacked, (2, 3, 0, 4, 1, 5)).reshape(
        frame_count, 2 * row_count, 2 * col_count, out_width
    )
    return (woven + spatial_bias).astype(jnp.bfloat16)


def on_device(
    latents, norm_gain, conv_weight, conv_bias, time_weight, time_bias, spatial_weight, spatial_bias
):
    frame_count, row_count, col_count, channels = latents.shape
    widened = latents.astype(jnp.float32)
    activated = normalize_silu(widened, norm_gain).astype(jnp.bfloat16)
    earlier = from_behind(activated[frame_count - 2 :], "tm", 1)
    joined = jnp.concatenate([earlier, activated], axis=0)
    extended = with_halo(joined, (("row", 1), ("col", 2)), 1)
    convolved = conv_cube(extended, conv_weight, frame_count, row_count, col_count)
    mixed = (convolved + conv_bias + widened).astype(jnp.bfloat16)
    earlier_mixed = from_behind(mixed[frame_count - 2 :], "tm", 1)
    mixed_ext = jnp.concatenate([earlier_mixed, mixed], axis=0)
    doubled = (conv_time(mixed_ext, time_weight, frame_count) + time_bias).astype(jnp.bfloat16)
    framed = with_halo(split_halves(doubled), (("row", 1), ("col", 2)), 1)
    return upsample_conv(framed, spatial_weight, spatial_bias, row_count, col_count)


def solution(mesh):
    placed = (P("tm", "row", "col", None), P(), P(), P(), P(), P(), P(), P())
    return jax.shard_map(
        on_device,
        mesh=mesh,
        in_specs=placed,
        out_specs=P("tm", "row", "col", None),
        check_vma=False,
    )
```

profile of v0, /device:TPU:104, one launch (start us, length us, event | category | flops | bytes accessed | tf_op | source)
XLA Modules:
  0.0 116.9 jit_solution(11018817019237071076)
XLA Ops:
  2.6 3.4 %collective-permute-start = (bf16[2,4,32,384]{3,2,1,0:T(8,128)(2,1)S(1)}, bf16[2,4,32,384]{3,2,1,0:T(8,128)(2,1)S(1)}, u32[]{:S(2)}, u32[]{:S(2)}) collective-permute-start(bf16[2,4,32,384]{3,2,1,0:T(8,128)(2,1)S(1)} %slice.531), channel_id=1, source_target_pairs={{0,16},{16,32},{32,48},{48,64},{64,80},{80,96},{96,112},{112,128},... | collective-permute-start | bytes 589832 | tf_op jit(solution)/shard_map/ppermute | solution.py:10
  8.3 1.4 %subtract_convert_fusion.7 = (bf16[384,192]{0,1:T(8,128)(2,1)}, bf16[384,192]{0,1:T(8,128)(2,1)}, f32[384,192]{0,1:T(8,128)S(1)}, bf16[384,192]{0,1:T(8,128)(2,1...) fusion(f32[3,3,384,192]{2,3,1,0:T(8,128)S(1)} %convert_element_, ...), kind=kLoop, calls=%fused_computation.210 | loop fusion | flops 2580480 | bytes 5013504 | tf_op jit(solution)/shard_map/convert_element_type | solution.py:85
  10.5 2.8 %collective-permute-done = bf16[2,4,32,384]{3,2,1,0:T(8,128)(2,1)S(1)} collective-permute-done((bf16[2,4,32,384]{3,2,1,0:T(8,128)(2,1)S(1)}, bf16[2,4,32,384]{3,2,1,0:T(8,128)(2,1)S(1)}, u32[]{:S(2)}, u32[]{:S(2)}) %collective-permute-start) | collective-permute-done | bytes 196640 | tf_op jit(solution)/shard_map/ppermute | solution.py:10
  18.0 5.0 %collective-permute-start.3 = (bf16[6,6,1,384]{3,2,1,0:T(2,128)(2,1)S(1)}, bf16[6,6,1,384]{3,2,1,0:T(2,128)(2,1)S(1)}, u32[]{:S(2)}, u32[]{:S(2)}) collective-permute-start(bf16[6,6,1,384]{3,2,1,0:T(2,128)(2,1)S(1)} %get-tuple-element.95), channel_id=1, source_target_pairs={{0,1},{1,2},{2,3},{3,4},{4,5},{5,6},{6,7},{8,9},{9,10},{10,11},{11... | collective-permute-start | bytes 82952 | tf_op jit(solution)/shard_map/ppermute | solution.py:18
  23.0 1.9 %collective-permute-start.4 = (bf16[6,6,1,384]{3,2,1,0:T(2,128)(2,1)S(1)}, bf16[6,6,1,384]{3,2,1,0:T(2,128)(2,1)S(1)}, u32[]{:S(2)}, u32[]{:S(2)}) collective-permute-start(bf16[6,6,1,384]{3,2,1,0:T(2,128)(2,1)S(1)} %get-tuple-element.96), channel_id=1, source_target_pairs={{1,0},{2,1},{3,2},{4,3},{5,4},{6,5},{7,6},{9,8},{10,9},{11,10},{12... | collective-permute-start | bytes 82952 | tf_op jit(solution)/shard_map/ppermute | solution.py:21
  26.8 3.5 %collective-permute-done.4 = bf16[6,6,1,384]{3,2,1,0:T(2,128)(2,1)S(1)} collective-permute-done((bf16[6,6,1,384]{3,2,1,0:T(2,128)(2,1)S(1)}, bf16[6,6,1,384]{3,2,1,0:T(2,128)(2,1)S(1)}, u32[]{:S(2)}, u32[]{:S(2)}) %collective-permute-start.4) | collective-permute-done | bytes 27680 | tf_op jit(solution)/shard_map/ppermute | solution.py:21
  44.5 2.1 %collective-permute-start.5 = (bf16[2,4,32,384]{3,2,1,0:T(8,128)(2,1)S(1)}, bf16[2,4,32,384]{3,2,1,0:T(8,128)(2,1)S(1)}, u32[]{:S(2)}, u32[]{:S(2)}) collective-permute-start(bf16[2,4,32,384]{3,2,1,0:T(8,128)(2,1)S(1)} %slice.562), channel_id=1, source_target_pairs={{0,16},{16,32},{32,48},{48,64},{64,80},{80,96},{96,112},{112,128},... | collective-permute-start | bytes 589832 | tf_op jit(solution)/shard_map/ppermute | solution.py:10
  47.2 7.0 %collective-permute-done.5 = bf16[2,4,32,384]{3,2,1,0:T(8,128)(2,1)S(1)} collective-permute-done((bf16[2,4,32,384]{3,2,1,0:T(8,128)(2,1)S(1)}, bf16[2,4,32,384]{3,2,1,0:T(8,128)(2,1)S(1)}, u32[]{:S(2)}, u32[]{:S(2)}) %collective-permute-start.5) | collective-permute-done | bytes 196640 | tf_op jit(solution)/shard_map/ppermute | solution.py:10
  60.0 1.8 %fusion.45 = f32[1024,384]{0,1:T(8,128)} fusion(bf16[1024,384]{1,0:T(8,128)(2,1)S(1)} %bitcast.367, bf16[384,192]{0,1:T(8,128)(2,1)S(1)} %copy-done.40, bf16[384,192]{0,1:T(8,128)(2,1)S(1)} %copy-done.41), kind=kOutput, calls=%fused_computation.132 | convolution fusion | flops 302579712 | bytes 2654208 | tf_op jit(solution)/shard_map/dot_general | solution.py:92
  61.8 1.8 %fusion.57 = f32[1024,384]{0,1:T(8,128)} fusion(bf16[1024,384]{1,0:T(8,128)(2,1)S(1)} %bitcast.368, bf16[384,192]{0,1:T(8,128)(2,1)S(1)} %copy-done.36, bf16[384,192]{0,1:T(8,128)(2,1)S(1)} %copy-done.37), kind=kOutput, calls=%fused_computation.144 | convolution fusion | flops 302579712 | bytes 2654208 | tf_op jit(solution)/shard_map/dot_general | solution.py:92
  63.5 1.8 %fusion.69 = f32[1024,384]{0,1:T(8,128)} fusion(bf16[1024,384]{1,0:T(8,128)(2,1)S(1)} %bitcast.369, bf16[384,192]{0,1:T(8,128)(2,1)S(1)} %copy-done.34, bf16[384,192]{0,1:T(8,128)(2,1)S(1)} %copy-done.35), kind=kOutput, calls=%fused_computation.156 | convolution fusion | flops 302579712 | bytes 2654208 | tf_op jit(solution)/shard_map/dot_general | solution.py:92
  65.5 2.4 %collective-permute-start.8 = (bf16[8,6,1,384]{3,2,1,0:T(2,128)(2,1)S(1)}, bf16[8,6,1,384]{3,2,1,0:T(2,128)(2,1)S(1)}, u32[]{:S(2)}, u32[]{:S(2)}) collective-permute-start(bf16[8,6,1,384]{3,2,1,0:T(2,128)(2,1)S(1)} %get-tuple-element.73), channel_id=1, source_target_pairs={{0,1},{1,2},{2,3},{3,4},{4,5},{5,6},{6,7},{8,9},{9,10},{10,11},{11... | collective-permute-start | bytes 110600 | tf_op jit(solution)/shard_map/ppermute | solution.py:18
  67.9 3.6 %collective-permute-start.9 = (bf16[8,6,1,384]{3,2,1,0:T(2,128)(2,1)S(1)}, bf16[8,6,1,384]{3,2,1,0:T(2,128)(2,1)S(1)}, u32[]{:S(2)}, u32[]{:S(2)}) collective-permute-start(bf16[8,6,1,384]{3,2,1,0:T(2,128)(2,1)S(1)} %get-tuple-element.74), channel_id=1, source_target_pairs={{1,0},{2,1},{3,2},{4,3},{5,4},{6,5},{7,6},{9,8},{10,9},{11,10},{12... | collective-permute-start | bytes 110600 | tf_op jit(solution)/shard_map/ppermute | solution.py:21
  72.3 1.9 %fusion.37 = f32[1024,384]{0,1:T(8,128)} fusion(bf16[1024,384]{1,0:T(8,128)(2,1)S(1)} %bitcast.384, bf16[384,192]{0,1:T(8,128)(2,1)S(1)} %copy-done.26, bf16[384,192]{0,1:T(8,128)(2,1)S(1)} %copy-done.27), kind=kOutput, calls=%fused_computation.124 | convolution fusion | flops 302579712 | bytes 2654208 | tf_op jit(solution)/shard_map/dot_general | solution.py:92
  74.2 1.8 %fusion.65 = f32[1024,384]{0,1:T(8,128)} fusion(bf16[1024,384]{1,0:T(8,128)(2,1)S(1)} %bitcast.381, bf16[384,192]{0,1:T(8,128)(2,1)S(1)} %copy-done.30, bf16[384,192]{0,1:T(8,128)(2,1)S(1)} %copy-done.31), kind=kOutput, calls=%fused_computation.152 | convolution fusion | flops 302579712 | bytes 2654208 | tf_op jit(solution)/shard_map/dot_general | solution.py:92
  76.0 1.7 %fusion.77 = f32[1024,384]{0,1:T(8,128)} fusion(bf16[1024,384]{1,0:T(8,128)(2,1)S(1)} %bitcast.382, bf16[384,192]{0,1:T(8,128)(2,1)S(1)} %copy-done.28, bf16[384,192]{0,1:T(8,128)(2,1)S(1)} %copy-done.29), kind=kOutput, calls=%fused_computation.164 | convolution fusion | flops 302579712 | bytes 2654208 | tf_op jit(solution)/shard_map/dot_general | solution.py:92
  83.3 1.5 %fusion.194 = (bf16[8,4,32,384]{3,2,1,0:T(8,128)(2,1)S(1)}, bf16[8,4,32,384]{3,2,1,0:T(8,128)(2,1)}, bf16[8,4,32,384]{3,2,1,0:T(8,128)(2,1)S(1)}) fusion(bf16[8,6,33,384]{3,2,1,0:T(8,128)(2,1)S(1)} %get-tuple-element.72), kind=kLoop, calls=%fused_computation.295 | loop fusion | bytes 4718592 | tf_op jit(solution)/shard_map/slice | solution.py:87
  88.8 1.7 %fusion.53 = f32[1024,384]{0,1:T(8,128)S(1)} fusion(bf16[1024,384]{1,0:T(8,128)(2,1)S(1)} %bitcast.378, bf16[384,192]{0,1:T(8,128)(2,1)} %get-tuple-element.23, bf16[384,192]{0,1:T(8,128)(2,1)} %get-tuple-element.24), kind=kOutput, calls=%fused_computation.140 | convolution fusion | flops 302579712 | bytes 2654208 | tf_op jit(solution)/shard_map/dot_general | solution.py:92
  95.2 1.6 %slice_add_fusion = f32[1024,192]{0,1:T(8,128)} fusion(f32[1024,384]{0,1:T(8,128)S(1)} %fusion.81, f32[1024,384]{0,1:T(8,128)S(1)} %copy-done.3, f32[1024,384]{0,1:T(8,128)S(1)} %fusion.73, f32[1024,384]{0,1:T(8,128)S(1)} %copy-done), kind=kLoop, calls=%fused_computation.50 | loop fusion | flops 1376256 | bytes 7077888 | tf_op jit(solution)/shard_map/add | solution.py:97
  96.8 2.5 %copy.14 = f32[1024,192]{1,0:T(8,128)} copy(f32[1024,192]{0,1:T(8,128)} %slice_add_fusion) | data formatting | bytes 1572864 | tf_op jit(solution)/shard_map/add | solution.py:97
  99.3 1.6 %pad_maximum_fusion = f32[4,8,4,32,192]{4,3,2,1,0:T(8,128)S(1)} fusion(f32[1,8,4,32,192]{4,3,2,1,0:T(8,128)} %bitcast.389, f32[1,8,4,32,192]{4,3,2,1,0:T(8,128)S(1)} %bitcast.388, f32[1,8,4,32,192]{4,3,2,1,0:T(8,128)S(1)} %bitcast.387, f32[1,8,4,32,192]{4,3,2,1,0:T(8,128)S(1)} %bitcast.386), kind=kLoop, calls=%fused_computation | loop fusion | flops 2359296 | bytes 6291456 | tf_op jit(solution)/shard_map/stack | solution.py:99
  100.9 5.8 %copy.15 = f32[8,4,2,32,2,192]{5,4,3,2,1,0:T(2,128)} copy(f32[8,4,2,32,2,192]{5,3,1,0,4,2:T(8,128)S(1)} %bitcast.374) | data formatting | bytes 6291456 | tf_op jit(solution)/shard_map/transpose | solution.py:100
  106.7 6.1 %reshape.191 = f32[8,8,64,192]{3,2,1,0:T(8,128)} reshape(f32[8,4,2,32,2,192]{5,4,3,2,1,0:T(2,128)} %copy.15) | data formatting | bytes 6291456 | tf_op jit(solution)/shard_map/reshape | solution.py:100
  112.8 4.1 %add_convert_fusion = bf16[8,8,64,192]{3,2,1,0:T(8,128)(2,1)} fusion(f32[8,8,64,192]{3,2,1,0:T(8,128)} %reshape.191, f32[192]{0:T(256)S(1)} %copy-done.44), kind=kLoop, calls=%fused_computation.1 | loop fusion | flops 1572864 | bytes 4719360 | tf_op jit(solution)/shard_map/convert_element_type | solution.py:103
  (178 shorter events, 47.3 us)
Async XLA Ops:
  0.0 6.0 %copy-start.13 = (bf16[3,3,384,192]{2,3,1,0:T(8,128)(2,1)S(1)}, bf16[3,3,384,192]{2,3,1,0:T(8,128)(2,1)}, u32[]{:S(2)}) copy-start(bf16[3,3,384,192]{2,3,1,0:T(8,128)(2,1)} %param.14) | copy-start | bytes 3981316
  2.6 10.6 %collective-permute-start = (bf16[2,4,32,384]{3,2,1,0:T(8,128)(2,1)S(1)}, bf16[2,4,32,384]{3,2,1,0:T(8,128)(2,1)S(1)}, u32[]{:S(2)}, u32[]{:S(2)}) collective-permute-start(bf16[2,4,32,384]{3,2,1,0:T(8,128)(2,1)S(1)} %slice.531), channel_id=1, source_target_pairs={{0,16},{16,32},{32,48},{48,64},{64,80},{80,96},{96,112},{112,128},... | collective-permute-start | bytes 589832 | tf_op jit(solution)/shard_map/ppermute | solution.py:10
  8.3 8.3 %copy-start.42 = (f32[768]{0:T(1024)S(1)}, f32[768]{0:T(1024)}, u32[]{:S(2)}) copy-start(f32[768]{0:T(1024)} %param.13) | copy-start | bytes 9220
  13.3 3.4 %collective-permute-start.1 = (bf16[6,1,32,384]{3,2,1,0:T(8,128)(2,1)S(1)}, bf16[6,1,32,384]{3,2,1,0:T(8,128)(2,1)S(1)}, u32[]{:S(2)}, u32[]{:S(2)}) collective-permute-start(bf16[6,1,32,384]{3,2,1,0:T(8,128)(2,1)S(1)} %get-tuple-element.113), channel_id=1, source_target_pairs={{0,8},{1,9},{2,10},{3,11},{4,12},{5,13},{6,14},{7,15},{16,24},{17,... | collective-permute-start | bytes 442376 | tf_op jit(solution)/shard_map/ppermute | solution.py:18
  14.6 3.3 %collective-permute-start.2 = (bf16[6,1,32,384]{3,2,1,0:T(8,128)(2,1)S(1)}, bf16[6,1,32,384]{3,2,1,0:T(8,128)(2,1)S(1)}, u32[]{:S(2)}, u32[]{:S(2)}) collective-permute-start(bf16[6,1,32,384]{3,2,1,0:T(8,128)(2,1)S(1)} %get-tuple-element.114), channel_id=1, source_target_pairs={{8,0},{9,1},{10,2},{11,3},{12,4},{13,5},{14,6},{15,7},{24,16},{25,... | collective-permute-start | bytes 442376 | tf_op jit(solution)/shard_map/ppermute | solution.py:21
  18.0 8.8 %collective-permute-start.3 = (bf16[6,6,1,384]{3,2,1,0:T(2,128)(2,1)S(1)}, bf16[6,6,1,384]{3,2,1,0:T(2,128)(2,1)S(1)}, u32[]{:S(2)}, u32[]{:S(2)}) collective-permute-start(bf16[6,6,1,384]{3,2,1,0:T(2,128)(2,1)S(1)} %get-tuple-element.95), channel_id=1, source_target_pairs={{0,1},{1,2},{2,3},{3,4},{4,5},{5,6},{6,7},{8,9},{9,10},{10,11},{11... | collective-permute-start | bytes 82952 | tf_op jit(solution)/shard_map/ppermute | solution.py:18
  23.0 7.3 %collective-permute-start.4 = (bf16[6,6,1,384]{3,2,1,0:T(2,128)(2,1)S(1)}, bf16[6,6,1,384]{3,2,1,0:T(2,128)(2,1)S(1)}, u32[]{:S(2)}, u32[]{:S(2)}) collective-permute-start(bf16[6,6,1,384]{3,2,1,0:T(2,128)(2,1)S(1)} %get-tuple-element.96), channel_id=1, source_target_pairs={{1,0},{2,1},{3,2},{4,3},{5,4},{6,5},{7,6},{9,8},{10,9},{11,10},{12... | collective-permute-start | bytes 82952 | tf_op jit(solution)/shard_map/ppermute | solution.py:21
  44.5 9.7 %collective-permute-start.5 = (bf16[2,4,32,384]{3,2,1,0:T(8,128)(2,1)S(1)}, bf16[2,4,32,384]{3,2,1,0:T(8,128)(2,1)S(1)}, u32[]{:S(2)}, u32[]{:S(2)}) collective-permute-start(bf16[2,4,32,384]{3,2,1,0:T(8,128)(2,1)S(1)} %slice.562), channel_id=1, source_target_pairs={{0,16},{16,32},{32,48},{48,64},{64,80},{80,96},{96,112},{112,128},... | collective-permute-start | bytes 589832 | tf_op jit(solution)/shard_map/ppermute | solution.py:10
  56.5 3.5 %copy-start.40 = (bf16[384,192]{0,1:T(8,128)(2,1)S(1)}, bf16[384,192]{0,1:T(8,128)(2,1)}, u32[]{:S(2)}) copy-start(bf16[384,192]{0,1:T(8,128)(2,1)} %get-tuple-element.19) | copy-start | bytes 442372
  56.6 8.8 %collective-permute-start.6 = (bf16[8,1,32,384]{3,2,1,0:T(8,128)(2,1)S(1)}, bf16[8,1,32,384]{3,2,1,0:T(8,128)(2,1)S(1)}, u32[]{:S(2)}, u32[]{:S(2)}) collective-permute-start(bf16[8,1,32,384]{3,2,1,0:T(8,128)(2,1)S(1)} %get-tuple-element.99), channel_id=1, source_target_pairs={{0,8},{1,9},{2,10},{3,11},{4,12},{5,13},{6,14},{7,15},{16,24},{17,... | collective-permute-start | bytes 589832 | tf_op jit(solution)/shard_map/ppermute | solution.py:18
  58.0 7.3 %collective-permute-start.7 = (bf16[8,1,32,384]{3,2,1,0:T(8,128)(2,1)S(1)}, bf16[8,1,32,384]{3,2,1,0:T(8,128)(2,1)S(1)}, u32[]{:S(2)}, u32[]{:S(2)}) collective-permute-start(bf16[8,1,32,384]{3,2,1,0:T(8,128)(2,1)S(1)} %get-tuple-element.100), channel_id=1, source_target_pairs={{8,0},{9,1},{10,2},{11,3},{12,4},{13,5},{14,6},{15,7},{24,16},{25,... | collective-permute-start | bytes 589832 | tf_op jit(solution)/shard_map/ppermute | solution.py:21
  60.0 3.6 %copy-start.34 = (bf16[384,192]{0,1:T(8,128)(2,1)S(1)}, bf16[384,192]{0,1:T(8,128)(2,1)}, u32[]{:S(2)}) copy-start(bf16[384,192]{0,1:T(8,128)(2,1)} %get-tuple-element.63) | copy-start | bytes 442372
  60.0 3.6 %copy-start.35 = (bf16[384,192]{0,1:T(8,128)(2,1)S(1)}, bf16[384,192]{0,1:T(8,128)(2,1)}, u32[]{:S(2)}) copy-start(bf16[384,192]{0,1:T(8,128)(2,1)} %get-tuple-element.64) | copy-start | bytes 442372
  65.3 6.3 %copy-start.32 = (bf16[384,192]{0,1:T(8,128)(2,1)S(1)}, bf16[384,192]{0,1:T(8,128)(2,1)}, u32[]{:S(2)}) copy-start(bf16[384,192]{0,1:T(8,128)(2,1)} %get-tuple-element.7) | copy-start | bytes 442372
  65.3 6.3 %copy-start.33 = (bf16[384,192]{0,1:T(8,128)(2,1)S(1)}, bf16[384,192]{0,1:T(8,128)(2,1)}, u32[]{:S(2)}) copy-start(bf16[384,192]{0,1:T(8,128)(2,1)} %get-tuple-element.8) | copy-start | bytes 442372
  65.5 12.2 %collective-permute-start.8 = (bf16[8,6,1,384]{3,2,1,0:T(2,128)(2,1)S(1)}, bf16[8,6,1,384]{3,2,1,0:T(2,128)(2,1)S(1)}, u32[]{:S(2)}, u32[]{:S(2)}) collective-permute-start(bf16[8,6,1,384]{3,2,1,0:T(2,128)(2,1)S(1)} %get-tuple-element.73), channel_id=1, source_target_pairs={{0,1},{1,2},{2,3},{3,4},{4,5},{5,6},{6,7},{8,9},{9,10},{10,11},{11... | collective-permute-start | bytes 110600 | tf_op jit(solution)/shard_map/ppermute | solution.py:18
  67.9 4.4 %copy-start.26 = (bf16[384,192]{0,1:T(8,128)(2,1)S(1)}, bf16[384,192]{0,1:T(8,128)(2,1)}, u32[]{:S(2)}) copy-start(bf16[384,192]{0,1:T(8,128)(2,1)} %get-tuple-element.48) | copy-start | bytes 442372
  67.9 4.4 %copy-start.27 = (bf16[384,192]{0,1:T(8,128)(2,1)S(1)}, bf16[384,192]{0,1:T(8,128)(2,1)}, u32[]{:S(2)}) copy-start(bf16[384,192]{0,1:T(8,128)(2,1)} %get-tuple-element.49) | copy-start | bytes 442372
  67.9 9.8 %collective-permute-start.9 = (bf16[8,6,1,384]{3,2,1,0:T(2,128)(2,1)S(1)}, bf16[8,6,1,384]{3,2,1,0:T(2,128)(2,1)S(1)}, u32[]{:S(2)}, u32[]{:S(2)}) collective-permute-start(bf16[8,6,1,384]{3,2,1,0:T(2,128)(2,1)S(1)} %get-tuple-element.74), channel_id=1, source_target_pairs={{1,0},{2,1},{3,2},{4,3},{5,4},{6,5},{7,6},{9,8},{10,9},{11,10},{12... | collective-permute-start | bytes 110600 | tf_op jit(solution)/shard_map/ppermute | solution.py:21
  72.3 3.7 %copy-start.28 = (bf16[384,192]{0,1:T(8,128)(2,1)S(1)}, bf16[384,192]{0,1:T(8,128)(2,1)}, u32[]{:S(2)}) copy-start(bf16[384,192]{0,1:T(8,128)(2,1)} %get-tuple-element.59) | copy-start | bytes 442372
  72.3 3.6 %copy-start.29 = (bf16[384,192]{0,1:T(8,128)(2,1)S(1)}, bf16[384,192]{0,1:T(8,128)(2,1)}, u32[]{:S(2)}) copy-start(bf16[384,192]{0,1:T(8,128)(2,1)} %get-tuple-element.60) | copy-start | bytes 442372
  95.2 4.1 %copy-start.7 = (f32[1024,192]{1,0:T(8,128)S(1)}, f32[1024,192]{1,0:T(8,128)}, u32[]{:S(2)}) copy-start(f32[1024,192]{1,0:T(8,128)} %copy.12) | copy-start | bytes 2359300
  95.2 4.1 %copy-start.8 = (f32[1024,192]{1,0:T(8,128)S(1)}, f32[1024,192]{1,0:T(8,128)}, u32[]{:S(2)}) copy-start(f32[1024,192]{1,0:T(8,128)} %copy.13) | copy-start | bytes 2359300
  106.7 6.2 %copy-start.44 = (f32[192]{0:T(256)S(1)}, f32[192]{0:T(256)}, u32[]{:S(2)}) copy-start(f32[192]{0:T(256)} %param.15) | copy-start | bytes 2308
  (33 other events, 65.0 us)
where the time goes:
time: 118 us; the launch traced here: 117 us
  matrix products  31 us (26%)
  local copies, waits for them, and re-layouts  27.1 us (23%)
  starting transfers between devices  23.7 us (20%)
  other arithmetic  19.7 us (17%)
  waiting for transfers between devices  14.3 us (12%)
    dot_general x16, matrix products, upsample_conv(): jnp.dot(slab_piece.reshape(-1, framed.shape[-1]), paired, preferred_eleme...  17.8 us
    dot_general x27, matrix products, conv_cube(): jnp.dot(slab_piece.reshape(-1, source.shape[-1]), weight[step_time, step_...  11.5 us
    ppermute x4, starting transfers between devices, with_halo(): lax.ppermute(lax.slice_in_dim(block, block.shape[dim] - width, None, axis...  10.2 us
    ppermute x2, waiting for transfers between devices, from_behind(): return lax.ppermute(block, axis, route)  9.74 us
    ppermute x4, starting transfers between devices, with_halo(): lax.ppermute(lax.slice_in_dim(block, 0, width, axis=dim), axis, backward)  8.07 us
    add x4, local copies, waits for them, and re-layouts, upsample_conv(): running = running + product[:, :out_width] + product[:, out_width:]  6.48 us
    reshape x1, local copies, waits for them, and re-layouts, upsample_conv(): jnp.transpose(stacked, (2, 3, 0, 4, 1, 5))  6.15 us
    transpose x1, local copies, waits for them, and re-layouts, upsample_conv(): jnp.transpose(stacked, (2, 3, 0, 4, 1, 5))  5.76 us
  transfers between devices with their start and end apart: 10, of which 4 were waited for; matrix products, arithmetic and copies ran while one was open for 17% of the time, Pallas kernels for 0%

commit v1 on v0

v1 whole, which is shorter than its diff:
```python
import jax
import jax.numpy as jnp
from jax import lax
from jax.experimental import pallas as pl
from jax.experimental.pallas import tpu as pltpu
from jax.sharding import PartitionSpec as P

F32 = jnp.float32
BF16 = jnp.bfloat16
HBM = pl.BlockSpec(memory_space=pltpu.HBM)
VMEM = pl.BlockSpec(memory_space=pltpu.VMEM)

C = 384
OUTC = 192
WIDE = 256
W = 32
OWN = 4
MROWS = 5
SIDE = 16
BLOCK = MROWS * W + SIDE
LIMIT = 24


def activate(values, gain):
    scale = lax.rsqrt(jnp.mean(values * values, axis=-1, keepdims=True) + 1e-06)
    half = values * scale * (0.5 * gain)
    return half + half * jnp.tanh(half)


def dot(left, right):
    return jnp.dot(left, right, preferred_element_type=F32)


def moved_columns(values, left, right):
    place = lax.broadcasted_iota(jnp.int32, values.shape, 0)
    before = jnp.where(place == 0, left, pltpu.roll(values, 1, 0))
    after = jnp.where(place == W - 1, right, pltpu.roll(values, W - 1, 0))
    return before.astype(BF16), values.astype(BF16), after.astype(BF16)


def slot_order(rows, core):
    place = lax.broadcasted_iota(jnp.int32, rows.shape, 0)
    upper = jnp.where(place == 0, 0.0, pltpu.roll(rows, 1, 0))
    lower = jnp.where(place >= 6, 0.0, pltpu.roll(rows, 6, 0))
    return jnp.where(core == 0, upper, lower)


def edge_kernel(own, other, edge, held):
    core = lax.axis_index("row")
    start = pl.multiple_of(core * 16, 16)
    for frame in range(4):
        for source, first in ((own, core * OWN), (other, OWN - core * OWN)):
            for row in range(OWN):
                values = source[frame, row, pl.ds(start, 16), :].astype(F32)
                values = jnp.where(core == 0, values, pltpu.roll(values, 2, 0))
                for col in range(2):
                    held[2 * frame + col, pl.ds(first + row, 1), :] = values[col : col + 1]
    for frame in range(4):
        for col in range(2):
            edge[frame, col] = held[2 * frame + col].astype(BF16)


def activate_kernel(own, other, gain, activated, edges):
    core = lax.axis_index("row")
    scale = gain[...].reshape(1, C)
    edges[...] = jnp.zeros(edges.shape, F32)

    def one(frame, carry):
        for slot in range(MROWS + 2):
            if slot == 0:
                values = other[frame, 2].astype(F32) * core.astype(F32)
            elif slot == 1:
                values = jnp.where(core == 0, own[frame, 0], other[frame, 3]).astype(F32)
            elif slot == 5:
                values = jnp.where(core == 0, other[frame, 0], own[frame, 3]).astype(F32)
            elif slot == 6:
                values = other[frame, 1].astype(F32) * (1 - core).astype(F32)
            else:
                values = own[frame, slot - 1 - core].astype(F32)
            values = activate(values, scale)
            edges[frame, 0, slot : slot + 1, :] = values[0:1]
            edges[frame, 1, slot : slot + 1, :] = values[W - 1 : W]
            activated[frame, slot] = values.astype(BF16)
        return carry

    lax.fori_loop(0, 4, one, 0)


def halo_columns(frame, mine, theirs, core):
    columns = []
    for col in range(4):
        first, second = (theirs, mine) if col < 2 else (mine, theirs)
        rows = jnp.where(core == 0, first[frame, col % 2], second[frame, col % 2]).astype(F32)
        columns.append(slot_order(rows, core))
    return columns


def fill_patches(frame, activated, edges, mine, theirs, gain, core, patches, line):
    columns = [activate(one, gain) for one in halo_columns(frame, mine, theirs, core)]
    line[frame, 0] = columns[1]
    line[frame, 1] = columns[2]
    at = frame * BLOCK
    for slot in range(MROWS + 2):
        moved = moved_columns(
            activated[frame, slot].astype(F32),
            line[frame, 0, slot : slot + 1, :],
            line[frame, 1, slot : slot + 1, :],
        )
        for tap_row in range(3):
            out_row = slot - tap_row
            if 0 <= out_row < MROWS:
                for tap_col in range(3):
                    tap = tap_row * 3 + tap_col
                    patches[at + out_row * W : at + (out_row + 1) * W, tap * C : (tap + 1) * C] = (
                        moved[tap_col]
                    )
    low = [columns[0], columns[1], edges[frame, 0]]
    high = [edges[frame, 1], columns[2], columns[3]]
    for tap_row in range(3):
        for tap_col in range(3):
            tap = tap_row * 3 + tap_col
            pair = [low[tap_col], high[tap_col]]
            if tap_row:
                pair = [pltpu.roll(one, 8 - tap_row, 0) for one in pair]
            patches[at + MROWS * W : at + BLOCK, tap * C : (tap + 1) * C] = jnp.concatenate(
                pair, axis=0
            ).astype(BF16)


def step_weight(weight, step):
    return weight[step].reshape(9 * C, C)


def send_kernel(
    activated, edges, mine, theirs, gain, weight, patches, onward, crossing, line
):
    core = lax.axis_index("row")
    scale = gain[...].reshape(1, C)
    for frame in (2, 3):
        fill_patches(frame, activated, edges, mine, theirs, scale, core, patches, line)
    both = jnp.concatenate([step_weight(weight, 0), step_weight(weight, 1)], axis=1)
    total = dot(patches[2 * BLOCK :], both)
    onward[0] = (total[:BLOCK, :C] + total[BLOCK:, C:]).astype(BF16)
    onward[1] = total[BLOCK:, :C].astype(BF16)
    crossing[...] = total[:BLOCK, C:]
    for frame in (0, 1):
        fill_patches(frame, activated, edges, mine, theirs, scale, core, patches, line)


def base_rows(frame, own, other, mine, theirs, bias, core):
    rows = []
    for out_row in range(MROWS):
        if out_row == 0:
            values = jnp.where(core == 0, own[frame, 0], other[frame, 3])
        elif out_row == OWN:
            values = jnp.where(core == 0, other[frame, 0], own[frame, 3])
        else:
            values = own[frame, out_row - core]
        rows.append(values.astype(F32) + bias)
    columns = halo_columns(frame, mine, theirs, core)
    rows.append(pltpu.roll(columns[1], 7, 0) + bias)
    rows.append(pltpu.roll(columns[2], 7, 0) + bias)
    return jnp.concatenate(rows, axis=0)


def own_kernel(
    patches, weight, crossing, own, other, mine, theirs, bias, mixed, early, late
):
    core = lax.axis_index("row")
    shift = bias[...].reshape(1, C)
    early[...] = dot(patches[: 2 * BLOCK], step_weight(weight, 0))
    late[...] = dot(patches[2 * BLOCK :], step_weight(weight, 2))
    middle = dot(patches[BLOCK : 2 * BLOCK], step_weight(weight, 1))
    third = base_rows(2, own, other, mine, theirs, shift, core)
    fourth = base_rows(3, own, other, mine, theirs, shift, core)
    mixed[0] = (third + early[:BLOCK] + late[:BLOCK] + middle).astype(BF16)
    mixed[1] = (fourth + early[BLOCK:] + late[BLOCK:] + crossing[...]).astype(BF16)


def upsampled(doubled, spatial, bias, last_col, framed, woven, out, target, frame0, sems):
    core = lax.axis_index("row")
    col = lax.axis_index("col")
    not_first = (col > 0).astype(F32)
    not_last = (col < last_col).astype(F32)
    for step in range(2):
        for half in range(2):
            lanes = slice(half * C, (half + 1) * C)
            for slot in range(MROWS + 1):
                row = jnp.clip(slot - 1 + core, 0, MROWS - 1)
                values = doubled[step, pl.ds(pl.multiple_of(row * W, W), W), lanes]
                left = doubled[step, pl.ds(MROWS * W + row, 1), lanes] * not_first
                right = doubled[step, pl.ds(MROWS * W + 8 + row, 1), lanes] * not_last
                if slot == 0 or slot == MROWS:
                    keep = core.astype(F32) if slot == 0 else (1 - core).astype(F32)
                    values, left, right = values * keep, left * keep, right * keep
                moved = moved_columns(values, left, right)
                for tap in range(3):
                    framed[2 * step + half, slot, :, tap * C : (tap + 1) * C] = moved[tap]
    shift = jnp.concatenate([bias[...].reshape(1, OUTC), jnp.zeros((1, WIDE - OUTC), F32)], axis=1)
    for parity_row in range(2):
        for parity_col in range(2):
            phase = parity_row * 2 + parity_col
            lanes = slice(parity_col * C, (parity_col + 2) * C)
            result = shift
            for near in range(2):
                rows = slice(parity_row + near, parity_row + near + OWN)
                result = result + lax.dot_general(
                    framed[:, rows, :, lanes].reshape(4 * OWN * W, 2 * C),
                    spatial[phase, near],
                    (((1,), (1,)), ((), ())),
                    preferred_element_type=F32,
                )
            for frame in range(4):
                for row in range(OWN):
                    start = (frame * OWN + row) * W
                    for lane in range(2):
                        woven[
                            lane, frame, 2 * row + parity_row, pl.ds(parity_col, W, stride=2), :
                        ] = result[start : start + W, lane * 128 : lane * 128 + 128]
    copies = []
    for frame in range(4):
        for row in range(2 * OWN):
            out[frame, row, :, :128] = woven[0, frame, row].astype(BF16)
            out[frame, row, :, 128:] = woven[1, frame, row][:, : OUTC - 128].astype(BF16)
        copies.append(
            pltpu.make_async_copy(out.at[frame], target.at[frame0 + frame], sems.at[frame])
        )
        copies[-1].start()
    for copy in copies:
        copy.wait()


def conv_time(frames, weight, bias, doubled):
    pair = [jnp.concatenate(frames[step : step + 3], axis=1) for step in range(2)]
    result = dot(
        jnp.concatenate(pair, axis=0), weight[...].reshape(3 * C, 2 * C)
    ) + bias[...].reshape(1, 2 * C)
    doubled[0] = result[:BLOCK]
    doubled[1] = result[BLOCK:]


def last_frames_kernel(
    last_col, patches, weight, own, other, mine, theirs, bias,
    onward, mixed, time, time_bias, spatial, spatial_bias,
    mixed_out, target,
    doubled, framed, woven, out, sems,
):
    core = lax.axis_index("row")
    shift = bias[...].reshape(1, C)
    late = dot(patches[: 2 * BLOCK], step_weight(weight, 2))
    middle = dot(patches[:BLOCK], step_weight(weight, 1))
    base = base_rows(0, own, other, mine, theirs, shift, core)
    first = (base + late[:BLOCK] + onward[0].astype(F32)).astype(BF16)
    base = base_rows(1, own, other, mine, theirs, shift, core)
    second = (base + late[BLOCK:] + middle + onward[1].astype(F32)).astype(BF16)
    mixed_out[0] = first
    mixed_out[1] = second
    conv_time([first, second, mixed[0], mixed[1]], time, time_bias, doubled)
    upsampled(doubled, spatial, spatial_bias, last_col, framed, woven, out, target, 4, sems)


def first_frames_kernel(
    last_col, previous, mixed, time, time_bias, spatial, spatial_bias, begun,
    target,
    doubled, framed, woven, out, sems,
):
    del begun
    conv_time([previous[0], previous[1], mixed[0], mixed[1]], time, time_bias, doubled)
    upsampled(doubled, spatial, spatial_bias, last_col, framed, woven, out, target, 0, sems)


def parity_kernel(weight, phases):
    for start in range(0, OUTC, 64):
        part = slice(start, start + 64)
        wide = [[weight[row, col, part, :].astype(F32) for col in range(3)] for row in range(3)]
        for parity_row in range(2):
            for near in range(2):
                first, last = ((0, 0), (1, 2)) if parity_row == 0 else ((0, 1), (2, 2))
                low, high = (first, last)[near]
                taps = wide[low]
                if high > low:
                    taps = [one + other for one, other in zip(wide[low], wide[high])]
                for parity_col in range(2):
                    phase = parity_row * 2 + parity_col
                    if parity_col == 0:
                        pair = [taps[0], taps[1] + taps[2]]
                    else:
                        pair = [taps[0] + taps[1], taps[2]]
                    for index in range(2):
                        phases[phase, near, part, index * C : (index + 1) * C] = pair[index].astype(
                            BF16
                        )
    for phase in range(4):
        for near in range(2):
            phases[phase, near, OUTC:, :] = jnp.zeros((WIDE - OUTC, 2 * C), BF16)


def cost(macs, bytes_accessed):
    return pl.CostEstimate(flops=2 * macs, bytes_accessed=bytes_accessed, transcendentals=0)


def call(kernel, name, estimate, limit=LIMIT, **rest):
    return pl.pallas_call(
        kernel,
        name=name,
        cost_estimate=estimate,
        compiler_params=pltpu.CompilerParams(vmem_limit_bytes=limit * 2**20),
        **rest,
    )


def swap_rows(block):
    return lax.ppermute(block, "row", [(0, 1), (1, 0)])


def to_later_frames(block):
    return lax.ppermute(block, "tm", [(i, i + 1) for i in range(lax.axis_size("tm") - 1)])


def across_columns(block):
    count = lax.axis_size("col")
    route = [(i, i - 1) for i in range(1, count)]
    route += [(count + i, count + i + 1) for i in range(count - 1)]
    return lax.ppermute(block, ("row", "col"), route)


def on_device(
    latents, norm_gain, conv_weight, conv_bias, time_weight, time_bias, spatial_weight, spatial_bias
):
    last_col = lax.axis_size("col") - 1
    other = swap_rows(latents)
    own = latents
    spatial_weight = jnp.swapaxes(spatial_weight, 2, 3)
    spatial = call(
        parity_kernel,
        "parity_weights",
        cost(2**30, 5 * 2**20),
        out_shape=jax.ShapeDtypeStruct((4, 2, WIDE, 2 * C), BF16),
        in_specs=[VMEM],
        out_specs=VMEM,
    )(spatial_weight)

    other, spatial = lax.optimization_barrier((other, spatial))
    edge = call(
        edge_kernel,
        "edge",
        cost(2**20, 2**20),
        out_shape=jax.ShapeDtypeStruct((4, 2, 8, C), BF16),
        in_specs=[VMEM] * 2,
        out_specs=VMEM,
        scratch_shapes=[pltpu.VMEM((8, 8, C), F32)],
    )(own, other)
    mine = across_columns(edge)

    activated, edges = call(
        activate_kernel,
        "activated",
        cost(2**32, 2**20),
        out_shape=(
            jax.ShapeDtypeStruct((4, MROWS + 2, W, C), BF16),
            jax.ShapeDtypeStruct((4, 2, 8, C), F32),
        ),
        in_specs=[VMEM] * 3,
        out_specs=(VMEM,) * 2,
    )(own, other, norm_gain)
    mine, activated = lax.optimization_barrier((mine, activated))
    theirs = swap_rows(mine)

    mixed_shape = jax.ShapeDtypeStruct((2, BLOCK, C), BF16)
    patches, onward, crossing = call(
        send_kernel,
        "partial_for_next",
        cost(4 * BLOCK * 9 * C * C, 10 * 2**20),
        out_shape=(
            jax.ShapeDtypeStruct((4 * BLOCK, 9 * C), BF16),
            mixed_shape,
            jax.ShapeDtypeStruct((BLOCK, C), F32),
        ),
        in_specs=[VMEM] * 6,
        out_specs=(VMEM,) * 3,
        scratch_shapes=[pltpu.VMEM((4, 2, 8, C), F32)],
    )(activated, edges, mine, theirs, norm_gain, conv_weight)
    onward = to_later_frames(onward)

    mixed = call(
        own_kernel,
        "mixed_last",
        cost(5 * BLOCK * 9 * C * C, 10 * 2**20),
        out_shape=mixed_shape,
        in_specs=[VMEM] * 8,
        out_specs=VMEM,
        scratch_shapes=[pltpu.VMEM((2 * BLOCK, C), F32), pltpu.VMEM((2 * BLOCK, C), F32)],
    )(patches, conv_weight, crossing, own, other, mine, theirs, conv_bias)
    previous = to_later_frames(mixed)

    out_shape = jax.ShapeDtypeStruct((8, 2 * OWN, 2 * W, OUTC), BF16)
    scratch = [
        pltpu.VMEM((2, BLOCK, 2 * C), F32),
        pltpu.VMEM((4, OWN + 2, W, 3 * C), BF16),
        pltpu.VMEM((2, 4, 2 * OWN, 2 * W, 128), F32),
        pltpu.VMEM((4, 2 * OWN, 2 * W, OUTC), BF16),
        pltpu.SemaphoreType.DMA((4,)),
    ]
    late_cost = cost(2 * BLOCK * 6 * C * C + 16 * 512 * C * WIDE, 6 * 2**20)

    def last_frames(*refs):
        last_frames_kernel(last_col, *refs)

    mixed_own, begun = call(
        last_frames,
        "upsample_last",
        late_cost,
        out_shape=(mixed_shape, out_shape),
        in_specs=[VMEM] * 13,
        out_specs=(VMEM, HBM),
        scratch_shapes=scratch,
    )(
        patches, conv_weight, own, other, mine, theirs, conv_bias,
        onward, mixed, time_weight, time_bias, spatial, spatial_bias,
    )

    def first_frames(*refs):
        first_frames_kernel(last_col, *refs)

    return call(
        first_frames,
        "upsample_first",
        late_cost,
        out_shape=out_shape,
        in_specs=[VMEM] * 6 + [HBM],
        out_specs=HBM,
        scratch_shapes=scratch,
        input_output_aliases={6: 0},
    )(previous, mixed_own, time_weight, time_bias, spatial, spatial_bias, begun)


def solution(mesh):
    placed = (P("tm", "row", "col", None), P(), P(), P(), P(), P(), P(), P())
    return jax.shard_map(
        on_device,
        mesh=mesh,
        in_specs=placed,
        out_specs=P("tm", "row", "col", None),
        check_vma=False,
    )
```

time: 118 us -> 37.4 us (0.32)
  matrix products: 31 us -> 0 us
  local copies, waits for them, and re-layouts: 27.1 us -> 1.75 us
  other arithmetic: 19.7 us -> 0.01 us
  Pallas kernels: 0 us -> 17.6 us
  starting transfers between devices: 23.7 us -> 9.39 us
  waiting for transfers between devices: 14.3 us -> 8.23 us
    dot_general x46 -> x0, matrix products: 31 us -> none  [the longest x16 17.8 us: upsample_conv(): jnp.dot(slab_piece.reshape(-1, framed.shape[-1]), paired, preferred_eleme...]
    pallas_call x0 -> x7, Pallas kernels: none -> 17.6 us  [the longest x1 6.15 us: on_device(): call(last_frames, 'upsample_last', late_cost, out_shape=(mixed_shape, out...]
    ppermute x10 -> x5, starting transfers between devices: 23.7 us -> 9.39 us  [the longest x2 6.98 us: to_later_frames(): lax.ppermute(block, 'tm', [(i, i + 1) for i in range(lax.axis_size('tm')...]
    convert_element_type x10 -> x0, other arithmetic: 10.8 us -> none  [the longest x5 5 us: upsample_conv(): low_part = (summed - high_part.astype(jnp.float32)).astype(jnp.bfloat16)]
    reshape x2 -> x0, local copies, waits for them, and re-layouts: 7 us -> none  [the longest x1 6.15 us: upsample_conv(): jnp.transpose(stacked, (2, 3, 0, 4, 1, 5))]
    add x5 -> x0, local copies, waits for them, and re-layouts: 6.48 us -> none  [the longest x4 6.48 us: upsample_conv(): running = running + product[:, :out_width] + product[:, out_width:]]
    ppermute x10 -> x5, waiting for transfers between devices: 14.3 us -> 8.23 us  [the longest x1 4.4 us: across_columns(): return lax.ppermute(block, ('row', 'col'), route)]
    transpose x1 -> x0, local copies, waits for them, and re-layouts: 5.76 us -> none  [upsample_conv(): jnp.transpose(stacked, (2, 3, 0, 4, 1, 5))]
  transfers between devices with their start and end apart: 10 -> 5, of which waited for: 4 -> 5; matrix products, arithmetic and copies ran while one was open for 17% -> 0% of each run, Pallas kernels for 0% -> 29%
where the time goes in v1:
time: 37.4 us; the launch traced here: 37.2 us
  Pallas kernels  17.6 us (47%)
  starting transfers between devices  9.39 us (25%)
  waiting for transfers between devices  8.23 us (22%)
  local copies, waits for them, and re-layouts  1.75 us (5%)
    ppermute x2, starting transfers between devices, to_later_frames(): lax.ppermute(block, 'tm', [(i, i + 1) for i in range(lax.axis_size('tm')...  6.98 us
    pallas_call x1, Pallas kernels, on_device(): call(last_frames, 'upsample_last', late_cost, out_shape=(mixed_shape, out...  6.15 us
    ppermute x1, waiting for transfers between devices, across_columns(): return lax.ppermute(block, ('row', 'col'), route)  4.4 us
    pallas_call x1, Pallas kernels, on_device(): call(first_frames, 'upsample_first', late_cost, out_shape=out_shape, in_s...  4.09 us
    pallas_call x1, Pallas kernels, on_device(): call(own_kernel, 'mixed_last', cost(5 * BLOCK * 9 * C * C, 10 * 2 ** 20),...  3.42 us
    pallas_call x1, Pallas kernels, on_device(): call(send_kernel, 'partial_for_next', cost(4 * BLOCK * 9 * C * C, 10 * 2...  2.54 us
    ppermute x2, waiting for transfers between devices, to_later_frames(): lax.ppermute(block, 'tm', [(i, i + 1) for i in range(lax.axis_size('tm')...  2.51 us
    ppermute x1, starting transfers between devices, across_columns(): return lax.ppermute(block, ('row', 'col'), route)  2.41 us
  transfers between devices with their start and end apart: 5, of which 5 were waited for; matrix products, arithmetic and copies ran while one was open for 0% of the time, Pallas kernels for 29%

profile of v1, /device:TPU:104, one launch (start us, length us, event | category | flops | bytes accessed | tf_op | source)
XLA Modules:
  0.0 37.2 jit_solution(13590263537390888699)
XLA Ops:
  0.0 0.0 collective-permute-start
  0.0 1.3 %copy-done.6 = bf16[3,3,384,192]{2,3,1,0:T(8,128)(2,1)S(1)} copy-done((bf16[3,3,384,192]{2,3,1,0:T(8,128)(2,1)S(1)}, bf16[3,3,384,192]{2,3,1,0:T(8,128)(2,1)}, u32[]{:S(2)}) %copy-start.6) | copy-done | bytes 1327128
  1.3 0.5 %parity_weights.1.refs_11_.refs_4_ = bf16[4,2,256,768]{3,2,1,0:T(8,128)(2,1)S(1)} custom-call(bf16[3,3,192,384]{3,2,1,0:T(8,128)(2,1)S(1)} %bitcast.3), custom_call_target="tpu_custom_call" | custom-call | flops 2147483648 | bytes 5242880 | tf_op jit(solution)/shard_map/parity_weights/pallas_call | solution.py:334
  1.8 0.1 collective-permute-done.other.refs_3_
  1.9 0.4 %copy-done.1 = bf16[4,4,32,384]{3,2,1,0:T(8,128)(2,1)S(1)} copy-done((bf16[4,4,32,384]{3,2,1,0:T(8,128)(2,1)S(1)}, bf16[4,4,32,384]{3,2,1,0:T(8,128)(2,1)}, u32[]{:S(2)}) %copy-start.1) | copy-done | bytes 393240
  2.3 0.1 edge.1
  2.5 0.0 slice-start.1
  2.5 2.4 %collective-permute-start.1 = (bf16[4,2,8,384]{3,2,1,0:T(8,128)(2,1)S(1)}, bf16[4,2,8,384]{3,2,1,0:T(8,128)(2,1)S(1)}, u32[]{:S(2)}, u32[]{:S(2)}) collective-permute-start(bf16[4,2,8,384]{3,2,1,0:T(8,128)(2,1)S(1)} %edge.1), channel_id=1, source_target_pairs={{1,0},{2,1},{3,2},{4,3},{5,4},{6,5},{7,6},{8,9},{9,10},{10,11},{11... | collective-permute-start | bytes 147464 | tf_op jit(solution)/shard_map/ppermute | solution.py:324
  4.9 0.7 %activated.1 = (bf16[4,7,32,384]{3,2,1,0:T(8,128)(2,1)S(1)}, f32[4,2,8,384]{3,2,1,0:T(8,128)S(1)}) custom-call(bf16[4,4,32,384]{3,2,1,0:T(8,128)(2,1)S(1)} %copy-done.1, bf16[4,4,32,384]{3,2,1,0:T(8,128)(2,1)S(1)} %collective-permute-done.other.refs_3_, f32[384]{0:T(512)S(1)} %copy-done.5), custom_call_target="tpu_custom_call" | custom-call | flops 8589934592 | bytes 1048576 | tf_op jit(solution)/shard_map/activated/pallas_call | solution.py:355
  5.6 4.4 %collective-permute-done.1.mine.refs_4_ = bf16[4,2,8,384]{3,2,1,0:T(8,128)(2,1)S(1)} collective-permute-done((bf16[4,2,8,384]{3,2,1,0:T(8,128)(2,1)S(1)}, bf16[4,2,8,384]{3,2,1,0:T(8,128)(2,1)S(1)}, u32[]{:S(2)}, u32[]{:S(2)}) %collective-permute-start.1) | collective-permute-done | bytes 49184 | tf_op jit(solution)/shard_map/ppermute | solution.py:324
  10.1 0.0 collective-permute-start.2
  10.1 1.2 %collective-permute-done.2.theirs.refs_5_ = bf16[4,2,8,384]{3,2,1,0:T(8,128)(2,1)S(1)} collective-permute-done((bf16[4,2,8,384]{3,2,1,0:T(8,128)(2,1)S(1)}, bf16[4,2,8,384]{3,2,1,0:T(8,128)(2,1)S(1)}, u32[]{:S(2)}, u32[]{:S(2)}) %collective-permute-start.2) | collective-permute-done | bytes 49184 | tf_op jit(solution)/shard_map/ppermute | solution.py:313
  11.3 2.5 %partial_for_next.1 = (bf16[704,3456]{1,0:T(8,128)(2,1)S(1)}, bf16[2,176,384]{2,1,0:T(8,128)(2,1)S(1)}, f32[176,384]{1,0:T(8,128)S(1)}) custom-call(bf16[4,7,32,384]{3,2,1,0:T(8,128)(2,1)S(1)} %get-tuple-element.18.activated, f32[4,2,8,384]{3,2,1,0:T(8,128)S(1)} %get-tuple-element.19.edges, bf16[4,2,8,384]{3,2,1,0:T(8,128)(2,1)S(1)} %collective-permute-done.1.mine.refs_4_, ...), custom_call_target="tpu_custom_call" | custom-call | flops 1868562432 | bytes 10485760 | tf_op jit(solution)/shard_map/partial_for_next/pallas_call | solution.py:370
  13.8 3.4 %collective-permute-start.4 = (bf16[2,176,384]{2,1,0:T(8,128)(2,1)S(1)}, bf16[2,176,384]{2,1,0:T(8,128)(2,1)S(1)}, u32[]{:S(2)}, u32[]{:S(2)}) collective-permute-start(bf16[2,176,384]{2,1,0:T(8,128)(2,1)S(1)} %get-tuple-element.23), channel_id=1, source_target_pairs={{0,16},{16,32},{32,48},{48,64},{64,80},{80,96},{96,112},{112,128},... | collective-permute-start | bytes 811016 | tf_op jit(solution)/shard_map/ppermute | solution.py:317
  17.3 0.0 copy-start
  17.3 0.0 copy-start.2
  17.3 0.0 copy-start.4
  17.3 3.4 %mixed_last.1.refs_8_ = bf16[2,176,384]{2,1,0:T(8,128)(2,1)S(1)} custom-call(bf16[704,3456]{1,0:T(8,128)(2,1)S(1)} %get-tuple-element.21.patches.refs_0_, bf16[3,3,3,384,384]{4,3,2,1,0:T(8,128)(2,1)S(1)} %bitcast.2, f32[176,384]{1,0:T(8,128)S(1)} %get-tuple-element.22.crossing, bf16[4,4,32,384]{3,2,1,0:T(8,128)(2,1)S(1)} %copy-done.1, ...), custom_call_target="tpu_custom_call" | custom-call | flops 2335703040 | bytes 10485760 | tf_op jit(solution)/shard_map/mixed_last/pallas_call | solution.py:385
  20.7 3.6 %collective-permute-start.3 = (bf16[2,176,384]{2,1,0:T(8,128)(2,1)S(1)}, bf16[2,176,384]{2,1,0:T(8,128)(2,1)S(1)}, u32[]{:S(2)}, u32[]{:S(2)}) collective-permute-start(bf16[2,176,384]{2,1,0:T(8,128)(2,1)S(1)} %mixed_last.1.refs_8_), channel_id=1, source_target_pairs={{0,16},{16,32},{32,48},{48,64},{64,80},{80,96},{96,112},{112,128},... | collective-permute-start | bytes 811016 | tf_op jit(solution)/shard_map/ppermute | solution.py:317
  24.3 2.1 %collective-permute-done.4.refs_7_ = bf16[2,176,384]{2,1,0:T(8,128)(2,1)S(1)} collective-permute-done((bf16[2,176,384]{2,1,0:T(8,128)(2,1)S(1)}, bf16[2,176,384]{2,1,0:T(8,128)(2,1)S(1)}, u32[]{:S(2)}, u32[]{:S(2)}) %collective-permute-start.4) | collective-permute-done | bytes 270368 | tf_op jit(solution)/shard_map/ppermute | solution.py:317
  26.4 0.0 copy-done.4
  26.4 6.2 %upsample_last.1 = (bf16[2,176,384]{2,1,0:T(8,128)(2,1)S(1)}, bf16[8,8,64,192]{3,2,1,0:T(8,128)(2,1)}) custom-call(bf16[704,3456]{1,0:T(8,128)(2,1)S(1)} %get-tuple-element.21.patches.refs_0_, bf16[3,3,3,384,384]{4,3,2,1,0:T(8,128)(2,1)S(1)} %bitcast.2, bf16[4,4,32,384]{3,2,1,0:T(8,128)(2,1)S(1)} %copy-done.1, ...), custom_call_target="tpu_custom_call" | custom-call | flops 2233466880 | bytes 6291456 | tf_op jit(solution)/shard_map/upsample_last/pallas_call | solution.py:409
  32.6 0.4 %collective-permute-done.3.refs_0_ = bf16[2,176,384]{2,1,0:T(8,128)(2,1)S(1)} collective-permute-done((bf16[2,176,384]{2,1,0:T(8,128)(2,1)S(1)}, bf16[2,176,384]{2,1,0:T(8,128)(2,1)S(1)}, u32[]{:S(2)}, u32[]{:S(2)}) %collective-permute-start.3) | collective-permute-done | bytes 270368 | tf_op jit(solution)/shard_map/ppermute | solution.py:317
  33.0 4.1 %upsample_first.1 = bf16[8,8,64,192]{3,2,1,0:T(8,128)(2,1)} custom-call(bf16[2,176,384]{2,1,0:T(8,128)(2,1)S(1)} %collective-permute-done.3.refs_0_, bf16[2,176,384]{2,1,0:T(8,128)(2,1)S(1)} %get-tuple-element.25.refs_1_, bf16[3,384,768]{2,1,0:T(8,128)(2,1)S(1)} %copy-done, f32[768]{0:T(1024)S(1)} %copy-done.2, ...), custom_call_target="tpu_custom_call", output_to_operand_aliasing={{}: (6, {})} | custom-call | flops 2233466880 | bytes 6291456 | tf_op jit(solution)/shard_map/upsample_first/pallas_call | solution.py:425
  (12 shorter events, 0.0 us)
Async XLA Ops:
  0.0 1.9 %collective-permute-start = (bf16[4,4,32,384]{3,2,1,0:T(8,128)(2,1)}, bf16[4,4,32,384]{3,2,1,0:T(8,128)(2,1)S(1)}, u32[]{:S(2)}, u32[]{:S(2)}) collective-permute-start(bf16[4,4,32,384]{3,2,1,0:T(8,128)(2,1)} %refs_2_.2), channel_id=1, source_target_pairs={{0,8},{8,0},{1,9},{9,1},{2,10},{10,2},{3,11},{11,3},{4,12},{12,4},... | collective-permute-start | bytes 1179656 | tf_op jit(solution)/shard_map/ppermute | solution.py:313
  0.0 1.3 %copy-start.6 = (bf16[3,3,384,192]{2,3,1,0:T(8,128)(2,1)S(1)}, bf16[3,3,384,192]{2,3,1,0:T(8,128)(2,1)}, u32[]{:S(2)}) copy-start(bf16[3,3,384,192]{2,3,1,0:T(8,128)(2,1)} %param.14) | copy-start | bytes 3981316
  1.3 1.0 %copy-start.1 = (bf16[4,4,32,384]{3,2,1,0:T(8,128)(2,1)S(1)}, bf16[4,4,32,384]{3,2,1,0:T(8,128)(2,1)}, u32[]{:S(2)}) copy-start(bf16[4,4,32,384]{3,2,1,0:T(8,128)(2,1)} %refs_2_.2) | copy-start | bytes 1179652
  1.3 3.6 %copy-start.5 = (f32[384]{0:T(512)S(1)}, f32[384]{0:T(512)}, u32[]{:S(2)}) copy-start(f32[384]{0:T(512)} %gain.3) | copy-start | bytes 4612
  2.3 9.0 %slice-start = ((s8[7962624]{0:T(1024)(128)(4,1)}), s8[4194304]{0:T(1024)(128)(4,1)S(1)}, s32[]{:S(2)}) async-start(s8[7962624]{0:T(1024)(128)(4,1)} %bitcast.1), calls=%async_computation | async-start | bytes 8388608
  2.5 8.8 %slice-start.1 = ((s8[7962624]{0:T(1024)(128)(4,1)}), s8[3768320]{0:T(1024)(128)(4,1)S(1)}, s32[]{:S(2)}) async-start(s8[7962624]{0:T(1024)(128)(4,1)} %bitcast.1), calls=%async_computation.1 | async-start | bytes 7536640
  2.5 7.6 %collective-permute-start.1 = (bf16[4,2,8,384]{3,2,1,0:T(8,128)(2,1)S(1)}, bf16[4,2,8,384]{3,2,1,0:T(8,128)(2,1)S(1)}, u32[]{:S(2)}, u32[]{:S(2)}) collective-permute-start(bf16[4,2,8,384]{3,2,1,0:T(8,128)(2,1)S(1)} %edge.1), channel_id=1, source_target_pairs={{1,0},{2,1},{3,2},{4,3},{5,4},{6,5},{7,6},{8,9},{9,10},{10,11},{11... | collective-permute-start | bytes 147464 | tf_op jit(solution)/shard_map/ppermute | solution.py:324
  10.1 1.2 %collective-permute-start.2 = (bf16[4,2,8,384]{3,2,1,0:T(8,128)(2,1)S(1)}, bf16[4,2,8,384]{3,2,1,0:T(8,128)(2,1)S(1)}, u32[]{:S(2)}, u32[]{:S(2)}) collective-permute-start(bf16[4,2,8,384]{3,2,1,0:T(8,128)(2,1)S(1)} %collective-permute-done.1.mine.refs_4_), channel_id=1, source_target_pairs={{0,8},{8,0},{1,9},{9,1},{2,10},{10,2},{3,11},{11,3},{4,12},{12,4},... | collective-permute-start | bytes 147464 | tf_op jit(solution)/shard_map/ppermute | solution.py:313
  11.3 6.0 %copy-start.3 = (f32[384]{0:T(512)S(1)}, f32[384]{0:T(512)}, u32[]{:S(2)}) copy-start(f32[384]{0:T(512)} %refs_6_.1) | copy-start | bytes 4612
  13.8 12.5 %collective-permute-start.4 = (bf16[2,176,384]{2,1,0:T(8,128)(2,1)S(1)}, bf16[2,176,384]{2,1,0:T(8,128)(2,1)S(1)}, u32[]{:S(2)}, u32[]{:S(2)}) collective-permute-start(bf16[2,176,384]{2,1,0:T(8,128)(2,1)S(1)} %get-tuple-element.23), channel_id=1, source_target_pairs={{0,16},{16,32},{32,48},{48,64},{64,80},{80,96},{96,112},{112,128},... | collective-permute-start | bytes 811016 | tf_op jit(solution)/shard_map/ppermute | solution.py:317
  17.3 9.1 %copy-start = (bf16[3,384,768]{2,1,0:T(8,128)(2,1)S(1)}, bf16[3,384,768]{2,1,0:T(8,128)(2,1)}, u32[]{:S(2)}) copy-start(bf16[3,384,768]{2,1,0:T(8,128)(2,1)} %refs_2_.3) | copy-start | bytes 5308420
  17.3 9.1 %copy-start.2 = (f32[768]{0:T(1024)S(1)}, f32[768]{0:T(1024)}, u32[]{:S(2)}) copy-start(f32[768]{0:T(1024)} %refs_3_.1) | copy-start | bytes 9220
  17.3 9.1 %copy-start.4 = (f32[192]{0:T(256)S(1)}, f32[192]{0:T(256)}, u32[]{:S(2)}) copy-start(f32[192]{0:T(256)} %refs_5_.1) | copy-start | bytes 2308
  20.7 12.3 %collective-permute-start.3 = (bf16[2,176,384]{2,1,0:T(8,128)(2,1)S(1)}, bf16[2,176,384]{2,1,0:T(8,128)(2,1)S(1)}, u32[]{:S(2)}, u32[]{:S(2)}) collective-permute-start(bf16[2,176,384]{2,1,0:T(8,128)(2,1)S(1)} %mixed_last.1.refs_8_), channel_id=1, source_target_pairs={{0,16},{16,32},{32,48},{48,64},{64,80},{80,96},{96,112},{112,128},... | collective-permute-start | bytes 811016 | tf_op jit(solution)/shard_map/ppermute | solution.py:317

commit v2 on v1

v2 whole, which is shorter than its diff:
```python
import jax
import jax.numpy as jnp
from jax import lax
from jax.experimental import pallas as pl
from jax.experimental.pallas import tpu as pltpu
from jax.sharding import PartitionSpec as P

F32 = jnp.float32
BF16 = jnp.bfloat16
HBM = pl.BlockSpec(memory_space=pltpu.HBM)
VMEM = pl.BlockSpec(memory_space=pltpu.VMEM)

C = 384
OUTC = 192
WIDE = 256
W = 32
OWN = 4
MROWS = 5
SIDE = 16
BLOCK = MROWS * W + SIDE
LIMIT = 24


def activate(values, gain):
    scale = lax.rsqrt(jnp.mean(values * values, axis=-1, keepdims=True) + 1e-06)
    half = values * scale * (0.5 * gain)
    return half + half * jnp.tanh(half)


def dot(left, right):
    return jnp.dot(left, right, preferred_element_type=F32)


def moved_columns(values, left, right):
    place = lax.broadcasted_iota(jnp.int32, values.shape, 0)
    before = jnp.where(place == 0, left, pltpu.roll(values, 1, 0))
    after = jnp.where(place == W - 1, right, pltpu.roll(values, W - 1, 0))
    return before.astype(BF16), values.astype(BF16), after.astype(BF16)


def slot_order(rows, core):
    place = lax.broadcasted_iota(jnp.int32, rows.shape, 0)
    upper = jnp.where(place == 0, 0.0, pltpu.roll(rows, 1, 0))
    lower = jnp.where(place >= 6, 0.0, pltpu.roll(rows, 6, 0))
    return jnp.where(core == 0, upper, lower)


def cut_columns(source, first, core, held):
    start = pl.multiple_of(core * 16, 16)
    for frame in range(4):
        for row in range(OWN):
            values = source[frame, row, pl.ds(start, 16), :].astype(F32)
            values = jnp.where(core == 0, values, pltpu.roll(values, 2, 0))
            for col in range(2):
                held[2 * frame + col, pl.ds(first + row, 1), :] = values[col : col + 1]


def own_edge_kernel(own, held):
    core = lax.axis_index("row")
    cut_columns(own, core * OWN, core, held)


def edge_kernel(held, other, edge, rest):
    core = lax.axis_index("row")
    cut_columns(other, OWN - core * OWN, core, rest)
    place = lax.broadcasted_iota(jnp.int32, (8, C), 0)
    mine = (place < OWN) == (core == 0)
    for frame in range(4):
        for col in range(2):
            index = 2 * frame + col
            edge[frame, col] = jnp.where(mine, held[index], rest[index]).astype(BF16)


def activate_kernel(
    own, other, gain, weight, activated, edges, third, first, third_patches, first_patches
):
    core = lax.axis_index("row")
    scale = gain[...].reshape(1, C)
    edges[...] = jnp.zeros(edges.shape, F32)

    def one(frame, carry):
        for slot in range(MROWS + 2):
            if slot == 0:
                values = other[frame, 2].astype(F32) * core.astype(F32)
            elif slot == 1:
                values = jnp.where(core == 0, own[frame, 0], other[frame, 3]).astype(F32)
            elif slot == 5:
                values = jnp.where(core == 0, other[frame, 0], own[frame, 3]).astype(F32)
            elif slot == 6:
                values = other[frame, 1].astype(F32) * (1 - core).astype(F32)
            else:
                values = own[frame, slot - 1 - core].astype(F32)
            values = activate(values, scale)
            edges[frame, 0, slot : slot + 1, :] = values[0:1]
            edges[frame, 1, slot : slot + 1, :] = values[W - 1 : W]
            activated[frame, slot] = values.astype(BF16)
        return carry

    lax.fori_loop(0, 4, one, 0)
    inner_products(3, activated, weight, third_patches, third)
    inner_products(1, activated, weight, first_patches, first)


def inner_kernel(activated, weight, total, patches):
    inner_products(2, activated, weight, patches, total)


def halo_columns(frame, mine, theirs, core):
    columns = []
    for col in range(4):
        first, second = (theirs, mine) if col < 2 else (mine, theirs)
        rows = jnp.where(core == 0, first[frame, col % 2], second[frame, col % 2]).astype(F32)
        columns.append(slot_order(rows, core))
    return columns


def fill_rows(at, slot, values, left, right, patches):
    moved = moved_columns(values, left, right)
    for tap_row in range(3):
        out_row = slot - tap_row
        if 0 <= out_row < MROWS:
            for tap_col in range(3):
                tap = tap_row * 3 + tap_col
                patches[at + out_row * W : at + (out_row + 1) * W, tap * C : (tap + 1) * C] = moved[
                    tap_col
                ]


def fill_patches(frame, at, activated, edges, columns, patches, line):
    line[frame, 0] = columns[1]
    line[frame, 1] = columns[2]
    for slot in range(MROWS + 2):
        left = line[frame, 0, slot : slot + 1, :]
        right = line[frame, 1, slot : slot + 1, :]
        fill_rows(at, slot, activated[frame, slot].astype(F32), left, right, patches)
    fill_sides(at + MROWS * W, frame, edges, columns, patches, False)


def fill_sides(at, frame, edges, columns, patches, inner):
    low = [columns[0], columns[1], edges[frame, 0]]
    high = [edges[frame, 1], columns[2], columns[3]]
    none = jnp.zeros((8, C), F32)
    for tap_row in range(3):
        for tap_col in range(3):
            tap = tap_row * 3 + tap_col
            parts = [low[tap_col], high[tap_col]]
            if inner:
                parts.append(columns[1] if tap_col == 0 else none)
                parts.append(columns[2] if tap_col == 2 else none)
            if tap_row:
                parts = [pltpu.roll(one, 8 - tap_row, 0) for one in parts]
            rows = slice(at, at + 8 * len(parts))
            patches[rows, tap * C : (tap + 1) * C] = jnp.concatenate(parts, axis=0).astype(BF16)


def early_weight(weight):
    return jnp.concatenate([step_weight(weight, 0), step_weight(weight, 1)], axis=1)


def inner_products(frame, activated, weight, patches, total):
    for slot in range(MROWS + 2):
        fill_rows(0, slot, activated[frame, slot].astype(F32), 0.0, 0.0, patches)
    total[...] = dot(patches[...], early_weight(weight))


def step_weight(weight, step):
    return weight[step].reshape(9 * C, C)


def outer_columns(frame, mine, theirs, gain, core):
    return [activate(one, gain) for one in halo_columns(frame, mine, theirs, core)]


def send_kernel(
    edges, mine, theirs, gain, weight, inner1, inner2, inner3, onward, crossing, sides, total
):
    core = lax.axis_index("row")
    scale = gain[...].reshape(1, C)
    for index in range(3):
        columns = outer_columns(1 + index, mine, theirs, scale, core)
        fill_sides(index * 32, 1 + index, edges, columns, sides, True)
    extra = dot(sides[...], early_weight(weight))
    for index, inner in enumerate((inner1, inner2, inner3)):
        base = index * 32
        total[index, : MROWS * W] = inner[...]
        total[index, MROWS * W :] = extra[base : base + SIDE]
        for row in range(MROWS):
            for at, side in ((row * W, 16), (row * W + W - 1, 24)):
                line = slice(at, at + 1)
                add = slice(base + side + row, base + side + row + 1)
                total[index, line] = inner[line] + extra[add]
    onward[0] = (total[1, :, :C] + total[2, :, C:]).astype(BF16)
    onward[1] = total[2, :, :C].astype(BF16)
    crossing[0] = total[0, :, C:]
    crossing[1] = total[0, :, :C] + total[1, :, C:]


def base_rows(frame, own, other, mine, theirs, bias, core):
    rows = []
    for out_row in range(MROWS):
        if out_row == 0:
            values = jnp.where(core == 0, own[frame, 0], other[frame, 3])
        elif out_row == OWN:
            values = jnp.where(core == 0, other[frame, 0], own[frame, 3])
        else:
            values = own[frame, out_row - core]
        rows.append(values.astype(F32) + bias)
    columns = halo_columns(frame, mine, theirs, core)
    rows.append(pltpu.roll(columns[1], 7, 0) + bias)
    rows.append(pltpu.roll(columns[2], 7, 0) + bias)
    return jnp.concatenate(rows, axis=0)


def own_kernel(
    activated, edges, gain, weight, crossing, own, other, mine, theirs, bias, mixed, patches,
    last_patches, line,
):
    core = lax.axis_index("row")
    shift = bias[...].reshape(1, C)
    scale = gain[...].reshape(1, C)

    def fill(frame, target, at):
        columns = outer_columns(frame, mine, theirs, scale, core)
        fill_patches(frame, at, activated, edges, columns, target, line)

    fill(2, last_patches, 0)
    fill(3, last_patches, BLOCK)
    late = dot(last_patches[...], step_weight(weight, 2))
    fill(0, patches, 0)
    early = dot(patches[...], step_weight(weight, 0))
    fourth = base_rows(3, own, other, mine, theirs, shift, core)
    mixed[1] = (fourth + late[BLOCK:] + crossing[1]).astype(BF16)
    third = base_rows(2, own, other, mine, theirs, shift, core)
    mixed[0] = (third + late[:BLOCK] + crossing[0] + early).astype(BF16)


def first_part_kernel(
    patches, activated, edges, gain, weight, own, other, mine, theirs, bias, spatial_weight,
    part, spatial,
    second_patches, line,
):
    core = lax.axis_index("row")
    shift = bias[...].reshape(1, C)
    scale = gain[...].reshape(1, C)
    both = jnp.concatenate([step_weight(weight, 1), step_weight(weight, 2)], axis=1)
    early = dot(patches[...], both)
    parity_weights(spatial_weight, spatial)
    columns = outer_columns(1, mine, theirs, scale, core)
    fill_patches(1, 0, activated, edges, columns, second_patches, line)
    part[0] = base_rows(0, own, other, mine, theirs, shift, core) + early[:, C:]
    late = dot(second_patches[...], step_weight(weight, 2))
    part[1] = base_rows(1, own, other, mine, theirs, shift, core) + early[:, :C] + late


def frame_step(doubled, last_col, framed):
    core = lax.axis_index("row")
    col = lax.axis_index("col")
    not_first = (col > 0).astype(F32)
    not_last = (col < last_col).astype(F32)
    for half in range(2):
        lanes = slice(half * C, (half + 1) * C)

        def row_of(row):
            return (
                doubled[row * W : (row + 1) * W, lanes],
                doubled[MROWS * W + row : MROWS * W + row + 1, lanes] * not_first,
                doubled[MROWS * W + 8 + row : MROWS * W + 9 + row, lanes] * not_last,
            )

        for slot in range(MROWS + 1):
            if slot == 0:
                parts = [jnp.where(core == 0, 0.0, one) for one in row_of(0)]
            elif slot == MROWS:
                parts = [jnp.where(core == 0, one, 0.0) for one in row_of(MROWS - 1)]
            else:
                pairs = zip(row_of(slot - 1), row_of(slot))
                parts = [jnp.where(core == 0, upper, lower) for upper, lower in pairs]
            moved = moved_columns(*parts)
            for tap in range(3):
                framed[half, slot, :, tap * C : (tap + 1) * C] = moved[tap]


def spatial_step(framed, spatial, bias, woven):
    shift = jnp.concatenate([bias[...].reshape(1, OUTC), jnp.zeros((1, WIDE - OUTC), F32)], axis=1)
    for parity_row in range(2):
        for parity_col in range(2):
            phase = parity_row * 2 + parity_col
            lanes = slice(parity_col * C, (parity_col + 2) * C)
            result = shift
            for near in range(2):
                rows = slice(parity_row + near, parity_row + near + OWN)
                result = result + lax.dot_general(
                    framed[:, rows, :, lanes].reshape(2 * OWN * W, 2 * C),
                    spatial[phase, near],
                    (((1,), (1,)), ((), ())),
                    preferred_element_type=F32,
                )
            for frame in range(2):
                for row in range(OWN):
                    start = (frame * OWN + row) * W
                    for lane in range(2):
                        woven[
                            lane, frame, 2 * row + parity_row, pl.ds(parity_col, W, stride=2), :
                        ] = result[start : start + W, lane * 128 : lane * 128 + 128]


def weave_step(woven, out, target, frame0, sems):
    copies = []
    for frame in range(2):
        for row in range(2 * OWN):
            out[frame, row, :, :128] = woven[0, frame, row].astype(BF16)
            out[frame, row, :, 128:] = woven[1, frame, row][:, : OUTC - 128].astype(BF16)
        copies.append(
            pltpu.make_async_copy(out.at[frame], target.at[frame0 + frame], sems.at[frame])
        )
        copies[-1].start()
    return copies


def upsampled(last_col, spatial, bias, target, frame0, first, second):
    frame_step(first[0], last_col, first[1])
    spatial_step(first[1], spatial, bias, first[2])
    frame_step(second[0], last_col, second[1])
    spatial_step(second[1], spatial, bias, second[2])
    copies = weave_step(first[2], first[3], target, frame0, first[4])
    copies += weave_step(second[2], second[3], target, frame0 + 2, second[4])
    for copy in copies:
        copy.wait()


def last_frames_kernel(
    last_col, part, onward, mixed, time, time_bias, spatial, spatial_bias, begun, target, *scratch
):
    first_half, second_half = scratch[:5], scratch[5:]
    first = (part[0] + onward[0].astype(F32)).astype(BF16)
    second = (part[1] + onward[1].astype(F32)).astype(BF16)
    whole = time[...].reshape(3 * C, 2 * C)
    shift = time_bias[...].reshape(1, 2 * C)
    first_half[0][...] = (
        dot(jnp.concatenate([first, second, mixed[0]], axis=1), whole) + shift
    )
    second_half[0][...] = (
        dot(jnp.concatenate([second, mixed[0], mixed[1]], axis=1), whole) + shift
    )
    begun[0] = dot(first, whole[2 * C :]) + shift
    begun[1] = dot(jnp.concatenate([first, second], axis=1), whole[C:]) + shift
    upsampled(last_col, spatial, spatial_bias, target, 4, first_half, second_half)


def first_frames_kernel(
    last_col, previous, begun, time, spatial, spatial_bias, half_done, target, *scratch
):
    del half_done
    first_half, second_half = scratch[:5], scratch[5:]
    whole = time[...].reshape(3 * C, 2 * C)
    first_half[0][...] = begun[0] + dot(
        jnp.concatenate([previous[0], previous[1]], axis=1), whole[: 2 * C]
    )
    second_half[0][...] = begun[1] + dot(previous[1], whole[:C])
    upsampled(last_col, spatial, spatial_bias, target, 0, first_half, second_half)


def parity_weights(weight, phases):
    for start in range(0, OUTC, 64):
        part = slice(start, start + 64)
        wide = [[weight[row, col, part, :].astype(F32) for col in range(3)] for row in range(3)]
        for parity_row in range(2):
            for near in range(2):
                first, last = ((0, 0), (1, 2)) if parity_row == 0 else ((0, 1), (2, 2))
                low, high = (first, last)[near]
                taps = wide[low]
                if high > low:
                    taps = [one + other for one, other in zip(wide[low], wide[high])]
                for parity_col in range(2):
                    phase = parity_row * 2 + parity_col
                    if parity_col == 0:
                        pair = [taps[0], taps[1] + taps[2]]
                    else:
                        pair = [taps[0] + taps[1], taps[2]]
                    for index in range(2):
                        phases[phase, near, part, index * C : (index + 1) * C] = pair[index].astype(
                            BF16
                        )
    for phase in range(4):
        for near in range(2):
            phases[phase, near, OUTC:, :] = jnp.zeros((WIDE - OUTC, 2 * C), BF16)


def cost(macs, bytes_accessed):
    return pl.CostEstimate(flops=2 * macs, bytes_accessed=bytes_accessed, transcendentals=0)


def call(kernel, name, estimate, limit=LIMIT, **rest):
    return pl.pallas_call(
        kernel,
        name=name,
        cost_estimate=estimate,
        compiler_params=pltpu.CompilerParams(vmem_limit_bytes=limit * 2**20),
        **rest,
    )


def swap_rows(block):
    return lax.ppermute(block, "row", [(0, 1), (1, 0)])


def to_later_frames(block):
    return lax.ppermute(block, "tm", [(i, i + 1) for i in range(lax.axis_size("tm") - 1)])


def across_columns(block):
    count = lax.axis_size("col")
    route = [(i, i - 1) for i in range(1, count)]
    route += [(count + i, count + i + 1) for i in range(count - 1)]
    return lax.ppermute(block, ("row", "col"), route)


def on_device(
    latents, norm_gain, conv_weight, conv_bias, time_weight, time_bias, spatial_weight, spatial_bias
):
    last_col = lax.axis_size("col") - 1
    other = swap_rows(latents)
    own = latents
    spatial_weight = jnp.swapaxes(spatial_weight, 2, 3)
    held = call(
        own_edge_kernel,
        "own_edge",
        cost(2**33, 2**20),
        out_shape=jax.ShapeDtypeStruct((8, 8, C), F32),
        in_specs=[VMEM],
        out_specs=VMEM,
    )(own)
    edge = call(
        edge_kernel,
        "edge",
        cost(2**33, 2**20),
        out_shape=jax.ShapeDtypeStruct((4, 2, 8, C), BF16),
        in_specs=[VMEM] * 2,
        out_specs=VMEM,
        scratch_shapes=[pltpu.VMEM((8, 8, C), F32)],
    )(held, other)
    mine = across_columns(edge)

    inner_shape = jax.ShapeDtypeStruct((MROWS * W, 2 * C), F32)
    inner_patches = pltpu.VMEM((MROWS * W, 9 * C), BF16)
    inner_cost = cost(2 * MROWS * W * 9 * C * C, 7 * 2**20)
    activated, edges, inner3, inner1 = call(
        activate_kernel,
        "activated",
        cost(4 * MROWS * W * 9 * C * C, 7 * 2**20),
        out_shape=(
            jax.ShapeDtypeStruct((4, MROWS + 2, W, C), BF16),
            jax.ShapeDtypeStruct((4, 2, 8, C), F32),
            inner_shape,
            inner_shape,
        ),
        in_specs=[VMEM] * 4,
        out_specs=(VMEM,) * 4,
        scratch_shapes=[inner_patches, inner_patches],
    )(own, other, norm_gain, conv_weight)
    mine, activated = lax.optimization_barrier((mine, activated))
    theirs = swap_rows(mine)
    inner2 = call(
        inner_kernel,
        "inner",
        inner_cost,
        out_shape=inner_shape,
        in_specs=[VMEM] * 2,
        out_specs=VMEM,
        scratch_shapes=[inner_patches],
    )(activated, conv_weight)

    mixed_shape = jax.ShapeDtypeStruct((2, BLOCK, C), BF16)
    onward, crossing = call(
        send_kernel,
        "partial_for_next",
        cost(2 * 96 * 9 * C * C, 10 * 2**20),
        out_shape=(mixed_shape, jax.ShapeDtypeStruct((2, BLOCK, C), F32)),
        in_specs=[VMEM] * 8,
        out_specs=(VMEM,) * 2,
        scratch_shapes=[pltpu.VMEM((96, 9 * C), BF16), pltpu.VMEM((3, BLOCK, 2 * C), F32)],
    )(edges, mine, theirs, norm_gain, conv_weight, inner1, inner2, inner3)
    onward = to_later_frames(onward)

    line = pltpu.VMEM((4, 2, 8, C), F32)
    mixed, patches = call(
        own_kernel,
        "mixed_last",
        cost(3 * BLOCK * 9 * C * C, 10 * 2**20),
        out_shape=(mixed_shape, jax.ShapeDtypeStruct((BLOCK, 9 * C), BF16)),
        in_specs=[VMEM] * 10,
        out_specs=(VMEM,) * 2,
        scratch_shapes=[pltpu.VMEM((2 * BLOCK, 9 * C), BF16), line],
    )(activated, edges, norm_gain, conv_weight, crossing, own, other, mine, theirs, conv_bias)
    previous = to_later_frames(mixed)

    out_shape = jax.ShapeDtypeStruct((8, 2 * OWN, 2 * W, OUTC), BF16)
    scratch = 2 * [
        pltpu.VMEM((BLOCK, 2 * C), F32),
        pltpu.VMEM((2, OWN + 2, W, 3 * C), BF16),
        pltpu.VMEM((2, 2, 2 * OWN, 2 * W, 128), F32),
        pltpu.VMEM((2, 2 * OWN, 2 * W, OUTC), BF16),
        pltpu.SemaphoreType.DMA((2,)),
    ]
    late_cost = cost(2 * BLOCK * 6 * C * C + 16 * 512 * C * WIDE, 6 * 2**20)

    part, spatial = call(
        first_part_kernel,
        "mixed_first",
        cost(3 * BLOCK * 9 * C * C, 10 * 2**20),
        out_shape=(
            jax.ShapeDtypeStruct((2, BLOCK, C), F32),
            jax.ShapeDtypeStruct((4, 2, WIDE, 2 * C), BF16),
        ),
        in_specs=[VMEM] * 11,
        out_specs=(VMEM,) * 2,
        scratch_shapes=[pltpu.VMEM((BLOCK, 9 * C), BF16), line],
    )(
        patches, activated, edges, norm_gain, conv_weight, own, other, mine, theirs, conv_bias,
        spatial_weight,
    )

    def last_frames(*refs):
        last_frames_kernel(last_col, *refs)

    begun, half_done = call(
        last_frames,
        "upsample_last",
        late_cost,
        out_shape=(jax.ShapeDtypeStruct((2, BLOCK, 2 * C), F32), out_shape),
        in_specs=[VMEM] * 7,
        out_specs=(VMEM, HBM),
        scratch_shapes=scratch,
    )(part, onward, mixed, time_weight, time_bias, spatial, spatial_bias)

    def first_frames(*refs):
        first_frames_kernel(last_col, *refs)

    return call(
        first_frames,
        "upsample_first",
        late_cost,
        out_shape=out_shape,
        in_specs=[VMEM] * 5 + [HBM],
        out_specs=HBM,
        scratch_shapes=scratch,
        input_output_aliases={5: 0},
    )(previous, begun, time_weight, spatial, spatial_bias, half_done)


def solution(mesh):
    placed = (P("tm", "row", "col", None), P(), P(), P(), P(), P(), P(), P())
    return jax.shard_map(
        on_device,
        mesh=mesh,
        in_specs=placed,
        out_specs=P("tm", "row", "col", None),
        check_vma=False,
    )
```

time: 37.4 us -> 34.3 us (0.917)
  waiting for transfers between devices: 8.23 us -> 5.44 us
  local copies, waits for them, and re-layouts: 1.75 us -> 1.1 us
  starting transfers between devices: 9.39 us -> 9.9 us
    ppermute x1, waiting for transfers between devices: 4.4 us -> 2.34 us  [across_columns(): return lax.ppermute(block, ('row', 'col'), route)]
    pallas_call x1, Pallas kernels: 4.09 us -> 3.33 us  [on_device(): call(first_frames, 'upsample_first', late_cost, out_shape=out_shape, in_s...]
    unnamed x18 -> x20, local copies, waits for them, and re-layouts: 1.75 us -> 1.1 us
    ppermute x2, starting transfers between devices: 0.01 us -> 0.62 us  [swap_rows(): return lax.ppermute(block, 'row', [(0, 1), (1, 0)])]
    pallas_call x6 -> x8, Pallas kernels: 13.5 us -> 14.1 us  [the longest x1 4.1 us: on_device(): call(last_frames, 'upsample_last', late_cost, out_shape=(jax.ShapeDtypeSt...]
    ppermute x2, waiting for transfers between devices: 1.32 us -> 0.83 us  [swap_rows(): return lax.ppermute(block, 'row', [(0, 1), (1, 0)])]
  transfers between devices with their start and end apart: 5 -> 5, of which waited for: 5 -> 4; matrix products, arithmetic and copies ran while one was open for 0% -> 0% of each run, Pallas kernels for 29% -> 38%
where the time goes in v2:
time: 34.3 us; the launch traced here: 34.2 us
  Pallas kernels  17.4 us (51%)
  starting transfers between devices  9.9 us (29%)
  waiting for transfers between devices  5.44 us (16%)
  local copies, waits for them, and re-layouts  1.1 us (3%)
    ppermute x2, starting transfers between devices, to_later_frames(): lax.ppermute(block, 'tm', [(i, i + 1) for i in range(lax.axis_size('tm')...  6.99 us
    pallas_call x1, Pallas kernels, on_device(): call(last_frames, 'upsample_last', late_cost, out_shape=(jax.ShapeDtypeSt...  4.1 us
    pallas_call x1, Pallas kernels, on_device(): call(first_frames, 'upsample_first', late_cost, out_shape=out_shape, in_s...  3.33 us
    pallas_call x1, Pallas kernels, on_device(): call(activate_kernel, 'activated', cost(4 * MROWS * W * 9 * C * C, 7 * 2...  2.76 us
    pallas_call x1, Pallas kernels, on_device(): call(first_part_kernel, 'mixed_first', cost(3 * BLOCK * 9 * C * C, 10 * 2...  2.43 us
    pallas_call x1, Pallas kernels, on_device(): call(own_kernel, 'mixed_last', cost(3 * BLOCK * 9 * C * C, 10 * 2 ** 20),...  2.35 us
    ppermute x1, waiting for transfers between devices, across_columns(): return lax.ppermute(block, ('row', 'col'), route)  2.34 us
    ppermute x1, starting transfers between devices, across_columns(): return lax.ppermute(block, ('row', 'col'), route)  2.28 us
  transfers between devices with their start and end apart: 5, of which 4 were waited for; matrix products, arithmetic and copies ran while one was open for 0% of the time, Pallas kernels for 38%

profile of v2, /device:TPU:104, one launch (start us, length us, event | category | flops | bytes accessed | tf_op | source)
XLA Modules:
  0.0 34.2 jit_solution(17013816929024403958)
XLA Ops:
  0.0 1.0 %copy-done = bf16[4,4,32,384]{3,2,1,0:T(8,128)(2,1)S(1)} copy-done((bf16[4,4,32,384]{3,2,1,0:T(8,128)(2,1)S(1)}, bf16[4,4,32,384]{3,2,1,0:T(8,128)(2,1)}, u32[]{:S(2)}) %copy-start) | copy-done | bytes 393240
  1.0 0.1 own_edge.1.held
  1.1 0.0 slice-start.1
  1.1 0.0 copy-start.1
  1.1 0.0 copy-start.4
  1.1 0.8 %collective-permute-done.other = bf16[4,4,32,384]{3,2,1,0:T(8,128)(2,1)S(1)} collective-permute-done((bf16[4,4,32,384]{3,2,1,0:T(8,128)(2,1)}, bf16[4,4,32,384]{3,2,1,0:T(8,128)(2,1)S(1)}, u32[]{:S(2)}, u32[]{:S(2)}) %collective-permute-start) | collective-permute-done | bytes 393248 | tf_op jit(solution)/shard_map/ppermute | solution.py:404
  1.9 0.1 edge.1
  2.0 2.3 %collective-permute-start.1 = (bf16[4,2,8,384]{3,2,1,0:T(8,128)(2,1)S(1)}, bf16[4,2,8,384]{3,2,1,0:T(8,128)(2,1)S(1)}, u32[]{:S(2)}, u32[]{:S(2)}) collective-permute-start(bf16[4,2,8,384]{3,2,1,0:T(8,128)(2,1)S(1)} %edge.1), channel_id=1, source_target_pairs={{1,0},{2,1},{3,2},{4,3},{5,4},{6,5},{7,6},{8,9},{9,10},{10,11},{11... | collective-permute-start | bytes 147464 | tf_op jit(solution)/shard_map/ppermute | solution.py:415
  4.3 0.1 slice-done.1
  4.4 2.8 %activated.1 = (bf16[4,7,32,384]{3,2,1,0:T(8,128)(2,1)S(1)}, f32[4,2,8,384]{3,2,1,0:T(8,128)S(1)}, f32[160,768]{1,0:T(8,128)S(1)}, f32[160,768]{1,0:T(8,128)S(1)}) custom-call(bf16[4,4,32,384]{3,2,1,0:T(8,128)(2,1)S(1)} %copy-done.1, bf16[4,4,32,384]{3,2,1,0:T(8,128)(2,1)S(1)} %collective-permute-done.other, f32[384]{0:T(512)S(1)} %copy-done.4, ...), custom_call_target="tpu_custom_call" | custom-call | flops 1698693120 | bytes 7340032 | tf_op jit(solution)/shard_map/activated/pallas_call | solution.py:447
  7.1 2.3 %collective-permute-done.1.mine = bf16[4,2,8,384]{3,2,1,0:T(8,128)(2,1)S(1)} collective-permute-done((bf16[4,2,8,384]{3,2,1,0:T(8,128)(2,1)S(1)}, bf16[4,2,8,384]{3,2,1,0:T(8,128)(2,1)S(1)}, u32[]{:S(2)}, u32[]{:S(2)}) %collective-permute-start.1) | collective-permute-done | bytes 49184 | tf_op jit(solution)/shard_map/ppermute | solution.py:415
  9.5 0.6 %collective-permute-start.2 = (bf16[4,2,8,384]{3,2,1,0:T(8,128)(2,1)S(1)}, bf16[4,2,8,384]{3,2,1,0:T(8,128)(2,1)S(1)}, u32[]{:S(2)}, u32[]{:S(2)}) collective-permute-start(bf16[4,2,8,384]{3,2,1,0:T(8,128)(2,1)S(1)} %collective-permute-done.1.mine), channel_id=1, source_target_pairs={{0,8},{8,0},{1,9},{9,1},{2,10},{10,2},{3,11},{11,3},{4,12},{12,4},... | collective-permute-start | bytes 147464 | tf_op jit(solution)/shard_map/ppermute | solution.py:404
  10.1 1.1 %inner.1.inner2 = f32[160,768]{1,0:T(8,128)S(1)} custom-call(bf16[4,7,32,384]{3,2,1,0:T(8,128)(2,1)S(1)} %get-tuple-element.20.activated, bf16[3,3,3,384,384]{4,3,2,1,0:T(8,128)(2,1)S(1)} %bitcast.2), custom_call_target="tpu_custom_call" | custom-call | flops 849346560 | bytes 7340032 | tf_op jit(solution)/shard_map/inner/pallas_call | solution.py:463
  11.2 0.0 copy-start.5
  11.3 1.2 %partial_for_next.1 = (bf16[2,176,384]{2,1,0:T(8,128)(2,1)S(1)}, f32[2,176,384]{2,1,0:T(8,128)S(1)}) custom-call(f32[4,2,8,384]{3,2,1,0:T(8,128)S(1)} %get-tuple-element.21.edges, bf16[4,2,8,384]{3,2,1,0:T(8,128)(2,1)S(1)} %collective-permute-done.1.mine, bf16[4,2,8,384]{3,2,1,0:T(8,128)(2,1)S(1)} %collective-permute-done.2.theirs, f32[384]{0:T(512)S(1)} %copy-done.4, ...), custom_call_target="tpu_custom_call" | custom-call | flops 509607936 | bytes 10485760 | tf_op jit(solution)/shard_map/partial_for_next/pallas_call | solution.py:474
  12.4 3.4 %collective-permute-start.4 = (bf16[2,176,384]{2,1,0:T(8,128)(2,1)S(1)}, bf16[2,176,384]{2,1,0:T(8,128)(2,1)S(1)}, u32[]{:S(2)}, u32[]{:S(2)}) collective-permute-start(bf16[2,176,384]{2,1,0:T(8,128)(2,1)S(1)} %get-tuple-element.29), channel_id=1, source_target_pairs={{0,16},{16,32},{32,48},{48,64},{64,80},{80,96},{96,112},{112,128},... | collective-permute-start | bytes 811016 | tf_op jit(solution)/shard_map/ppermute | solution.py:408
  15.8 2.4 %mixed_last.1 = (bf16[2,176,384]{2,1,0:T(8,128)(2,1)S(1)}, bf16[176,3456]{1,0:T(8,128)(2,1)S(1)}) custom-call(bf16[4,7,32,384]{3,2,1,0:T(8,128)(2,1)S(1)} %get-tuple-element.20.activated, f32[4,2,8,384]{3,2,1,0:T(8,128)S(1)} %get-tuple-element.21.edges, f32[384]{0:T(512)S(1)} %copy-done.4, bf16[3,3,3,384,384]{4,3,2,1,0:T(8,128)(2,1)S(1)} %bitcast.2, ...), custom_call_target="tpu_custom_call" | custom-call | flops 1401421824 | bytes 10485760 | tf_op jit(solution)/shard_map/mixed_last/pallas_call | solution.py:486
  18.2 3.6 %collective-permute-start.3 = (bf16[2,176,384]{2,1,0:T(8,128)(2,1)S(1)}, bf16[2,176,384]{2,1,0:T(8,128)(2,1)S(1)}, u32[]{:S(2)}, u32[]{:S(2)}) collective-permute-start(bf16[2,176,384]{2,1,0:T(8,128)(2,1)S(1)} %get-tuple-element.26.refs_2_), channel_id=1, source_target_pairs={{0,16},{16,32},{32,48},{48,64},{64,80},{80,96},{96,112},{112,128},... | collective-permute-start | bytes 811016 | tf_op jit(solution)/shard_map/ppermute | solution.py:408
  21.8 0.0 copy-start.2
  21.8 2.4 %mixed_first.1 = (f32[2,176,384]{2,1,0:T(8,128)S(1)}, bf16[4,2,256,768]{3,2,1,0:T(8,128)(2,1)S(1)}) custom-call(bf16[176,3456]{1,0:T(8,128)(2,1)S(1)} %get-tuple-element.27.patches, bf16[4,7,32,384]{3,2,1,0:T(8,128)(2,1)S(1)} %get-tuple-element.20.activated, f32[4,2,8,384]{3,2,1,0:T(8,128)S(1)} %get-tuple-element.21.edges, f32[384]{0:T(512)S(1)} %copy-done.4, ...), custom_call_target="tpu_custom_call" | custom-call | flops 1401421824 | bytes 10485760 | tf_op jit(solution)/shard_map/mixed_first/pallas_call | solution.py:507
  24.3 0.8 %collective-permute-done.4.refs_1_ = bf16[2,176,384]{2,1,0:T(8,128)(2,1)S(1)} collective-permute-done((bf16[2,176,384]{2,1,0:T(8,128)(2,1)S(1)}, bf16[2,176,384]{2,1,0:T(8,128)(2,1)S(1)}, u32[]{:S(2)}, u32[]{:S(2)}) %collective-permute-start.4) | collective-permute-done | bytes 270368 | tf_op jit(solution)/shard_map/ppermute | solution.py:408
  25.1 4.1 %upsample_last.1 = (f32[2,176,768]{2,1,0:T(8,128)S(1)}, bf16[8,8,64,192]{3,2,1,0:T(8,128)(2,1)}) custom-call(f32[2,176,384]{2,1,0:T(8,128)S(1)} %get-tuple-element.28.refs_0_, bf16[2,176,384]{2,1,0:T(8,128)(2,1)S(1)} %collective-permute-done.4.refs_1_, bf16[2,176,384]{2,1,0:T(8,128)(2,1)S(1)} %get-tuple-element.26.refs_2_, ...), custom_call_target="tpu_custom_call" | custom-call | flops 2233466880 | bytes 6291456 | tf_op jit(solution)/shard_map/upsample_last/pallas_call | solution.py:526
  29.2 1.5 %collective-permute-done.3.refs_0_ = bf16[2,176,384]{2,1,0:T(8,128)(2,1)S(1)} collective-permute-done((bf16[2,176,384]{2,1,0:T(8,128)(2,1)S(1)}, bf16[2,176,384]{2,1,0:T(8,128)(2,1)S(1)}, u32[]{:S(2)}, u32[]{:S(2)}) %collective-permute-start.3) | collective-permute-done | bytes 270368 | tf_op jit(solution)/shard_map/ppermute | solution.py:408
  30.7 3.3 %upsample_first.1 = bf16[8,8,64,192]{3,2,1,0:T(8,128)(2,1)} custom-call(bf16[2,176,384]{2,1,0:T(8,128)(2,1)S(1)} %collective-permute-done.3.refs_0_, f32[2,176,768]{2,1,0:T(8,128)S(1)} %get-tuple-element.31.refs_1_, bf16[3,384,768]{2,1,0:T(8,128)(2,1)S(1)} %copy-done.2, ...), custom_call_target="tpu_custom_call", output_to_operand_aliasing={{}: (5, {})} | custom-call | flops 2233466880 | bytes 6291456 | tf_op jit(solution)/shard_map/upsample_first/pallas_call | solution.py:539
  (16 shorter events, 0.0 us)
Async XLA Ops:
  0.0 1.9 %collective-permute-start = (bf16[4,4,32,384]{3,2,1,0:T(8,128)(2,1)}, bf16[4,4,32,384]{3,2,1,0:T(8,128)(2,1)S(1)}, u32[]{:S(2)}, u32[]{:S(2)}) collective-permute-start(bf16[4,4,32,384]{3,2,1,0:T(8,128)(2,1)} %own.7), channel_id=1, source_target_pairs={{0,8},{8,0},{1,9},{9,1},{2,10},{10,2},{3,11},{11,3},{4,12},{12,4},... | collective-permute-start | bytes 1179656 | tf_op jit(solution)/shard_map/ppermute | solution.py:404
  0.0 1.0 %copy-start = (bf16[4,4,32,384]{3,2,1,0:T(8,128)(2,1)S(1)}, bf16[4,4,32,384]{3,2,1,0:T(8,128)(2,1)}, u32[]{:S(2)}) copy-start(bf16[4,4,32,384]{3,2,1,0:T(8,128)(2,1)} %own.7) | copy-start | bytes 1179652
  1.0 3.3 %slice-start = ((s8[7962624]{0:T(1024)(128)(4,1)}), s8[4194304]{0:T(1024)(128)(4,1)S(1)}, s32[]{:S(2)}) async-start(s8[7962624]{0:T(1024)(128)(4,1)} %bitcast.1), calls=%async_computation | async-start | bytes 8388608
  1.1 3.3 %slice-start.1 = ((s8[7962624]{0:T(1024)(128)(4,1)}), s8[3768320]{0:T(1024)(128)(4,1)S(1)}, s32[]{:S(2)}) async-start(s8[7962624]{0:T(1024)(128)(4,1)} %bitcast.1), calls=%async_computation.1 | async-start | bytes 7536640
  1.1 3.3 %copy-start.1 = (bf16[4,4,32,384]{3,2,1,0:T(8,128)(2,1)S(1)}, bf16[4,4,32,384]{3,2,1,0:T(8,128)(2,1)}, u32[]{:S(2)}) copy-start(bf16[4,4,32,384]{3,2,1,0:T(8,128)(2,1)} %own.7) | copy-start | bytes 1179652
  1.1 3.3 %copy-start.4 = (f32[384]{0:T(512)S(1)}, f32[384]{0:T(512)}, u32[]{:S(2)}) copy-start(f32[384]{0:T(512)} %gain.7) | copy-start | bytes 4612
  2.0 7.5 %collective-permute-start.1 = (bf16[4,2,8,384]{3,2,1,0:T(8,128)(2,1)S(1)}, bf16[4,2,8,384]{3,2,1,0:T(8,128)(2,1)S(1)}, u32[]{:S(2)}, u32[]{:S(2)}) collective-permute-start(bf16[4,2,8,384]{3,2,1,0:T(8,128)(2,1)S(1)} %edge.1), channel_id=1, source_target_pairs={{1,0},{2,1},{3,2},{4,3},{5,4},{6,5},{7,6},{8,9},{9,10},{10,11},{11... | collective-permute-start | bytes 147464 | tf_op jit(solution)/shard_map/ppermute | solution.py:415
  9.5 1.8 %collective-permute-start.2 = (bf16[4,2,8,384]{3,2,1,0:T(8,128)(2,1)S(1)}, bf16[4,2,8,384]{3,2,1,0:T(8,128)(2,1)S(1)}, u32[]{:S(2)}, u32[]{:S(2)}) collective-permute-start(bf16[4,2,8,384]{3,2,1,0:T(8,128)(2,1)S(1)} %collective-permute-done.1.mine), channel_id=1, source_target_pairs={{0,8},{8,0},{1,9},{9,1},{2,10},{10,2},{3,11},{11,3},{4,12},{12,4},... | collective-permute-start | bytes 147464 | tf_op jit(solution)/shard_map/ppermute | solution.py:404
  11.2 4.6 %copy-start.5 = (f32[384]{0:T(512)S(1)}, f32[384]{0:T(512)}, u32[]{:S(2)}) copy-start(f32[384]{0:T(512)} %bias.3) | copy-start | bytes 4612
  12.4 12.7 %collective-permute-start.4 = (bf16[2,176,384]{2,1,0:T(8,128)(2,1)S(1)}, bf16[2,176,384]{2,1,0:T(8,128)(2,1)S(1)}, u32[]{:S(2)}, u32[]{:S(2)}) collective-permute-start(bf16[2,176,384]{2,1,0:T(8,128)(2,1)S(1)} %get-tuple-element.29), channel_id=1, source_target_pairs={{0,16},{16,32},{32,48},{48,64},{64,80},{80,96},{96,112},{112,128},... | collective-permute-start | bytes 811016 | tf_op jit(solution)/shard_map/ppermute | solution.py:408
  15.8 6.0 %copy-start.3 = (bf16[3,3,384,192]{2,3,1,0:T(8,128)(2,1)S(1)}, bf16[3,3,384,192]{2,3,1,0:T(8,128)(2,1)}, u32[]{:S(2)}) copy-start(bf16[3,3,384,192]{2,3,1,0:T(8,128)(2,1)} %param.14) | copy-start | bytes 3981316
  18.2 12.5 %collective-permute-start.3 = (bf16[2,176,384]{2,1,0:T(8,128)(2,1)S(1)}, bf16[2,176,384]{2,1,0:T(8,128)(2,1)S(1)}, u32[]{:S(2)}, u32[]{:S(2)}) collective-permute-start(bf16[2,176,384]{2,1,0:T(8,128)(2,1)S(1)} %get-tuple-element.26.refs_2_), channel_id=1, source_target_pairs={{0,16},{16,32},{32,48},{48,64},{64,80},{80,96},{96,112},{112,128},... | collective-permute-start | bytes 811016 | tf_op jit(solution)/shard_map/ppermute | solution.py:408
  21.8 3.3 %copy-start.2 = (bf16[3,384,768]{2,1,0:T(8,128)(2,1)S(1)}, bf16[3,384,768]{2,1,0:T(8,128)(2,1)}, u32[]{:S(2)}) copy-start(bf16[3,384,768]{2,1,0:T(8,128)(2,1)} %refs_2_.1) | copy-start | bytes 5308420
  21.8 3.3 %copy-start.6 = (f32[192]{0:T(256)S(1)}, f32[192]{0:T(256)}, u32[]{:S(2)}) copy-start(f32[192]{0:T(256)} %refs_4_.3) | copy-start | bytes 2308
  21.8 3.3 %copy-start.7 = (f32[768]{0:T(1024)S(1)}, f32[768]{0:T(1024)}, u32[]{:S(2)}) copy-start(f32[768]{0:T(1024)} %refs_4_.2) | copy-start | bytes 9220

commit v3 on v2

--- a/solution.py
+++ b/solution.py
@@ -78,7 +78,7 @@
     scale = gain[...].reshape(1, C)
     edges[...] = jnp.zeros(edges.shape, F32)
 
-    def one(frame, carry):
+    def one(frame):
         for slot in range(MROWS + 2):
             if slot == 0:
                 values = other[frame, 2].astype(F32) * core.astype(F32)
@@ -94,11 +94,13 @@
             edges[frame, 0, slot : slot + 1, :] = values[0:1]
             edges[frame, 1, slot : slot + 1, :] = values[W - 1 : W]
             activated[frame, slot] = values.astype(BF16)
-        return carry
-
-    lax.fori_loop(0, 4, one, 0)
+
+    one(3)
     inner_products(3, activated, weight, third_patches, third)
+    one(1)
     inner_products(1, activated, weight, first_patches, first)
+    one(0)
+    one(2)
 
 
 def inner_kernel(activated, weight, total, patches):
@@ -126,12 +128,11 @@
                 ]
 
 
-def fill_patches(frame, at, activated, edges, columns, patches, line):
-    line[frame, 0] = columns[1]
-    line[frame, 1] = columns[2]
+def fill_patches(frame, at, activated, edges, outer, patches):
+    columns = [outer[frame, index] for index in range(4)]
     for slot in range(MROWS + 2):
-        left = line[frame, 0, slot : slot + 1, :]
-        right = line[frame, 1, slot : slot + 1, :]
+        left = outer[frame, 1, slot : slot + 1, :]
+        right = outer[frame, 2, slot : slot + 1, :]
         fill_rows(at, slot, activated[frame, slot].astype(F32), left, right, patches)
     fill_sides(at + MROWS * W, frame, edges, columns, patches, False)
 
@@ -172,14 +173,19 @@
 
 
 def send_kernel(
-    edges, mine, theirs, gain, weight, inner1, inner2, inner3, onward, crossing, sides, total
+    edges, mine, theirs, gain, weight, inner1, inner2, inner3, onward, crossing, outer, sides, total
 ):
     core = lax.axis_index("row")
     scale = gain[...].reshape(1, C)
-    for index in range(3):
-        columns = outer_columns(1 + index, mine, theirs, scale, core)
-        fill_sides(index * 32, 1 + index, edges, columns, sides, True)
+    for frame in (1, 2, 3):
+        columns = outer_columns(frame, mine, theirs, scale, core)
+        for index in range(4):
+            outer[frame, index] = columns[index]
+        fill_sides((frame - 1) * 32, frame, edges, columns, sides, True)
     extra = dot(sides[...], early_weight(weight))
+    columns = outer_columns(0, mine, theirs, scale, core)
+    for index in range(4):
+        outer[0, index] = columns[index]
     for index, inner in enumerate((inner1, inner2, inner3)):
         base = index * 32
         total[index, : MROWS * W] = inner[...]
@@ -212,41 +218,34 @@
 
 
 def own_kernel(
-    activated, edges, gain, weight, crossing, own, other, mine, theirs, bias, mixed, patches,
-    last_patches, line,
+    activated, edges, outer, weight, crossing, own, other, mine, theirs, bias, mixed, patches,
+    third_patches, fourth_patches,
 ):
     core = lax.axis_index("row")
     shift = bias[...].reshape(1, C)
-    scale = gain[...].reshape(1, C)
-
-    def fill(frame, target, at):
-        columns = outer_columns(frame, mine, theirs, scale, core)
-        fill_patches(frame, at, activated, edges, columns, target, line)
-
-    fill(2, last_patches, 0)
-    fill(3, last_patches, BLOCK)
-    late = dot(last_patches[...], step_weight(weight, 2))
-    fill(0, patches, 0)
+    fill_patches(3, 0, activated, edges, outer, fourth_patches)
+    late = dot(fourth_patches[...], step_weight(weight, 2))
+    fill_patches(2, 0, activated, edges, outer, third_patches)
+    fourth = base_rows(3, own, other, mine, theirs, shift, core)
+    mixed[1] = (fourth + late + crossing[1]).astype(BF16)
+    late = dot(third_patches[...], step_weight(weight, 2))
+    fill_patches(0, 0, activated, edges, outer, patches)
+    third = base_rows(2, own, other, mine, theirs, shift, core)
     early = dot(patches[...], step_weight(weight, 0))
-    fourth = base_rows(3, own, other, mine, theirs, shift, core)
-    mixed[1] = (fourth + late[BLOCK:] + crossing[1]).astype(BF16)
-    third = base_rows(2, own, other, mine, theirs, shift, core)
-    mixed[0] = (third + late[:BLOCK] + crossing[0] + early).astype(BF16)
+    mixed[0] = (third + late + crossing[0] + early).astype(BF16)
 
 
 def first_part_kernel(
-    patches, activated, edges, gain, weight, own, other, mine, theirs, bias, spatial_weight,
+    patches, activated, edges, outer, weight, own, other, mine, theirs, bias, spatial_weight,
     part, spatial,
-    second_patches, line,
+    second_patches,
 ):
     core = lax.axis_index("row")
     shift = bias[...].reshape(1, C)
-    scale = gain[...].reshape(1, C)
     both = jnp.concatenate([step_weight(weight, 1), step_weight(weight, 2)], axis=1)
     early = dot(patches[...], both)
     parity_weights(spatial_weight, spatial)
-    columns = outer_columns(1, mine, theirs, scale, core)
-    fill_patches(1, 0, activated, edges, columns, second_patches, line)
+    fill_patches(1, 0, activated, edges, outer, second_patches)
     part[0] = base_rows(0, own, other, mine, theirs, shift, core) + early[:, C:]
     late = dot(second_patches[...], step_weight(weight, 2))
     part[1] = base_rows(1, own, other, mine, theirs, shift, core) + early[:, :C] + late
@@ -289,11 +288,9 @@
             result = shift
             for near in range(2):
                 rows = slice(parity_row + near, parity_row + near + OWN)
-                result = result + lax.dot_general(
+                result = result + dot(
                     framed[:, rows, :, lanes].reshape(2 * OWN * W, 2 * C),
                     spatial[phase, near],
-                    (((1,), (1,)), ((), ())),
-                    preferred_element_type=F32,
                 )
             for frame in range(2):
                 for row in range(OWN):
@@ -361,8 +358,8 @@
 
 
 def parity_weights(weight, phases):
-    for start in range(0, OUTC, 64):
-        part = slice(start, start + 64)
+    for start, count in ((0, 128), (128, OUTC - 128)):
+        part = slice(start, start + count)
         wide = [[weight[row, col, part, :].astype(F32) for col in range(3)] for row in range(3)]
         for parity_row in range(2):
             for near in range(2):
@@ -378,12 +375,13 @@
                     else:
                         pair = [taps[0] + taps[1], taps[2]]
                     for index in range(2):
-                        phases[phase, near, part, index * C : (index + 1) * C] = pair[index].astype(
-                            BF16
+                        block = pair[index]
+                        if count < 128:
+                            none = jnp.zeros((128 - count, C), F32)
+                            block = jnp.concatenate([block, none], axis=0)
+                        phases[phase, near, index * C : (index + 1) * C, start : start + 128] = (
+                            block.T.astype(BF16)
                         )
-    for phase in range(4):
-        for near in range(2):
-            phases[phase, near, OUTC:, :] = jnp.zeros((WIDE - OUTC, 2 * C), BF16)
 
 
 def cost(macs, bytes_accessed):
@@ -471,18 +469,22 @@
     )(activated, conv_weight)
 
     mixed_shape = jax.ShapeDtypeStruct((2, BLOCK, C), BF16)
-    onward, crossing = call(
+    onward, crossing, outer = call(
         send_kernel,
         "partial_for_next",
         cost(2 * 96 * 9 * C * C, 10 * 2**20),
-        out_shape=(mixed_shape, jax.ShapeDtypeStruct((2, BLOCK, C), F32)),
+        out_shape=(
+            mixed_shape,
+            jax.ShapeDtypeStruct((2, BLOCK, C), F32),
+            jax.ShapeDtypeStruct((4, 4, 8, C), F32),
+        ),
         in_specs=[VMEM] * 8,
-        out_specs=(VMEM,) * 2,
+        out_specs=(VMEM,) * 3,
         scratch_shapes=[pltpu.VMEM((96, 9 * C), BF16), pltpu.VMEM((3, BLOCK, 2 * C), F32)],
     )(edges, mine, theirs, norm_gain, conv_weight, inner1, inner2, inner3)
     onward = to_later_frames(onward)
 
-    line = pltpu.VMEM((4, 2, 8, C), F32)
+    frame_patches = pltpu.VMEM((BLOCK, 9 * C), BF16)
     mixed, patches = call(
         own_kernel,
         "mixed_last",
@@ -490,8 +492,8 @@
         out_shape=(mixed_shape, jax.ShapeDtypeStruct((BLOCK, 9 * C), BF16)),
         in_specs=[VMEM] * 10,
         out_specs=(VMEM,) * 2,
-        scratch_shapes=[pltpu.VMEM((2 * BLOCK, 9 * C), BF16), line],
-    )(activated, edges, norm_gain, conv_weight, crossing, own, other, mine, theirs, conv_bias)
+        scratch_shapes=[frame_patches, frame_patches],
+    )(activated, edges, outer, conv_weight, crossing, own, other, mine, theirs, conv_bias)
     previous = to_later_frames(mixed)
 
     out_shape = jax.ShapeDtypeStruct((8, 2 * OWN, 2 * W, OUTC), BF16)
@@ -510,13 +512,13 @@
         cost(3 * BLOCK * 9 * C * C, 10 * 2**20),
         out_shape=(
             jax.ShapeDtypeStruct((2, BLOCK, C), F32),
-            jax.ShapeDtypeStruct((4, 2, WIDE, 2 * C), BF16),
+            jax.ShapeDtypeStruct((4, 2, 2 * C, WIDE), BF16),
         ),
         in_specs=[VMEM] * 11,
         out_specs=(VMEM,) * 2,
-        scratch_shapes=[pltpu.VMEM((BLOCK, 9 * C), BF16), line],
+        scratch_shapes=[frame_patches],
     )(
-        patches, activated, edges, norm_gain, conv_weight, own, other, mine, theirs, conv_bias,
+        patches, activated, edges, outer, conv_weight, own, other, mine, theirs, conv_bias,
         spatial_weight,
     )
 

time: 34.3 us -> 34.2 us (level)
  waiting for transfers between devices: 5.44 us -> 6.16 us
  starting transfers between devices: 9.9 us -> 9.44 us
  Pallas kernels: 17.4 us -> 17 us
    ppermute x2, starting transfers between devices: 0.62 us -> 0.18 us  [swap_rows(): return lax.ppermute(block, 'row', [(0, 1), (1, 0)])]
    pallas_call x1, Pallas kernels: 2.76 us -> 2.31 us  [on_device(): call(activate_kernel, 'activated', cost(4 * MROWS * W * 9 * C * C, 7 * 2...]
    ppermute x1, waiting for transfers between devices: 2.34 us -> 2.78 us  [across_columns(): return lax.ppermute(block, ('row', 'col'), route)]
  transfers between devices with their start and end apart: 5 -> 5, of which waited for: 4 -> 4; matrix products, arithmetic and copies ran while one was open for 0% -> 0% of each run, Pallas kernels for 38% -> 36%
where the time goes in v3:
time: 34.2 us; the launch traced here: 34.1 us
  Pallas kernels  17 us (50%)
  starting transfers between devices  9.44 us (28%)
  waiting for transfers between devices  6.16 us (18%)
  local copies, waits for them, and re-layouts  1.1 us (3%)
    ppermute x2, starting transfers between devices, to_later_frames(): lax.ppermute(block, 'tm', [(i, i + 1) for i in range(lax.axis_size('tm')...  6.98 us
    pallas_call x1, Pallas kernels, on_device(): call(last_frames, 'upsample_last', late_cost, out_shape=(jax.ShapeDtypeSt...  4.14 us
    pallas_call x1, Pallas kernels, on_device(): call(first_frames, 'upsample_first', late_cost, out_shape=out_shape, in_s...  3.4 us
    ppermute x1, waiting for transfers between devices, across_columns(): return lax.ppermute(block, ('row', 'col'), route)  2.78 us
    ppermute x2, waiting for transfers between devices, to_later_frames(): lax.ppermute(block, 'tm', [(i, i + 1) for i in range(lax.axis_size('tm')...  2.55 us
    pallas_call x1, Pallas kernels, on_device(): call(first_part_kernel, 'mixed_first', cost(3 * BLOCK * 9 * C * C, 10 * 2...  2.45 us
    pallas_call x1, Pallas kernels, on_device(): call(activate_kernel, 'activated', cost(4 * MROWS * W * 9 * C * C, 7 * 2...  2.31 us
    pallas_call x1, Pallas kernels, on_device(): call(own_kernel, 'mixed_last', cost(3 * BLOCK * 9 * C * C, 10 * 2 ** 20),...  2.28 us
  transfers between devices with their start and end apart: 5, of which 4 were waited for; matrix products, arithmetic and copies ran while one was open for 0% of the time, Pallas kernels for 36%

profile of v3, /device:TPU:104, one launch (start us, length us, event | category | flops | bytes accessed | tf_op | source)
XLA Modules:
  0.0 34.1 jit_solution(7808764797832656311)
XLA Ops:
  0.0 1.0 %copy-done = bf16[4,4,32,384]{3,2,1,0:T(8,128)(2,1)S(1)} copy-done((bf16[4,4,32,384]{3,2,1,0:T(8,128)(2,1)S(1)}, bf16[4,4,32,384]{3,2,1,0:T(8,128)(2,1)}, u32[]{:S(2)}) %copy-start) | copy-done | bytes 393240
  1.0 0.1 own_edge.1.held
  1.1 0.0 slice-start.1
  1.1 0.0 copy-start.1
  1.1 0.0 copy-start.4
  1.1 0.8 %collective-permute-done.other = bf16[4,4,32,384]{3,2,1,0:T(8,128)(2,1)S(1)} collective-permute-done((bf16[4,4,32,384]{3,2,1,0:T(8,128)(2,1)}, bf16[4,4,32,384]{3,2,1,0:T(8,128)(2,1)S(1)}, u32[]{:S(2)}, u32[]{:S(2)}) %collective-permute-start) | collective-permute-done | bytes 393248 | tf_op jit(solution)/shard_map/ppermute | solution.py:402
  1.9 0.1 edge.1
  2.0 2.3 %collective-permute-start.1 = (bf16[4,2,8,384]{3,2,1,0:T(8,128)(2,1)S(1)}, bf16[4,2,8,384]{3,2,1,0:T(8,128)(2,1)S(1)}, u32[]{:S(2)}, u32[]{:S(2)}) collective-permute-start(bf16[4,2,8,384]{3,2,1,0:T(8,128)(2,1)S(1)} %edge.1), channel_id=1, source_target_pairs={{1,0},{2,1},{3,2},{4,3},{5,4},{6,5},{7,6},{8,9},{9,10},{10,11},{11... | collective-permute-start | bytes 147464 | tf_op jit(solution)/shard_map/ppermute | solution.py:413
  4.3 0.1 slice-done.1
  4.4 2.3 %activated.1 = (bf16[4,7,32,384]{3,2,1,0:T(8,128)(2,1)S(1)}, f32[4,2,8,384]{3,2,1,0:T(8,128)S(1)}, f32[160,768]{1,0:T(8,128)S(1)}, f32[160,768]{1,0:T(8,128)S(1)}) custom-call(bf16[4,4,32,384]{3,2,1,0:T(8,128)(2,1)S(1)} %copy-done.1, bf16[4,4,32,384]{3,2,1,0:T(8,128)(2,1)S(1)} %collective-permute-done.other, f32[384]{0:T(512)S(1)} %copy-done.4, ...), custom_call_target="tpu_custom_call" | custom-call | flops 1698693120 | bytes 7340032 | tf_op jit(solution)/shard_map/activated/pallas_call | solution.py:445
  6.7 2.8 %collective-permute-done.1.mine = bf16[4,2,8,384]{3,2,1,0:T(8,128)(2,1)S(1)} collective-permute-done((bf16[4,2,8,384]{3,2,1,0:T(8,128)(2,1)S(1)}, bf16[4,2,8,384]{3,2,1,0:T(8,128)(2,1)S(1)}, u32[]{:S(2)}, u32[]{:S(2)}) %collective-permute-start.1) | collective-permute-done | bytes 49184 | tf_op jit(solution)/shard_map/ppermute | solution.py:413
  9.5 0.2 collective-permute-start.2
  9.6 1.2 %inner.1.inner2 = f32[160,768]{1,0:T(8,128)S(1)} custom-call(bf16[4,7,32,384]{3,2,1,0:T(8,128)(2,1)S(1)} %get-tuple-element.21.activated, bf16[3,3,3,384,384]{4,3,2,1,0:T(8,128)(2,1)S(1)} %bitcast.2), custom_call_target="tpu_custom_call" | custom-call | flops 849346560 | bytes 7340032 | tf_op jit(solution)/shard_map/inner/pallas_call | solution.py:461
  10.8 1.2 %partial_for_next.1 = (bf16[2,176,384]{2,1,0:T(8,128)(2,1)S(1)}, f32[2,176,384]{2,1,0:T(8,128)S(1)}, f32[4,4,8,384]{3,2,1,0:T(8,128)S(1)}) custom-call(f32[4,2,8,384]{3,2,1,0:T(8,128)S(1)} %get-tuple-element.22.edges, bf16[4,2,8,384]{3,2,1,0:T(8,128)(2,1)S(1)} %collective-permute-done.1.mine, bf16[4,2,8,384]{3,2,1,0:T(8,128)(2,1)S(1)} %collective-permute-done.2.theirs, ...), custom_call_target="tpu_custom_call" | custom-call | flops 509607936 | bytes 10485760 | tf_op jit(solution)/shard_map/partial_for_next/pallas_call | solution.py:472
  12.0 3.4 %collective-permute-start.4 = (bf16[2,176,384]{2,1,0:T(8,128)(2,1)S(1)}, bf16[2,176,384]{2,1,0:T(8,128)(2,1)S(1)}, u32[]{:S(2)}, u32[]{:S(2)}) collective-permute-start(bf16[2,176,384]{2,1,0:T(8,128)(2,1)S(1)} %get-tuple-element.31), channel_id=1, source_target_pairs={{0,16},{16,32},{32,48},{48,64},{64,80},{80,96},{96,112},{112,128},... | collective-permute-start | bytes 811016 | tf_op jit(solution)/shard_map/ppermute | solution.py:406
  15.4 2.3 %mixed_last.1 = (bf16[2,176,384]{2,1,0:T(8,128)(2,1)S(1)}, bf16[176,3456]{1,0:T(8,128)(2,1)S(1)}) custom-call(bf16[4,7,32,384]{3,2,1,0:T(8,128)(2,1)S(1)} %get-tuple-element.21.activated, f32[4,2,8,384]{3,2,1,0:T(8,128)S(1)} %get-tuple-element.22.edges, f32[4,4,8,384]{3,2,1,0:T(8,128)S(1)} %get-tuple-element.26.outer, ...), custom_call_target="tpu_custom_call" | custom-call | flops 1401421824 | bytes 10485760 | tf_op jit(solution)/shard_map/mixed_last/pallas_call | solution.py:488
  17.7 3.6 %collective-permute-start.3 = (bf16[2,176,384]{2,1,0:T(8,128)(2,1)S(1)}, bf16[2,176,384]{2,1,0:T(8,128)(2,1)S(1)}, u32[]{:S(2)}, u32[]{:S(2)}) collective-permute-start(bf16[2,176,384]{2,1,0:T(8,128)(2,1)S(1)} %get-tuple-element.28.refs_2_), channel_id=1, source_target_pairs={{0,16},{16,32},{32,48},{48,64},{64,80},{80,96},{96,112},{112,128},... | collective-permute-start | bytes 811016 | tf_op jit(solution)/shard_map/ppermute | solution.py:406
  21.3 0.0 copy-start.2
  21.3 0.0 copy-start.6
  21.4 2.4 %mixed_first.1 = (f32[2,176,384]{2,1,0:T(8,128)S(1)}, bf16[4,2,768,256]{3,2,1,0:T(8,128)(2,1)S(1)}) custom-call(bf16[176,3456]{1,0:T(8,128)(2,1)S(1)} %get-tuple-element.29.patches, bf16[4,7,32,384]{3,2,1,0:T(8,128)(2,1)S(1)} %get-tuple-element.21.activated, f32[4,2,8,384]{3,2,1,0:T(8,128)S(1)} %get-tuple-element.22.edges, ...), custom_call_target="tpu_custom_call" | custom-call | flops 1401421824 | bytes 10485760 | tf_op jit(solution)/shard_map/mixed_first/pallas_call | solution.py:509
  23.8 1.2 %collective-permute-done.4.refs_1_ = bf16[2,176,384]{2,1,0:T(8,128)(2,1)S(1)} collective-permute-done((bf16[2,176,384]{2,1,0:T(8,128)(2,1)S(1)}, bf16[2,176,384]{2,1,0:T(8,128)(2,1)S(1)}, u32[]{:S(2)}, u32[]{:S(2)}) %collective-permute-start.4) | collective-permute-done | bytes 270368 | tf_op jit(solution)/shard_map/ppermute | solution.py:406
  25.0 4.1 %upsample_last.1 = (f32[2,176,768]{2,1,0:T(8,128)S(1)}, bf16[8,8,64,192]{3,2,1,0:T(8,128)(2,1)}) custom-call(f32[2,176,384]{2,1,0:T(8,128)S(1)} %get-tuple-element.30.refs_0_, bf16[2,176,384]{2,1,0:T(8,128)(2,1)S(1)} %collective-permute-done.4.refs_1_, bf16[2,176,384]{2,1,0:T(8,128)(2,1)S(1)} %get-tuple-element.28.refs_2_, ...), custom_call_target="tpu_custom_call" | custom-call | flops 2233466880 | bytes 6291456 | tf_op jit(solution)/shard_map/upsample_last/pallas_call | solution.py:528
  29.2 1.3 %collective-permute-done.3.refs_0_ = bf16[2,176,384]{2,1,0:T(8,128)(2,1)S(1)} collective-permute-done((bf16[2,176,384]{2,1,0:T(8,128)(2,1)S(1)}, bf16[2,176,384]{2,1,0:T(8,128)(2,1)S(1)}, u32[]{:S(2)}, u32[]{:S(2)}) %collective-permute-start.3) | collective-permute-done | bytes 270368 | tf_op jit(solution)/shard_map/ppermute | solution.py:406
  30.5 3.4 %upsample_first.1 = bf16[8,8,64,192]{3,2,1,0:T(8,128)(2,1)} custom-call(bf16[2,176,384]{2,1,0:T(8,128)(2,1)S(1)} %collective-permute-done.3.refs_0_, f32[2,176,768]{2,1,0:T(8,128)S(1)} %get-tuple-element.33.refs_1_, bf16[3,384,768]{2,1,0:T(8,128)(2,1)S(1)} %copy-done.2, ...), custom_call_target="tpu_custom_call", output_to_operand_aliasing={{}: (5, {})} | custom-call | flops 2233466880 | bytes 6291456 | tf_op jit(solution)/shard_map/upsample_first/pallas_call | solution.py:541
  (16 shorter events, 0.0 us)
Async XLA Ops:
  0.0 1.9 %collective-permute-start = (bf16[4,4,32,384]{3,2,1,0:T(8,128)(2,1)}, bf16[4,4,32,384]{3,2,1,0:T(8,128)(2,1)S(1)}, u32[]{:S(2)}, u32[]{:S(2)}) collective-permute-start(bf16[4,4,32,384]{3,2,1,0:T(8,128)(2,1)} %own.7), channel_id=1, source_target_pairs={{0,8},{8,0},{1,9},{9,1},{2,10},{10,2},{3,11},{11,3},{4,12},{12,4},... | collective-permute-start | bytes 1179656 | tf_op jit(solution)/shard_map/ppermute | solution.py:402
  0.0 1.0 %copy-start = (bf16[4,4,32,384]{3,2,1,0:T(8,128)(2,1)S(1)}, bf16[4,4,32,384]{3,2,1,0:T(8,128)(2,1)}, u32[]{:S(2)}) copy-start(bf16[4,4,32,384]{3,2,1,0:T(8,128)(2,1)} %own.7) | copy-start | bytes 1179652
  1.0 3.3 %slice-start = ((s8[7962624]{0:T(1024)(128)(4,1)}), s8[4194304]{0:T(1024)(128)(4,1)S(1)}, s32[]{:S(2)}) async-start(s8[7962624]{0:T(1024)(128)(4,1)} %bitcast.1), calls=%async_computation | async-start | bytes 8388608
  1.1 3.3 %slice-start.1 = ((s8[7962624]{0:T(1024)(128)(4,1)}), s8[3768320]{0:T(1024)(128)(4,1)S(1)}, s32[]{:S(2)}) async-start(s8[7962624]{0:T(1024)(128)(4,1)} %bitcast.1), calls=%async_computation.1 | async-start | bytes 7536640
  1.1 3.3 %copy-start.1 = (bf16[4,4,32,384]{3,2,1,0:T(8,128)(2,1)S(1)}, bf16[4,4,32,384]{3,2,1,0:T(8,128)(2,1)}, u32[]{:S(2)}) copy-start(bf16[4,4,32,384]{3,2,1,0:T(8,128)(2,1)} %own.7) | copy-start | bytes 1179652
  1.1 3.3 %copy-start.4 = (f32[384]{0:T(512)S(1)}, f32[384]{0:T(512)}, u32[]{:S(2)}) copy-start(f32[384]{0:T(512)} %gain.3) | copy-start | bytes 4612
  2.0 7.5 %collective-permute-start.1 = (bf16[4,2,8,384]{3,2,1,0:T(8,128)(2,1)S(1)}, bf16[4,2,8,384]{3,2,1,0:T(8,128)(2,1)S(1)}, u32[]{:S(2)}, u32[]{:S(2)}) collective-permute-start(bf16[4,2,8,384]{3,2,1,0:T(8,128)(2,1)S(1)} %edge.1), channel_id=1, source_target_pairs={{1,0},{2,1},{3,2},{4,3},{5,4},{6,5},{7,6},{8,9},{9,10},{10,11},{11... | collective-permute-start | bytes 147464 | tf_op jit(solution)/shard_map/ppermute | solution.py:413
  9.5 1.3 %collective-permute-start.2 = (bf16[4,2,8,384]{3,2,1,0:T(8,128)(2,1)S(1)}, bf16[4,2,8,384]{3,2,1,0:T(8,128)(2,1)S(1)}, u32[]{:S(2)}, u32[]{:S(2)}) collective-permute-start(bf16[4,2,8,384]{3,2,1,0:T(8,128)(2,1)S(1)} %collective-permute-done.1.mine), channel_id=1, source_target_pairs={{0,8},{8,0},{1,9},{9,1},{2,10},{10,2},{3,11},{11,3},{4,12},{12,4},... | collective-permute-start | bytes 147464 | tf_op jit(solution)/shard_map/ppermute | solution.py:402
  10.8 4.6 %copy-start.5 = (f32[384]{0:T(512)S(1)}, f32[384]{0:T(512)}, u32[]{:S(2)}) copy-start(f32[384]{0:T(512)} %bias.3) | copy-start | bytes 4612
  12.0 13.0 %collective-permute-start.4 = (bf16[2,176,384]{2,1,0:T(8,128)(2,1)S(1)}, bf16[2,176,384]{2,1,0:T(8,128)(2,1)S(1)}, u32[]{:S(2)}, u32[]{:S(2)}) collective-permute-start(bf16[2,176,384]{2,1,0:T(8,128)(2,1)S(1)} %get-tuple-element.31), channel_id=1, source_target_pairs={{0,16},{16,32},{32,48},{48,64},{64,80},{80,96},{96,112},{112,128},... | collective-permute-start | bytes 811016 | tf_op jit(solution)/shard_map/ppermute | solution.py:406
  15.4 5.9 %copy-start.3 = (bf16[3,3,384,192]{2,3,1,0:T(8,128)(2,1)S(1)}, bf16[3,3,384,192]{2,3,1,0:T(8,128)(2,1)}, u32[]{:S(2)}) copy-start(bf16[3,3,384,192]{2,3,1,0:T(8,128)(2,1)} %param.14) | copy-start | bytes 3981316
  17.7 12.8 %collective-permute-start.3 = (bf16[2,176,384]{2,1,0:T(8,128)(2,1)S(1)}, bf16[2,176,384]{2,1,0:T(8,128)(2,1)S(1)}, u32[]{:S(2)}, u32[]{:S(2)}) collective-permute-start(bf16[2,176,384]{2,1,0:T(8,128)(2,1)S(1)} %get-tuple-element.28.refs_2_), channel_id=1, source_target_pairs={{0,16},{16,32},{32,48},{48,64},{64,80},{80,96},{96,112},{112,128},... | collective-permute-start | bytes 811016 | tf_op jit(solution)/shard_map/ppermute | solution.py:406
  21.3 3.7 %copy-start.2 = (bf16[3,384,768]{2,1,0:T(8,128)(2,1)S(1)}, bf16[3,384,768]{2,1,0:T(8,128)(2,1)}, u32[]{:S(2)}) copy-start(bf16[3,384,768]{2,1,0:T(8,128)(2,1)} %refs_2_.1) | copy-start | bytes 5308420
  21.3 3.7 %copy-start.6 = (f32[192]{0:T(256)S(1)}, f32[192]{0:T(256)}, u32[]{:S(2)}) copy-start(f32[192]{0:T(256)} %refs_4_.3) | copy-start | bytes 2308
  21.3 3.7 %copy-start.7 = (f32[768]{0:T(1024)S(1)}, f32[768]{0:T(1024)}, u32[]{:S(2)}) copy-start(f32[768]{0:T(1024)} %refs_4_.2) | copy-start | bytes 9220

commit v4 on v3

--- a/solution.py
+++ b/solution.py
@@ -18,6 +18,7 @@
 MROWS = 5
 SIDE = 16
 BLOCK = MROWS * W + SIDE
+SENT = OWN * W + SIDE
 LIMIT = 24
 
 
@@ -72,7 +73,8 @@
 
 
 def activate_kernel(
-    own, other, gain, weight, activated, edges, third, first, third_patches, first_patches
+    own, other, gain, weight, activated, edges, third, first, second_patches,
+    third_patches, first_patches,
 ):
     core = lax.axis_index("row")
     scale = gain[...].reshape(1, C)
@@ -96,15 +98,18 @@
             activated[frame, slot] = values.astype(BF16)
 
     one(3)
-    inner_products(3, activated, weight, third_patches, third)
+    inner_patches(3, activated, third_patches)
+    third[...] = dot(third_patches[...], early_weight(weight))
     one(1)
-    inner_products(1, activated, weight, first_patches, first)
+    inner_patches(1, activated, first_patches)
+    first[...] = dot(first_patches[...], early_weight(weight))
+    one(2)
+    inner_patches(2, activated, second_patches)
     one(0)
-    one(2)
-
-
-def inner_kernel(activated, weight, total, patches):
-    inner_products(2, activated, weight, patches, total)
+
+
+def inner_kernel(patches, weight, total):
+    total[...] = dot(patches[...], early_weight(weight))
 
 
 def halo_columns(frame, mine, theirs, core):
@@ -158,10 +163,9 @@
     return jnp.concatenate([step_weight(weight, 0), step_weight(weight, 1)], axis=1)
 
 
-def inner_products(frame, activated, weight, patches, total):
+def inner_patches(frame, activated, patches):
     for slot in range(MROWS + 2):
         fill_rows(0, slot, activated[frame, slot].astype(F32), 0.0, 0.0, patches)
-    total[...] = dot(patches[...], early_weight(weight))
 
 
 def step_weight(weight, step):
@@ -195,8 +199,11 @@
                 line = slice(at, at + 1)
                 add = slice(base + side + row, base + side + row + 1)
                 total[index, line] = inner[line] + extra[add]
-    onward[0] = (total[1, :, :C] + total[2, :, C:]).astype(BF16)
-    onward[1] = total[2, :, :C].astype(BF16)
+    own = pl.ds(pl.multiple_of(core * W, W), OWN * W)
+    outer_rows = slice(MROWS * W, BLOCK)
+    for target, source in ((slice(0, OWN * W), own), (slice(OWN * W, SENT), outer_rows)):
+        onward[0, target] = (total[1, source, :C] + total[2, source, C:]).astype(BF16)
+        onward[1, target] = total[2, source, :C].astype(BF16)
     crossing[0] = total[0, :, C:]
     crossing[1] = total[0, :, :C] + total[1, :, C:]
 
@@ -326,11 +333,24 @@
 
 
 def last_frames_kernel(
-    last_col, part, onward, mixed, time, time_bias, spatial, spatial_bias, begun, target, *scratch
+    last_col, part, onward, near, mixed, time, time_bias, spatial, spatial_bias, begun, target,
+    *scratch,
 ):
     first_half, second_half = scratch[:5], scratch[5:]
-    first = (part[0] + onward[0].astype(F32)).astype(BF16)
-    second = (part[1] + onward[1].astype(F32)).astype(BF16)
+    core = lax.axis_index("row")
+
+    def whole_block(frame):
+        own = onward[frame, : OWN * W].astype(F32)
+        extra = near[frame].astype(F32)
+        rows = jnp.where(
+            core == 0,
+            jnp.concatenate([own, extra], axis=0),
+            jnp.concatenate([extra, own], axis=0),
+        )
+        return jnp.concatenate([rows, onward[frame, OWN * W :].astype(F32)], axis=0)
+
+    first = (part[0] + whole_block(0)).astype(BF16)
+    second = (part[1] + whole_block(1)).astype(BF16)
     whole = time[...].reshape(3 * C, 2 * C)
     shift = time_bias[...].reshape(1, 2 * C)
     first_half[0][...] = (
@@ -440,9 +460,8 @@
     mine = across_columns(edge)
 
     inner_shape = jax.ShapeDtypeStruct((MROWS * W, 2 * C), F32)
-    inner_patches = pltpu.VMEM((MROWS * W, 9 * C), BF16)
     inner_cost = cost(2 * MROWS * W * 9 * C * C, 7 * 2**20)
-    activated, edges, inner3, inner1 = call(
+    activated, edges, inner3, inner1, patches2 = call(
         activate_kernel,
         "activated",
         cost(4 * MROWS * W * 9 * C * C, 7 * 2**20),
@@ -451,12 +470,13 @@
             jax.ShapeDtypeStruct((4, 2, 8, C), F32),
             inner_shape,
             inner_shape,
+            jax.ShapeDtypeStruct((MROWS * W, 9 * C), BF16),
         ),
         in_specs=[VMEM] * 4,
-        out_specs=(VMEM,) * 4,
-        scratch_shapes=[inner_patches, inner_patches],
+        out_specs=(VMEM,) * 5,
+        scratch_shapes=2 * [pltpu.VMEM((MROWS * W, 9 * C), BF16)],
     )(own, other, norm_gain, conv_weight)
-    mine, activated = lax.optimization_barrier((mine, activated))
+    mine, activated, patches2 = lax.optimization_barrier((mine, activated, patches2))
     theirs = swap_rows(mine)
     inner2 = call(
         inner_kernel,
@@ -465,8 +485,7 @@
         out_shape=inner_shape,
         in_specs=[VMEM] * 2,
         out_specs=VMEM,
-        scratch_shapes=[inner_patches],
-    )(activated, conv_weight)
+    )(patches2, conv_weight)
 
     mixed_shape = jax.ShapeDtypeStruct((2, BLOCK, C), BF16)
     onward, crossing, outer = call(
@@ -474,7 +493,7 @@
         "partial_for_next",
         cost(2 * 96 * 9 * C * C, 10 * 2**20),
         out_shape=(
-            mixed_shape,
+            jax.ShapeDtypeStruct((2, SENT, C), BF16),
             jax.ShapeDtypeStruct((2, BLOCK, C), F32),
             jax.ShapeDtypeStruct((4, 4, 8, C), F32),
         ),
@@ -522,6 +541,12 @@
         spatial_weight,
     )
 
+    onward, part = lax.optimization_barrier((onward, part))
+    near = jnp.where(
+        lax.axis_index("row") == 0, onward[:, (OWN - 1) * W : OWN * W], onward[:, :W]
+    )
+    near = swap_rows(near)
+
     def last_frames(*refs):
         last_frames_kernel(last_col, *refs)
 
@@ -530,10 +555,10 @@
         "upsample_last",
         late_cost,
         out_shape=(jax.ShapeDtypeStruct((2, BLOCK, 2 * C), F32), out_shape),
-        in_specs=[VMEM] * 7,
+        in_specs=[VMEM] * 8,
         out_specs=(VMEM, HBM),
         scratch_shapes=scratch,
-    )(part, onward, mixed, time_weight, time_bias, spatial, spatial_bias)
+    )(part, onward, near, mixed, time_weight, time_bias, spatial, spatial_bias)
 
     def first_frames(*refs):
         first_frames_kernel(last_col, *refs)

time: 34.2 us -> 34 us (level)
  waiting for transfers between devices: 6.16 us -> 4.9 us
  local copies, waits for them, and re-layouts: 1.1 us -> 1.81 us
    ppermute x2, waiting for transfers between devices: 2.55 us -> 0.9 us  [to_later_frames(): lax.ppermute(block, 'tm', [(i, i + 1) for i in range(lax.axis_size('tm')...]
    ppermute x2 -> x3, waiting for transfers between devices: 0.83 us -> 2.06 us  [swap_rows(): return lax.ppermute(block, 'row', [(0, 1), (1, 0)])]
    ppermute x1, waiting for transfers between devices: 2.78 us -> 1.93 us  [across_columns(): return lax.ppermute(block, ('row', 'col'), route)]
    unnamed x20 -> x18, local copies, waits for them, and re-layouts: 1.1 us -> 1.81 us
  transfers between devices with their start and end apart: 5 -> 6, of which waited for: 4 -> 4; matrix products, arithmetic and copies ran while one was open for 0% -> 0% of each run, Pallas kernels for 36% -> 37%
where the time goes in v4:
time: 34 us; the launch traced here: 33.9 us
  Pallas kernels  17.1 us (50%)
  starting transfers between devices  9.65 us (28%)
  waiting for transfers between devices  4.9 us (14%)
  local copies, waits for them, and re-layouts  1.81 us (5%)
  between operations  0.35 us (1%)
    ppermute x2, starting transfers between devices, to_later_frames(): lax.ppermute(block, 'tm', [(i, i + 1) for i in range(lax.axis_size('tm')...  6.82 us
    pallas_call x1, Pallas kernels, on_device(): call(last_frames, 'upsample_last', late_cost, out_shape=(jax.ShapeDtypeSt...  4.11 us
    pallas_call x1, Pallas kernels, on_device(): call(first_frames, 'upsample_first', late_cost, out_shape=out_shape, in_s...  3.4 us
    pallas_call x1, Pallas kernels, on_device(): call(first_part_kernel, 'mixed_first', cost(3 * BLOCK * 9 * C * C, 10 * 2...  2.46 us
    pallas_call x1, Pallas kernels, on_device(): call(activate_kernel, 'activated', cost(4 * MROWS * W * 9 * C * C, 7 * 2...  2.43 us
    ppermute x1, starting transfers between devices, across_columns(): return lax.ppermute(block, ('row', 'col'), route)  2.41 us
    pallas_call x1, Pallas kernels, on_device(): call(own_kernel, 'mixed_last', cost(3 * BLOCK * 9 * C * C, 10 * 2 ** 20),...  2.28 us
    ppermute x3, waiting for transfers between devices, swap_rows(): return lax.ppermute(block, 'row', [(0, 1), (1, 0)])  2.06 us
  transfers between devices with their start and end apart: 6, of which 4 were waited for; matrix products, arithmetic and copies ran while one was open for 0% of the time, Pallas kernels for 37%

profile of v4, /device:TPU:104, one launch (start us, length us, event | category | flops | bytes accessed | tf_op | source)
XLA Modules:
  0.0 33.9 jit_solution(6434037110691101644)
XLA Ops:
  0.0 1.0 %copy-done.1 = bf16[4,4,32,384]{3,2,1,0:T(8,128)(2,1)S(1)} copy-done((bf16[4,4,32,384]{3,2,1,0:T(8,128)(2,1)S(1)}, bf16[4,4,32,384]{3,2,1,0:T(8,128)(2,1)}, u32[]{:S(2)}) %copy-start.1) | copy-done | bytes 393240
  1.0 0.1 own_edge.1.held
  1.1 0.0 copy-start.5
  1.1 0.8 %collective-permute-done.other = bf16[4,4,32,384]{3,2,1,0:T(8,128)(2,1)S(1)} collective-permute-done((bf16[4,4,32,384]{3,2,1,0:T(8,128)(2,1)}, bf16[4,4,32,384]{3,2,1,0:T(8,128)(2,1)S(1)}, u32[]{:S(2)}, u32[]{:S(2)}) %collective-permute-start) | collective-permute-done | bytes 393248 | tf_op jit(solution)/shard_map/ppermute | solution.py:422
  1.9 0.1 edge.1
  2.0 2.4 %collective-permute-start.1 = (bf16[4,2,8,384]{3,2,1,0:T(8,128)(2,1)S(1)}, bf16[4,2,8,384]{3,2,1,0:T(8,128)(2,1)S(1)}, u32[]{:S(2)}, u32[]{:S(2)}) collective-permute-start(bf16[4,2,8,384]{3,2,1,0:T(8,128)(2,1)S(1)} %edge.1), channel_id=1, source_target_pairs={{1,0},{2,1},{3,2},{4,3},{5,4},{6,5},{7,6},{8,9},{9,10},{10,11},{11... | collective-permute-start | bytes 147464 | tf_op jit(solution)/shard_map/ppermute | solution.py:433
  4.5 0.8 %copy-done = bf16[3,3,3,384,384]{4,3,2,1,0:T(8,128)(2,1)S(1)} copy-done((bf16[3,3,3,384,384]{4,3,2,1,0:T(8,128)(2,1)S(1)}, bf16[3,3,3,384,384]{4,3,2,1,0:T(8,128)(2,1)}, u32[]{:S(2)}) %copy-start) | copy-done | bytes 7962648
  5.2 2.4 %activated.1 = (bf16[4,7,32,384]{3,2,1,0:T(8,128)(2,1)S(1)}, f32[4,2,8,384]{3,2,1,0:T(8,128)S(1)}, f32[160,768]{1,0:T(8,128)S(1)}, f32[160,768]{1,0:T(8,128)S(1)}, bf16[160,3456]{1,0:T(8,128)(2,1)S(1)}) custom-call(bf16[4,4,32,384]{3,2,1,0:T(8,128)(2,1)S(1)} %copy-done.2, bf16[4,4,32,384]{3,2,1,0:T(8,128)(2,1)S(1)} %collective-permute-done.other, ...), custom_call_target="tpu_custom_call" | custom-call | flops 1698693120 | bytes 7340032 | tf_op jit(solution)/shard_map/activated/pallas_call | solution.py:464
  7.7 1.9 %collective-permute-done.1.mine = bf16[4,2,8,384]{3,2,1,0:T(8,128)(2,1)S(1)} collective-permute-done((bf16[4,2,8,384]{3,2,1,0:T(8,128)(2,1)S(1)}, bf16[4,2,8,384]{3,2,1,0:T(8,128)(2,1)S(1)}, u32[]{:S(2)}, u32[]{:S(2)}) %collective-permute-start.1) | collective-permute-done | bytes 49184 | tf_op jit(solution)/shard_map/ppermute | solution.py:433
  9.6 0.2 collective-permute-start.2
  9.8 1.1 %inner.1.inner2 = f32[160,768]{1,0:T(8,128)S(1)} custom-call(bf16[160,3456]{1,0:T(8,128)(2,1)S(1)} %get-tuple-element.30.patches, bf16[3,3,3,384,384]{4,3,2,1,0:T(8,128)(2,1)S(1)} %copy-done), custom_call_target="tpu_custom_call" | custom-call | flops 849346560 | bytes 7340032 | tf_op jit(solution)/shard_map/inner/pallas_call | solution.py:481
  10.9 1.2 %partial_for_next.1 = (bf16[2,144,384]{2,1,0:T(8,128)(2,1)S(1)}, f32[2,176,384]{2,1,0:T(8,128)S(1)}, f32[4,4,8,384]{3,2,1,0:T(8,128)S(1)}) custom-call(f32[4,2,8,384]{3,2,1,0:T(8,128)S(1)} %get-tuple-element.27.edges, bf16[4,2,8,384]{3,2,1,0:T(8,128)(2,1)S(1)} %collective-permute-done.1.mine, bf16[4,2,8,384]{3,2,1,0:T(8,128)(2,1)S(1)} %collective-permute-done.2.theirs, ...), custom_call_target="tpu_custom_call" | custom-call | flops 509607936 | bytes 10485760 | tf_op jit(solution)/shard_map/partial_for_next/pallas_call | solution.py:491
  12.1 3.4 %collective-permute-start.4 = (bf16[2,144,384]{2,1,0:T(8,128)(2,1)S(1)}, bf16[2,144,384]{2,1,0:T(8,128)(2,1)S(1)}, u32[]{:S(2)}, u32[]{:S(2)}) collective-permute-start(bf16[2,144,384]{2,1,0:T(8,128)(2,1)S(1)} %get-tuple-element.35), channel_id=1, source_target_pairs={{0,16},{16,32},{32,48},{48,64},{64,80},{80,96},{96,112},{112,128},... | collective-permute-start | bytes 663560 | tf_op jit(solution)/shard_map/ppermute | solution.py:426
  15.6 2.3 %mixed_last.1 = (bf16[2,176,384]{2,1,0:T(8,128)(2,1)S(1)}, bf16[176,3456]{1,0:T(8,128)(2,1)S(1)}) custom-call(bf16[4,7,32,384]{3,2,1,0:T(8,128)(2,1)S(1)} %get-tuple-element.26.activated, f32[4,2,8,384]{3,2,1,0:T(8,128)S(1)} %get-tuple-element.27.edges, f32[4,4,8,384]{3,2,1,0:T(8,128)S(1)} %get-tuple-element.32.outer, ...), custom_call_target="tpu_custom_call" | custom-call | flops 1401421824 | bytes 10485760 | tf_op jit(solution)/shard_map/mixed_last/pallas_call | solution.py:507
  17.8 3.4 %collective-permute-start.3 = (bf16[2,176,384]{2,1,0:T(8,128)(2,1)S(1)}, bf16[2,176,384]{2,1,0:T(8,128)(2,1)S(1)}, u32[]{:S(2)}, u32[]{:S(2)}) collective-permute-start(bf16[2,176,384]{2,1,0:T(8,128)(2,1)S(1)} %get-tuple-element.34.refs_3_), channel_id=1, source_target_pairs={{0,16},{16,32},{32,48},{48,64},{64,80},{80,96},{96,112},{112,128},... | collective-permute-start | bytes 811016 | tf_op jit(solution)/shard_map/ppermute | solution.py:426
  21.3 0.0 copy-start.7
  21.3 0.0 copy-start.8
  21.3 2.5 %mixed_first.1 = (f32[2,176,384]{2,1,0:T(8,128)S(1)}, bf16[4,2,768,256]{3,2,1,0:T(8,128)(2,1)S(1)}) custom-call(bf16[176,3456]{1,0:T(8,128)(2,1)S(1)} %get-tuple-element.36.patches, bf16[4,7,32,384]{3,2,1,0:T(8,128)(2,1)S(1)} %get-tuple-element.26.activated, f32[4,2,8,384]{3,2,1,0:T(8,128)S(1)} %get-tuple-element.27.edges, ...), custom_call_target="tpu_custom_call" | custom-call | flops 1401421824 | bytes 10485760 | tf_op jit(solution)/shard_map/mixed_first/pallas_call | solution.py:528
  23.8 0.0 collective-permute-done.4.refs_1_
  23.8 0.3 collective-permute-start.5
  24.1 1.2 %collective-permute-done.5.refs_2_ = bf16[2,32,384]{2,1,0:T(8,128)(2,1)S(1)} collective-permute-done((bf16[2,32,384]{2,1,0:T(8,128)(2,1)S(1)}, bf16[2,32,384]{2,1,0:T(8,128)(2,1)S(1)}, u32[]{:S(2)}, u32[]{:S(2)}) %collective-permute-start.5) | collective-permute-done | bytes 49184 | tf_op jit(solution)/shard_map/ppermute | solution.py:422
  25.3 4.1 %upsample_last.1 = (f32[2,176,768]{2,1,0:T(8,128)S(1)}, bf16[8,8,64,192]{3,2,1,0:T(8,128)(2,1)}) custom-call(f32[2,176,384]{2,1,0:T(8,128)S(1)} %get-tuple-element.38.refs_0_, bf16[2,144,384]{2,1,0:T(8,128)(2,1)S(1)} %collective-permute-done.4.refs_1_, bf16[2,32,384]{2,1,0:T(8,128)(2,1)S(1)} %collective-permute-done.5.refs_2_, ...), custom_call_target="tpu_custom_call" | custom-call | flops 2233466880 | bytes 6291456 | tf_op jit(solution)/shard_map/upsample_last/pallas_call | solution.py:553
  29.4 0.9 %collective-permute-done.3.refs_0_ = bf16[2,176,384]{2,1,0:T(8,128)(2,1)S(1)} collective-permute-done((bf16[2,176,384]{2,1,0:T(8,128)(2,1)S(1)}, bf16[2,176,384]{2,1,0:T(8,128)(2,1)S(1)}, u32[]{:S(2)}, u32[]{:S(2)}) %collective-permute-start.3) | collective-permute-done | bytes 270368 | tf_op jit(solution)/shard_map/ppermute | solution.py:426
  30.3 3.4 %upsample_first.1 = bf16[8,8,64,192]{3,2,1,0:T(8,128)(2,1)} custom-call(bf16[2,176,384]{2,1,0:T(8,128)(2,1)S(1)} %collective-permute-done.3.refs_0_, f32[2,176,768]{2,1,0:T(8,128)S(1)} %get-tuple-element.41.refs_1_, bf16[3,384,768]{2,1,0:T(8,128)(2,1)S(1)} %copy-done.3, ...), custom_call_target="tpu_custom_call", output_to_operand_aliasing={{}: (5, {})} | custom-call | flops 2233466880 | bytes 6291456 | tf_op jit(solution)/shard_map/upsample_first/pallas_call | solution.py:566
  (16 shorter events, 0.1 us)
Async XLA Ops:
  0.0 1.9 %collective-permute-start = (bf16[4,4,32,384]{3,2,1,0:T(8,128)(2,1)}, bf16[4,4,32,384]{3,2,1,0:T(8,128)(2,1)S(1)}, u32[]{:S(2)}, u32[]{:S(2)}) collective-permute-start(bf16[4,4,32,384]{3,2,1,0:T(8,128)(2,1)} %own.7), channel_id=1, source_target_pairs={{0,8},{8,0},{1,9},{9,1},{2,10},{10,2},{3,11},{11,3},{4,12},{12,4},... | collective-permute-start | bytes 1179656 | tf_op jit(solution)/shard_map/ppermute | solution.py:422
  0.0 1.0 %copy-start.1 = (bf16[4,4,32,384]{3,2,1,0:T(8,128)(2,1)S(1)}, bf16[4,4,32,384]{3,2,1,0:T(8,128)(2,1)}, u32[]{:S(2)}) copy-start(bf16[4,4,32,384]{3,2,1,0:T(8,128)(2,1)} %own.7) | copy-start | bytes 1179652
  1.1 3.4 %copy-start.2 = (bf16[4,4,32,384]{3,2,1,0:T(8,128)(2,1)S(1)}, bf16[4,4,32,384]{3,2,1,0:T(8,128)(2,1)}, u32[]{:S(2)}) copy-start(bf16[4,4,32,384]{3,2,1,0:T(8,128)(2,1)} %own.7) | copy-start | bytes 1179652
  1.1 3.4 %copy-start.5 = (f32[384]{0:T(512)S(1)}, f32[384]{0:T(512)}, u32[]{:S(2)}) copy-start(f32[384]{0:T(512)} %gain.3) | copy-start | bytes 4612
  1.9 3.3 %copy-start = (bf16[3,3,3,384,384]{4,3,2,1,0:T(8,128)(2,1)S(1)}, bf16[3,3,3,384,384]{4,3,2,1,0:T(8,128)(2,1)}, u32[]{:S(2)}) copy-start(bf16[3,3,3,384,384]{4,3,2,1,0:T(8,128)(2,1)} %weight.9) | copy-start | bytes 23887876
  2.0 7.6 %collective-permute-start.1 = (bf16[4,2,8,384]{3,2,1,0:T(8,128)(2,1)S(1)}, bf16[4,2,8,384]{3,2,1,0:T(8,128)(2,1)S(1)}, u32[]{:S(2)}, u32[]{:S(2)}) collective-permute-start(bf16[4,2,8,384]{3,2,1,0:T(8,128)(2,1)S(1)} %edge.1), channel_id=1, source_target_pairs={{1,0},{2,1},{3,2},{4,3},{5,4},{6,5},{7,6},{8,9},{9,10},{10,11},{11... | collective-permute-start | bytes 147464 | tf_op jit(solution)/shard_map/ppermute | solution.py:433
  9.6 1.2 %collective-permute-start.2 = (bf16[4,2,8,384]{3,2,1,0:T(8,128)(2,1)S(1)}, bf16[4,2,8,384]{3,2,1,0:T(8,128)(2,1)S(1)}, u32[]{:S(2)}, u32[]{:S(2)}) collective-permute-start(bf16[4,2,8,384]{3,2,1,0:T(8,128)(2,1)S(1)} %collective-permute-done.1.mine), channel_id=1, source_target_pairs={{0,8},{8,0},{1,9},{9,1},{2,10},{10,2},{3,11},{11,3},{4,12},{12,4},... | collective-permute-start | bytes 147464 | tf_op jit(solution)/shard_map/ppermute | solution.py:422
  10.9 4.7 %copy-start.6 = (f32[384]{0:T(512)S(1)}, f32[384]{0:T(512)}, u32[]{:S(2)}) copy-start(f32[384]{0:T(512)} %bias.3) | copy-start | bytes 4612
  12.1 11.7 %collective-permute-start.4 = (bf16[2,144,384]{2,1,0:T(8,128)(2,1)S(1)}, bf16[2,144,384]{2,1,0:T(8,128)(2,1)S(1)}, u32[]{:S(2)}, u32[]{:S(2)}) collective-permute-start(bf16[2,144,384]{2,1,0:T(8,128)(2,1)S(1)} %get-tuple-element.35), channel_id=1, source_target_pairs={{0,16},{16,32},{32,48},{48,64},{64,80},{80,96},{96,112},{112,128},... | collective-permute-start | bytes 663560 | tf_op jit(solution)/shard_map/ppermute | solution.py:426
  15.5 5.7 %copy-start.4 = (bf16[3,3,384,192]{2,3,1,0:T(8,128)(2,1)S(1)}, bf16[3,3,384,192]{2,3,1,0:T(8,128)(2,1)}, u32[]{:S(2)}) copy-start(bf16[3,3,384,192]{2,3,1,0:T(8,128)(2,1)} %param.14) | copy-start | bytes 3981316
  17.8 12.5 %collective-permute-start.3 = (bf16[2,176,384]{2,1,0:T(8,128)(2,1)S(1)}, bf16[2,176,384]{2,1,0:T(8,128)(2,1)S(1)}, u32[]{:S(2)}, u32[]{:S(2)}) collective-permute-start(bf16[2,176,384]{2,1,0:T(8,128)(2,1)S(1)} %get-tuple-element.34.refs_3_), channel_id=1, source_target_pairs={{0,16},{16,32},{32,48},{48,64},{64,80},{80,96},{96,112},{112,128},... | collective-permute-start | bytes 811016 | tf_op jit(solution)/shard_map/ppermute | solution.py:426
  21.3 4.1 %copy-start.3 = (bf16[3,384,768]{2,1,0:T(8,128)(2,1)S(1)}, bf16[3,384,768]{2,1,0:T(8,128)(2,1)}, u32[]{:S(2)}) copy-start(bf16[3,384,768]{2,1,0:T(8,128)(2,1)} %refs_2_.1) | copy-start | bytes 5308420
  21.3 4.1 %copy-start.7 = (f32[192]{0:T(256)S(1)}, f32[192]{0:T(256)}, u32[]{:S(2)}) copy-start(f32[192]{0:T(256)} %refs_4_.3) | copy-start | bytes 2308
  21.3 4.0 %copy-start.8 = (f32[768]{0:T(1024)S(1)}, f32[768]{0:T(1024)}, u32[]{:S(2)}) copy-start(f32[768]{0:T(1024)} %refs_5_.1) | copy-start | bytes 9220
  23.8 1.5 %collective-permute-start.5 = (bf16[2,32,384]{2,1,0:T(8,128)(2,1)S(1)}, bf16[2,32,384]{2,1,0:T(8,128)(2,1)S(1)}, u32[]{:S(2)}, u32[]{:S(2)}) collective-permute-start(bf16[2,32,384]{2,1,0:T(8,128)(2,1)S(1)} %slice_select_fusion), channel_id=1, source_target_pairs={{0,8},{8,0},{1,9},{9,1},{2,10},{10,2},{3,11},{11,3},{4,12},{12,4},... | collective-permute-start | bytes 147464 | tf_op jit(solution)/shard_map/ppermute | solution.py:422

commit v5 on v4

--- a/solution.py
+++ b/solution.py
@@ -19,6 +19,7 @@
 SIDE = 16
 BLOCK = MROWS * W + SIDE
 SENT = OWN * W + SIDE
+SPLIT = 4 * C
 LIMIT = 24
 
 
@@ -73,7 +74,7 @@
 
 
 def activate_kernel(
-    own, other, gain, weight, activated, edges, third, first, second_patches,
+    own, other, gain, weight, activated, edges, third, first, zero, second_patches, zero_patches,
     third_patches, first_patches,
 ):
     core = lax.axis_index("row")
@@ -103,9 +104,11 @@
     one(1)
     inner_patches(1, activated, first_patches)
     first[...] = dot(first_patches[...], early_weight(weight))
+    one(0)
+    inner_patches(0, activated, zero_patches)
+    zero[...] = dot(zero_patches[:, :SPLIT], step_weight(weight, 0)[:SPLIT])
     one(2)
     inner_patches(2, activated, second_patches)
-    one(0)
 
 
 def inner_kernel(patches, weight, total):
@@ -177,35 +180,34 @@
 
 
 def send_kernel(
-    edges, mine, theirs, gain, weight, inner1, inner2, inner3, onward, crossing, outer, sides, total
+    edges, mine, theirs, gain, weight, inner0, inner1, inner2, inner3, onward, crossing, outer,
+    sides, total,
 ):
     core = lax.axis_index("row")
     scale = gain[...].reshape(1, C)
-    for frame in (1, 2, 3):
+    for frame in range(4):
         columns = outer_columns(frame, mine, theirs, scale, core)
         for index in range(4):
             outer[frame, index] = columns[index]
-        fill_sides((frame - 1) * 32, frame, edges, columns, sides, True)
+        fill_sides(frame * 32, frame, edges, columns, sides, True)
     extra = dot(sides[...], early_weight(weight))
-    columns = outer_columns(0, mine, theirs, scale, core)
-    for index in range(4):
-        outer[0, index] = columns[index]
-    for index, inner in enumerate((inner1, inner2, inner3)):
+    for index, inner in enumerate((inner0, inner1, inner2, inner3)):
         base = index * 32
-        total[index, : MROWS * W] = inner[...]
-        total[index, MROWS * W :] = extra[base : base + SIDE]
+        lanes = slice(0, inner.shape[1])
+        total[index, : MROWS * W, lanes] = inner[...]
+        total[index, MROWS * W :, lanes] = extra[base : base + SIDE, lanes]
         for row in range(MROWS):
             for at, side in ((row * W, 16), (row * W + W - 1, 24)):
                 line = slice(at, at + 1)
                 add = slice(base + side + row, base + side + row + 1)
-                total[index, line] = inner[line] + extra[add]
+                total[index, line, lanes] = inner[line] + extra[add, lanes]
     own = pl.ds(pl.multiple_of(core * W, W), OWN * W)
     outer_rows = slice(MROWS * W, BLOCK)
     for target, source in ((slice(0, OWN * W), own), (slice(OWN * W, SENT), outer_rows)):
-        onward[0, target] = (total[1, source, :C] + total[2, source, C:]).astype(BF16)
-        onward[1, target] = total[2, source, :C].astype(BF16)
-    crossing[0] = total[0, :, C:]
-    crossing[1] = total[0, :, :C] + total[1, :, C:]
+        onward[0, target] = (total[2, source, :C] + total[3, source, C:]).astype(BF16)
+        onward[1, target] = total[3, source, :C].astype(BF16)
+    crossing[0] = total[1, :, C:] + total[0, :, :C]
+    crossing[1] = total[1, :, :C] + total[2, :, C:]
 
 
 def base_rows(frame, own, other, mine, theirs, bias, core):
@@ -225,7 +227,7 @@
 
 
 def own_kernel(
-    activated, edges, outer, weight, crossing, own, other, mine, theirs, bias, mixed, patches,
+    zero_patches, activated, edges, outer, weight, crossing, own, other, mine, theirs, bias, mixed,
     third_patches, fourth_patches,
 ):
     core = lax.axis_index("row")
@@ -236,20 +238,21 @@
     fourth = base_rows(3, own, other, mine, theirs, shift, core)
     mixed[1] = (fourth + late + crossing[1]).astype(BF16)
     late = dot(third_patches[...], step_weight(weight, 2))
-    fill_patches(0, 0, activated, edges, outer, patches)
     third = base_rows(2, own, other, mine, theirs, shift, core)
-    early = dot(patches[...], step_weight(weight, 0))
+    early = dot(zero_patches[:, SPLIT:], step_weight(weight, 0)[SPLIT:])
+    early = jnp.concatenate([early, jnp.zeros((SIDE, C), F32)], axis=0)
     mixed[0] = (third + late + crossing[0] + early).astype(BF16)
 
 
 def first_part_kernel(
-    patches, activated, edges, outer, weight, own, other, mine, theirs, bias, spatial_weight,
+    activated, edges, outer, weight, own, other, mine, theirs, bias, spatial_weight,
     part, spatial,
-    second_patches,
+    patches, second_patches,
 ):
     core = lax.axis_index("row")
     shift = bias[...].reshape(1, C)
     both = jnp.concatenate([step_weight(weight, 1), step_weight(weight, 2)], axis=1)
+    fill_patches(0, 0, activated, edges, outer, patches)
     early = dot(patches[...], both)
     parity_weights(spatial_weight, spatial)
     fill_patches(1, 0, activated, edges, outer, second_patches)
@@ -461,7 +464,7 @@
 
     inner_shape = jax.ShapeDtypeStruct((MROWS * W, 2 * C), F32)
     inner_cost = cost(2 * MROWS * W * 9 * C * C, 7 * 2**20)
-    activated, edges, inner3, inner1, patches2 = call(
+    activated, edges, inner3, inner1, inner0, patches2, patches0 = call(
         activate_kernel,
         "activated",
         cost(4 * MROWS * W * 9 * C * C, 7 * 2**20),
@@ -470,10 +473,12 @@
             jax.ShapeDtypeStruct((4, 2, 8, C), F32),
             inner_shape,
             inner_shape,
+            jax.ShapeDtypeStruct((MROWS * W, C), F32),
+            jax.ShapeDtypeStruct((MROWS * W, 9 * C), BF16),
             jax.ShapeDtypeStruct((MROWS * W, 9 * C), BF16),
         ),
         in_specs=[VMEM] * 4,
-        out_specs=(VMEM,) * 5,
+        out_specs=(VMEM,) * 7,
         scratch_shapes=2 * [pltpu.VMEM((MROWS * W, 9 * C), BF16)],
     )(own, other, norm_gain, conv_weight)
     mine, activated, patches2 = lax.optimization_barrier((mine, activated, patches2))
@@ -497,22 +502,25 @@
             jax.ShapeDtypeStruct((2, BLOCK, C), F32),
             jax.ShapeDtypeStruct((4, 4, 8, C), F32),
         ),
-        in_specs=[VMEM] * 8,
+        in_specs=[VMEM] * 9,
         out_specs=(VMEM,) * 3,
-        scratch_shapes=[pltpu.VMEM((96, 9 * C), BF16), pltpu.VMEM((3, BLOCK, 2 * C), F32)],
-    )(edges, mine, theirs, norm_gain, conv_weight, inner1, inner2, inner3)
+        scratch_shapes=[pltpu.VMEM((128, 9 * C), BF16), pltpu.VMEM((4, BLOCK, 2 * C), F32)],
+    )(edges, mine, theirs, norm_gain, conv_weight, inner0, inner1, inner2, inner3)
     onward = to_later_frames(onward)
 
     frame_patches = pltpu.VMEM((BLOCK, 9 * C), BF16)
-    mixed, patches = call(
+    mixed = call(
         own_kernel,
         "mixed_last",
         cost(3 * BLOCK * 9 * C * C, 10 * 2**20),
-        out_shape=(mixed_shape, jax.ShapeDtypeStruct((BLOCK, 9 * C), BF16)),
-        in_specs=[VMEM] * 10,
-        out_specs=(VMEM,) * 2,
+        out_shape=mixed_shape,
+        in_specs=[VMEM] * 11,
+        out_specs=VMEM,
         scratch_shapes=[frame_patches, frame_patches],
-    )(activated, edges, outer, conv_weight, crossing, own, other, mine, theirs, conv_bias)
+    )(
+        patches0, activated, edges, outer, conv_weight, crossing, own, other, mine, theirs,
+        conv_bias,
+    )
     previous = to_later_frames(mixed)
 
     out_shape = jax.ShapeDtypeStruct((8, 2 * OWN, 2 * W, OUTC), BF16)
@@ -533,11 +541,11 @@
             jax.ShapeDtypeStruct((2, BLOCK, C), F32),
             jax.ShapeDtypeStruct((4, 2, 2 * C, WIDE), BF16),
         ),
-        in_specs=[VMEM] * 11,
+        in_specs=[VMEM] * 10,
         out_specs=(VMEM,) * 2,
-        scratch_shapes=[frame_patches],
+        scratch_shapes=[frame_patches, frame_patches],
     )(
-        patches, activated, edges, outer, conv_weight, own, other, mine, theirs, conv_bias,
+        activated, edges, outer, conv_weight, own, other, mine, theirs, conv_bias,
         spatial_weight,
     )
 

time: 34 us -> 33.5 us (0.985)
  waiting for transfers between devices: 4.9 us -> 4.55 us
    pallas_call x1, Pallas kernels: 2.28 us -> 1.87 us  [on_device(): call(own_kernel, 'mixed_last', cost(3 * BLOCK * 9 * C * C, 10 * 2 ** 20),...]
  transfers between devices with their start and end apart: 6 -> 6, of which waited for: 4 -> 5; matrix products, arithmetic and copies ran while one was open for 0% -> 0% of each run, Pallas kernels for 37% -> 36%
where the time goes in v5:
time: 33.5 us; the launch traced here: 33.3 us
  Pallas kernels  16.8 us (50%)
  starting transfers between devices  9.84 us (29%)
  waiting for transfers between devices  4.55 us (14%)
  local copies, waits for them, and re-layouts  1.81 us (5%)
  between operations  0.35 us (1%)
    ppermute x2, starting transfers between devices, to_later_frames(): lax.ppermute(block, 'tm', [(i, i + 1) for i in range(lax.axis_size('tm')...  6.8 us
    pallas_call x1, Pallas kernels, on_device(): call(last_frames, 'upsample_last', late_cost, out_shape=(jax.ShapeDtypeSt...  4.04 us
    pallas_call x1, Pallas kernels, on_device(): call(first_frames, 'upsample_first', late_cost, out_shape=out_shape, in_s...  3.34 us
    pallas_call x1, Pallas kernels, on_device(): call(activate_kernel, 'activated', cost(4 * MROWS * W * 9 * C * C, 7 * 2...  2.64 us
    pallas_call x1, Pallas kernels, on_device(): call(first_part_kernel, 'mixed_first', cost(3 * BLOCK * 9 * C * C, 10 * 2...  2.47 us
    ppermute x1, starting transfers between devices, across_columns(): return lax.ppermute(block, ('row', 'col'), route)  2.41 us
    ppermute x3, waiting for transfers between devices, swap_rows(): return lax.ppermute(block, 'row', [(0, 1), (1, 0)])  2.06 us
    pallas_call x1, Pallas kernels, on_device(): call(own_kernel, 'mixed_last', cost(3 * BLOCK * 9 * C * C, 10 * 2 ** 20),...  1.87 us
  transfers between devices with their start and end apart: 6, of which 5 were waited for; matrix products, arithmetic and copies ran while one was open for 0% of the time, Pallas kernels for 36%

profile of v5, /device:TPU:104, one launch (start us, length us, event | category | flops | bytes accessed | tf_op | source)
XLA Modules:
  0.0 33.3 jit_solution(14319967619732239274)
XLA Ops:
  0.0 1.0 %copy-done.1 = bf16[4,4,32,384]{3,2,1,0:T(8,128)(2,1)S(1)} copy-done((bf16[4,4,32,384]{3,2,1,0:T(8,128)(2,1)S(1)}, bf16[4,4,32,384]{3,2,1,0:T(8,128)(2,1)}, u32[]{:S(2)}) %copy-start.1) | copy-done | bytes 393240
  1.0 0.1 own_edge.1.held
  1.1 0.0 copy-start.6
  1.1 0.8 %collective-permute-done.other = bf16[4,4,32,384]{3,2,1,0:T(8,128)(2,1)S(1)} collective-permute-done((bf16[4,4,32,384]{3,2,1,0:T(8,128)(2,1)}, bf16[4,4,32,384]{3,2,1,0:T(8,128)(2,1)S(1)}, u32[]{:S(2)}, u32[]{:S(2)}) %collective-permute-start) | collective-permute-done | bytes 393248 | tf_op jit(solution)/shard_map/ppermute | solution.py:425
  1.9 0.1 edge.1
  2.0 2.4 %collective-permute-start.1 = (bf16[4,2,8,384]{3,2,1,0:T(8,128)(2,1)S(1)}, bf16[4,2,8,384]{3,2,1,0:T(8,128)(2,1)S(1)}, u32[]{:S(2)}, u32[]{:S(2)}) collective-permute-start(bf16[4,2,8,384]{3,2,1,0:T(8,128)(2,1)S(1)} %edge.1), channel_id=1, source_target_pairs={{1,0},{2,1},{3,2},{4,3},{5,4},{6,5},{7,6},{8,9},{9,10},{10,11},{11... | collective-permute-start | bytes 147464 | tf_op jit(solution)/shard_map/ppermute | solution.py:436
  4.5 0.8 %copy-done = bf16[3,3,3,384,384]{4,3,2,1,0:T(8,128)(2,1)S(1)} copy-done((bf16[3,3,3,384,384]{4,3,2,1,0:T(8,128)(2,1)S(1)}, bf16[3,3,3,384,384]{4,3,2,1,0:T(8,128)(2,1)}, u32[]{:S(2)}) %copy-start) | copy-done | bytes 7962648
  5.2 2.6 %activated.1 = (bf16[4,7,32,384]{3,2,1,0:T(8,128)(2,1)S(1)}, f32[4,2,8,384]{3,2,1,0:T(8,128)S(1)}, f32[160,768]{1,0:T(8,128)S(1)}, f32[160,768]{1,0:T(8,128)S(1)...) custom-call(bf16[4,4,32,384]{3,2,1,0:T(8,128)(2,1)S(1)} %copy-done.2, ...), custom_call_target="tpu_custom_call" | custom-call | flops 1698693120 | bytes 7340032 | tf_op jit(solution)/shard_map/activated/pallas_call | solution.py:467
  7.9 1.7 %collective-permute-done.1.mine = bf16[4,2,8,384]{3,2,1,0:T(8,128)(2,1)S(1)} collective-permute-done((bf16[4,2,8,384]{3,2,1,0:T(8,128)(2,1)S(1)}, bf16[4,2,8,384]{3,2,1,0:T(8,128)(2,1)S(1)}, u32[]{:S(2)}, u32[]{:S(2)}) %collective-permute-start.1) | collective-permute-done | bytes 49184 | tf_op jit(solution)/shard_map/ppermute | solution.py:436
  9.6 0.4 %collective-permute-start.2 = (bf16[4,2,8,384]{3,2,1,0:T(8,128)(2,1)S(1)}, bf16[4,2,8,384]{3,2,1,0:T(8,128)(2,1)S(1)}, u32[]{:S(2)}, u32[]{:S(2)}) collective-permute-start(bf16[4,2,8,384]{3,2,1,0:T(8,128)(2,1)S(1)} %collective-permute-done.1.mine), channel_id=1, source_target_pairs={{0,8},{8,0},{1,9},{9,1},{2,10},{10,2},{3,11},{11,3},{4,12},{12,4},... | collective-permute-start | bytes 147464 | tf_op jit(solution)/shard_map/ppermute | solution.py:425
  10.0 1.1 %inner.1.inner2 = f32[160,768]{1,0:T(8,128)S(1)} custom-call(bf16[160,3456]{1,0:T(8,128)(2,1)S(1)} %get-tuple-element.32.patches, bf16[3,3,3,384,384]{4,3,2,1,0:T(8,128)(2,1)S(1)} %copy-done), custom_call_target="tpu_custom_call" | custom-call | flops 849346560 | bytes 7340032 | tf_op jit(solution)/shard_map/inner/pallas_call | solution.py:486
  11.0 1.2 %partial_for_next.1 = (bf16[2,144,384]{2,1,0:T(8,128)(2,1)S(1)}, f32[2,176,384]{2,1,0:T(8,128)S(1)}, f32[4,4,8,384]{3,2,1,0:T(8,128)S(1)}) custom-call(f32[4,2,8,384]{3,2,1,0:T(8,128)S(1)} %get-tuple-element.28.edges, bf16[4,2,8,384]{3,2,1,0:T(8,128)(2,1)S(1)} %collective-permute-done.1.mine, bf16[4,2,8,384]{3,2,1,0:T(8,128)(2,1)S(1)} %collective-permute-done.2.theirs, ...), custom_call_target="tpu_custom_call" | custom-call | flops 509607936 | bytes 10485760 | tf_op jit(solution)/shard_map/partial_for_next/pallas_call | solution.py:496
  12.3 3.4 %collective-permute-start.4 = (bf16[2,144,384]{2,1,0:T(8,128)(2,1)S(1)}, bf16[2,144,384]{2,1,0:T(8,128)(2,1)S(1)}, u32[]{:S(2)}, u32[]{:S(2)}) collective-permute-start(bf16[2,144,384]{2,1,0:T(8,128)(2,1)S(1)} %get-tuple-element.36), channel_id=1, source_target_pairs={{0,16},{16,32},{32,48},{48,64},{64,80},{80,96},{96,112},{112,128},... | collective-permute-start | bytes 663560 | tf_op jit(solution)/shard_map/ppermute | solution.py:429
  15.7 0.0 copy-start.4
  15.7 1.9 %mixed_last.1.refs_3_ = bf16[2,176,384]{2,1,0:T(8,128)(2,1)S(1)} custom-call(bf16[160,3456]{1,0:T(8,128)(2,1)S(1)} %get-tuple-element.24.zero_patches, bf16[4,7,32,384]{3,2,1,0:T(8,128)(2,1)S(1)} %get-tuple-element.27.activated, f32[4,2,8,384]{3,2,1,0:T(8,128)S(1)} %get-tuple-element.28.edges, f32[4,4,8,384]{3,2,1,0:T(8,128)S(1)} %get-tuple-element.34.outer, ...), custom_call_target="tpu_custom_call" | custom-call | flops 1401421824 | bytes 10485760 | tf_op jit(solution)/shard_map/mixed_last/pallas_call | solution.py:512
  17.6 3.4 %collective-permute-start.3 = (bf16[2,176,384]{2,1,0:T(8,128)(2,1)S(1)}, bf16[2,176,384]{2,1,0:T(8,128)(2,1)S(1)}, u32[]{:S(2)}, u32[]{:S(2)}) collective-permute-start(bf16[2,176,384]{2,1,0:T(8,128)(2,1)S(1)} %mixed_last.1.refs_3_), channel_id=1, source_target_pairs={{0,16},{16,32},{32,48},{48,64},{64,80},{80,96},{96,112},{112,128},... | collective-permute-start | bytes 811016 | tf_op jit(solution)/shard_map/ppermute | solution.py:429
  21.0 0.0 copy-start.8
  21.0 2.5 %mixed_first.1 = (f32[2,176,384]{2,1,0:T(8,128)S(1)}, bf16[4,2,768,256]{3,2,1,0:T(8,128)(2,1)S(1)}) custom-call(bf16[4,7,32,384]{3,2,1,0:T(8,128)(2,1)S(1)} %get-tuple-element.27.activated, f32[4,2,8,384]{3,2,1,0:T(8,128)S(1)} %get-tuple-element.28.edges, f32[4,4,8,384]{3,2,1,0:T(8,128)S(1)} %get-tuple-element.34.outer, ...), custom_call_target="tpu_custom_call" | custom-call | flops 1401421824 | bytes 10485760 | tf_op jit(solution)/shard_map/mixed_first/pallas_call | solution.py:536
  23.5 0.2 collective-permute-done.4.refs_1_
  23.8 0.3 collective-permute-start.5
  24.0 1.2 %collective-permute-done.5.refs_2_ = bf16[2,32,384]{2,1,0:T(8,128)(2,1)S(1)} collective-permute-done((bf16[2,32,384]{2,1,0:T(8,128)(2,1)S(1)}, bf16[2,32,384]{2,1,0:T(8,128)(2,1)S(1)}, u32[]{:S(2)}, u32[]{:S(2)}) %collective-permute-start.5) | collective-permute-done | bytes 49184 | tf_op jit(solution)/shard_map/ppermute | solution.py:425
  25.3 4.0 %upsample_last.1 = (f32[2,176,768]{2,1,0:T(8,128)S(1)}, bf16[8,8,64,192]{3,2,1,0:T(8,128)(2,1)}) custom-call(f32[2,176,384]{2,1,0:T(8,128)S(1)} %get-tuple-element.38.refs_0_, bf16[2,144,384]{2,1,0:T(8,128)(2,1)S(1)} %collective-permute-done.4.refs_1_, bf16[2,32,384]{2,1,0:T(8,128)(2,1)S(1)} %collective-permute-done.5.refs_2_, ...), custom_call_target="tpu_custom_call" | custom-call | flops 2233466880 | bytes 6291456 | tf_op jit(solution)/shard_map/upsample_last/pallas_call | solution.py:561
  29.3 0.5 %collective-permute-done.3.refs_0_ = bf16[2,176,384]{2,1,0:T(8,128)(2,1)S(1)} collective-permute-done((bf16[2,176,384]{2,1,0:T(8,128)(2,1)S(1)}, bf16[2,176,384]{2,1,0:T(8,128)(2,1)S(1)}, u32[]{:S(2)}, u32[]{:S(2)}) %collective-permute-start.3) | collective-permute-done | bytes 270368 | tf_op jit(solution)/shard_map/ppermute | solution.py:429
  29.8 3.3 %upsample_first.1 = bf16[8,8,64,192]{3,2,1,0:T(8,128)(2,1)} custom-call(bf16[2,176,384]{2,1,0:T(8,128)(2,1)S(1)} %collective-permute-done.3.refs_0_, f32[2,176,768]{2,1,0:T(8,128)S(1)} %get-tuple-element.41.refs_1_, bf16[3,384,768]{2,1,0:T(8,128)(2,1)S(1)} %copy-done.3, ...), custom_call_target="tpu_custom_call", output_to_operand_aliasing={{}: (5, {})} | custom-call | flops 2233466880 | bytes 6291456 | tf_op jit(solution)/shard_map/upsample_first/pallas_call | solution.py:574
  (16 shorter events, 0.1 us)
Async XLA Ops:
  0.0 1.9 %collective-permute-start = (bf16[4,4,32,384]{3,2,1,0:T(8,128)(2,1)}, bf16[4,4,32,384]{3,2,1,0:T(8,128)(2,1)S(1)}, u32[]{:S(2)}, u32[]{:S(2)}) collective-permute-start(bf16[4,4,32,384]{3,2,1,0:T(8,128)(2,1)} %own.7), channel_id=1, source_target_pairs={{0,8},{8,0},{1,9},{9,1},{2,10},{10,2},{3,11},{11,3},{4,12},{12,4},... | collective-permute-start | bytes 1179656 | tf_op jit(solution)/shard_map/ppermute | solution.py:425
  0.0 1.0 %copy-start.1 = (bf16[4,4,32,384]{3,2,1,0:T(8,128)(2,1)S(1)}, bf16[4,4,32,384]{3,2,1,0:T(8,128)(2,1)}, u32[]{:S(2)}) copy-start(bf16[4,4,32,384]{3,2,1,0:T(8,128)(2,1)} %own.7) | copy-start | bytes 1179652
  1.1 3.4 %copy-start.2 = (bf16[4,4,32,384]{3,2,1,0:T(8,128)(2,1)S(1)}, bf16[4,4,32,384]{3,2,1,0:T(8,128)(2,1)}, u32[]{:S(2)}) copy-start(bf16[4,4,32,384]{3,2,1,0:T(8,128)(2,1)} %own.7) | copy-start | bytes 1179652
  1.1 3.4 %copy-start.6 = (f32[384]{0:T(512)S(1)}, f32[384]{0:T(512)}, u32[]{:S(2)}) copy-start(f32[384]{0:T(512)} %gain.3) | copy-start | bytes 4612
  1.9 3.3 %copy-start = (bf16[3,3,3,384,384]{4,3,2,1,0:T(8,128)(2,1)S(1)}, bf16[3,3,3,384,384]{4,3,2,1,0:T(8,128)(2,1)}, u32[]{:S(2)}) copy-start(bf16[3,3,3,384,384]{4,3,2,1,0:T(8,128)(2,1)} %weight.9) | copy-start | bytes 23887876
  2.0 7.6 %collective-permute-start.1 = (bf16[4,2,8,384]{3,2,1,0:T(8,128)(2,1)S(1)}, bf16[4,2,8,384]{3,2,1,0:T(8,128)(2,1)S(1)}, u32[]{:S(2)}, u32[]{:S(2)}) collective-permute-start(bf16[4,2,8,384]{3,2,1,0:T(8,128)(2,1)S(1)} %edge.1), channel_id=1, source_target_pairs={{1,0},{2,1},{3,2},{4,3},{5,4},{6,5},{7,6},{8,9},{9,10},{10,11},{11... | collective-permute-start | bytes 147464 | tf_op jit(solution)/shard_map/ppermute | solution.py:436
  9.6 1.4 %collective-permute-start.2 = (bf16[4,2,8,384]{3,2,1,0:T(8,128)(2,1)S(1)}, bf16[4,2,8,384]{3,2,1,0:T(8,128)(2,1)S(1)}, u32[]{:S(2)}, u32[]{:S(2)}) collective-permute-start(bf16[4,2,8,384]{3,2,1,0:T(8,128)(2,1)S(1)} %collective-permute-done.1.mine), channel_id=1, source_target_pairs={{0,8},{8,0},{1,9},{9,1},{2,10},{10,2},{3,11},{11,3},{4,12},{12,4},... | collective-permute-start | bytes 147464 | tf_op jit(solution)/shard_map/ppermute | solution.py:425
  11.0 4.6 %copy-start.5 = (f32[384]{0:T(512)S(1)}, f32[384]{0:T(512)}, u32[]{:S(2)}) copy-start(f32[384]{0:T(512)} %bias.3) | copy-start | bytes 4612
  12.3 11.5 %collective-permute-start.4 = (bf16[2,144,384]{2,1,0:T(8,128)(2,1)S(1)}, bf16[2,144,384]{2,1,0:T(8,128)(2,1)S(1)}, u32[]{:S(2)}, u32[]{:S(2)}) collective-permute-start(bf16[2,144,384]{2,1,0:T(8,128)(2,1)S(1)} %get-tuple-element.36), channel_id=1, source_target_pairs={{0,16},{16,32},{32,48},{48,64},{64,80},{80,96},{96,112},{112,128},... | collective-permute-start | bytes 663560 | tf_op jit(solution)/shard_map/ppermute | solution.py:429
  15.7 5.3 %copy-start.4 = (bf16[3,3,384,192]{2,3,1,0:T(8,128)(2,1)S(1)}, bf16[3,3,384,192]{2,3,1,0:T(8,128)(2,1)}, u32[]{:S(2)}) copy-start(bf16[3,3,384,192]{2,3,1,0:T(8,128)(2,1)} %param.14) | copy-start | bytes 3981316
  17.6 12.3 %collective-permute-start.3 = (bf16[2,176,384]{2,1,0:T(8,128)(2,1)S(1)}, bf16[2,176,384]{2,1,0:T(8,128)(2,1)S(1)}, u32[]{:S(2)}, u32[]{:S(2)}) collective-permute-start(bf16[2,176,384]{2,1,0:T(8,128)(2,1)S(1)} %mixed_last.1.refs_3_), channel_id=1, source_target_pairs={{0,16},{16,32},{32,48},{48,64},{64,80},{80,96},{96,112},{112,128},... | collective-permute-start | bytes 811016 | tf_op jit(solution)/shard_map/ppermute | solution.py:429
  21.0 4.3 %copy-start.3 = (bf16[3,384,768]{2,1,0:T(8,128)(2,1)S(1)}, bf16[3,384,768]{2,1,0:T(8,128)(2,1)}, u32[]{:S(2)}) copy-start(bf16[3,384,768]{2,1,0:T(8,128)(2,1)} %refs_2_.1) | copy-start | bytes 5308420
  21.0 4.3 %copy-start.7 = (f32[192]{0:T(256)S(1)}, f32[192]{0:T(256)}, u32[]{:S(2)}) copy-start(f32[192]{0:T(256)} %refs_4_.3) | copy-start | bytes 2308
  21.0 4.3 %copy-start.8 = (f32[768]{0:T(1024)S(1)}, f32[768]{0:T(1024)}, u32[]{:S(2)}) copy-start(f32[768]{0:T(1024)} %refs_5_.1) | copy-start | bytes 9220
  23.8 1.5 %collective-permute-start.5 = (bf16[2,32,384]{2,1,0:T(8,128)(2,1)S(1)}, bf16[2,32,384]{2,1,0:T(8,128)(2,1)S(1)}, u32[]{:S(2)}, u32[]{:S(2)}) collective-permute-start(bf16[2,32,384]{2,1,0:T(8,128)(2,1)S(1)} %slice_select_fusion), channel_id=1, source_target_pairs={{0,8},{8,0},{1,9},{9,1},{2,10},{10,2},{3,11},{11,3},{4,12},{12,4},... | collective-permute-start | bytes 147464 | tf_op jit(solution)/shard_map/ppermute | solution.py:425

commit v6 on v5

--- a/solution.py
+++ b/solution.py
@@ -19,7 +19,7 @@
 SIDE = 16
 BLOCK = MROWS * W + SIDE
 SENT = OWN * W + SIDE
-SPLIT = 4 * C
+SPLIT = 6 * C
 LIMIT = 24
 
 

time: 33.5 us -> 33.5 us (level)
  no operation moved by 1% of the time
where the time goes in v6:
time: 33.5 us; the launch traced here: 33.3 us
  Pallas kernels  16.8 us (50%)
  starting transfers between devices  9.97 us (30%)
  waiting for transfers between devices  4.41 us (13%)
  local copies, waits for them, and re-layouts  1.81 us (5%)
  between operations  0.35 us (1%)
    ppermute x2, starting transfers between devices, to_later_frames(): lax.ppermute(block, 'tm', [(i, i + 1) for i in range(lax.axis_size('tm')...  6.8 us
    pallas_call x1, Pallas kernels, on_device(): call(last_frames, 'upsample_last', late_cost, out_shape=(jax.ShapeDtypeSt...  4.04 us
    pallas_call x1, Pallas kernels, on_device(): call(first_frames, 'upsample_first', late_cost, out_shape=out_shape, in_s...  3.34 us
    pallas_call x1, Pallas kernels, on_device(): call(activate_kernel, 'activated', cost(4 * MROWS * W * 9 * C * C, 7 * 2...  2.78 us
    pallas_call x1, Pallas kernels, on_device(): call(first_part_kernel, 'mixed_first', cost(3 * BLOCK * 9 * C * C, 10 * 2...  2.47 us
    ppermute x1, starting transfers between devices, across_columns(): return lax.ppermute(block, ('row', 'col'), route)  2.41 us
    ppermute x3, waiting for transfers between devices, swap_rows(): return lax.ppermute(block, 'row', [(0, 1), (1, 0)])  2.06 us
    unnamed x18, local copies, waits for them, and re-layouts  1.81 us
  transfers between devices with their start and end apart: 6, of which 5 were waited for; matrix products, arithmetic and copies ran while one was open for 0% of the time, Pallas kernels for 36%

profile of v6, /device:TPU:104, one launch (start us, length us, event | category | flops | bytes accessed | tf_op | source)
XLA Modules:
  0.0 33.3 jit_solution(18381747474405530735)
XLA Ops:
  0.0 1.0 %copy-done.1 = bf16[4,4,32,384]{3,2,1,0:T(8,128)(2,1)S(1)} copy-done((bf16[4,4,32,384]{3,2,1,0:T(8,128)(2,1)S(1)}, bf16[4,4,32,384]{3,2,1,0:T(8,128)(2,1)}, u32[]{:S(2)}) %copy-start.1) | copy-done | bytes 393240
  1.0 0.1 own_edge.1.held
  1.1 0.0 copy-start.2
  1.1 0.0 copy-start.6
  1.1 0.8 %collective-permute-done.other = bf16[4,4,32,384]{3,2,1,0:T(8,128)(2,1)S(1)} collective-permute-done((bf16[4,4,32,384]{3,2,1,0:T(8,128)(2,1)}, bf16[4,4,32,384]{3,2,1,0:T(8,128)(2,1)S(1)}, u32[]{:S(2)}, u32[]{:S(2)}) %collective-permute-start) | collective-permute-done | bytes 393248 | tf_op jit(solution)/shard_map/ppermute | solution.py:425
  1.9 0.1 edge.1
  2.0 2.4 %collective-permute-start.1 = (bf16[4,2,8,384]{3,2,1,0:T(8,128)(2,1)S(1)}, bf16[4,2,8,384]{3,2,1,0:T(8,128)(2,1)S(1)}, u32[]{:S(2)}, u32[]{:S(2)}) collective-permute-start(bf16[4,2,8,384]{3,2,1,0:T(8,128)(2,1)S(1)} %edge.1), channel_id=1, source_target_pairs={{1,0},{2,1},{3,2},{4,3},{5,4},{6,5},{7,6},{8,9},{9,10},{10,11},{11... | collective-permute-start | bytes 147464 | tf_op jit(solution)/shard_map/ppermute | solution.py:436
  4.5 0.8 %copy-done = bf16[3,3,3,384,384]{4,3,2,1,0:T(8,128)(2,1)S(1)} copy-done((bf16[3,3,3,384,384]{4,3,2,1,0:T(8,128)(2,1)S(1)}, bf16[3,3,3,384,384]{4,3,2,1,0:T(8,128)(2,1)}, u32[]{:S(2)}) %copy-start) | copy-done | bytes 7962648
  5.2 2.8 %activated.1 = (bf16[4,7,32,384]{3,2,1,0:T(8,128)(2,1)S(1)}, f32[4,2,8,384]{3,2,1,0:T(8,128)S(1)}, f32[160,768]{1,0:T(8,128)S(1)}, f32[160,768]{1,0:T(8,128)S(1)...) custom-call(bf16[4,4,32,384]{3,2,1,0:T(8,128)(2,1)S(1)} %copy-done.2, ...), custom_call_target="tpu_custom_call" | custom-call | flops 1698693120 | bytes 7340032 | tf_op jit(solution)/shard_map/activated/pallas_call | solution.py:467
  8.0 1.6 %collective-permute-done.1.mine = bf16[4,2,8,384]{3,2,1,0:T(8,128)(2,1)S(1)} collective-permute-done((bf16[4,2,8,384]{3,2,1,0:T(8,128)(2,1)S(1)}, bf16[4,2,8,384]{3,2,1,0:T(8,128)(2,1)S(1)}, u32[]{:S(2)}, u32[]{:S(2)}) %collective-permute-start.1) | collective-permute-done | bytes 49184 | tf_op jit(solution)/shard_map/ppermute | solution.py:436
  9.6 0.5 %collective-permute-start.2 = (bf16[4,2,8,384]{3,2,1,0:T(8,128)(2,1)S(1)}, bf16[4,2,8,384]{3,2,1,0:T(8,128)(2,1)S(1)}, u32[]{:S(2)}, u32[]{:S(2)}) collective-permute-start(bf16[4,2,8,384]{3,2,1,0:T(8,128)(2,1)S(1)} %collective-permute-done.1.mine), channel_id=1, source_target_pairs={{0,8},{8,0},{1,9},{9,1},{2,10},{10,2},{3,11},{11,3},{4,12},{12,4},... | collective-permute-start | bytes 147464 | tf_op jit(solution)/shard_map/ppermute | solution.py:425
  10.1 1.1 %inner.1.inner2 = f32[160,768]{1,0:T(8,128)S(1)} custom-call(bf16[160,3456]{1,0:T(8,128)(2,1)S(1)} %get-tuple-element.32.patches, bf16[3,3,3,384,384]{4,3,2,1,0:T(8,128)(2,1)S(1)} %copy-done), custom_call_target="tpu_custom_call" | custom-call | flops 849346560 | bytes 7340032 | tf_op jit(solution)/shard_map/inner/pallas_call | solution.py:486
  11.2 0.0 copy-start.5
  11.2 1.2 %partial_for_next.1 = (bf16[2,144,384]{2,1,0:T(8,128)(2,1)S(1)}, f32[2,176,384]{2,1,0:T(8,128)S(1)}, f32[4,4,8,384]{3,2,1,0:T(8,128)S(1)}) custom-call(f32[4,2,8,384]{3,2,1,0:T(8,128)S(1)} %get-tuple-element.28.edges, bf16[4,2,8,384]{3,2,1,0:T(8,128)(2,1)S(1)} %collective-permute-done.1.mine, bf16[4,2,8,384]{3,2,1,0:T(8,128)(2,1)S(1)} %collective-permute-done.2.theirs, ...), custom_call_target="tpu_custom_call" | custom-call | flops 509607936 | bytes 10485760 | tf_op jit(solution)/shard_map/partial_for_next/pallas_call | solution.py:496
  12.4 3.4 %collective-permute-start.4 = (bf16[2,144,384]{2,1,0:T(8,128)(2,1)S(1)}, bf16[2,144,384]{2,1,0:T(8,128)(2,1)S(1)}, u32[]{:S(2)}, u32[]{:S(2)}) collective-permute-start(bf16[2,144,384]{2,1,0:T(8,128)(2,1)S(1)} %get-tuple-element.36), channel_id=1, source_target_pairs={{0,16},{16,32},{32,48},{48,64},{64,80},{80,96},{96,112},{112,128},... | collective-permute-start | bytes 663560 | tf_op jit(solution)/shard_map/ppermute | solution.py:429
  15.8 1.7 %mixed_last.1.refs_3_ = bf16[2,176,384]{2,1,0:T(8,128)(2,1)S(1)} custom-call(bf16[160,3456]{1,0:T(8,128)(2,1)S(1)} %get-tuple-element.24.zero_patches, bf16[4,7,32,384]{3,2,1,0:T(8,128)(2,1)S(1)} %get-tuple-element.27.activated, f32[4,2,8,384]{3,2,1,0:T(8,128)S(1)} %get-tuple-element.28.edges, f32[4,4,8,384]{3,2,1,0:T(8,128)S(1)} %get-tuple-element.34.outer, ...), custom_call_target="tpu_custom_call" | custom-call | flops 1401421824 | bytes 10485760 | tf_op jit(solution)/shard_map/mixed_last/pallas_call | solution.py:512
  17.6 3.4 %collective-permute-start.3 = (bf16[2,176,384]{2,1,0:T(8,128)(2,1)S(1)}, bf16[2,176,384]{2,1,0:T(8,128)(2,1)S(1)}, u32[]{:S(2)}, u32[]{:S(2)}) collective-permute-start(bf16[2,176,384]{2,1,0:T(8,128)(2,1)S(1)} %mixed_last.1.refs_3_), channel_id=1, source_target_pairs={{0,16},{16,32},{32,48},{48,64},{64,80},{80,96},{96,112},{112,128},... | collective-permute-start | bytes 811016 | tf_op jit(solution)/shard_map/ppermute | solution.py:429
  21.0 2.5 %mixed_first.1 = (f32[2,176,384]{2,1,0:T(8,128)S(1)}, bf16[4,2,768,256]{3,2,1,0:T(8,128)(2,1)S(1)}) custom-call(bf16[4,7,32,384]{3,2,1,0:T(8,128)(2,1)S(1)} %get-tuple-element.27.activated, f32[4,2,8,384]{3,2,1,0:T(8,128)S(1)} %get-tuple-element.28.edges, f32[4,4,8,384]{3,2,1,0:T(8,128)S(1)} %get-tuple-element.34.outer, ...), custom_call_target="tpu_custom_call" | custom-call | flops 1401421824 | bytes 10485760 | tf_op jit(solution)/shard_map/mixed_first/pallas_call | solution.py:536
  23.5 0.4 %collective-permute-done.4.refs_1_ = bf16[2,144,384]{2,1,0:T(8,128)(2,1)S(1)} collective-permute-done((bf16[2,144,384]{2,1,0:T(8,128)(2,1)S(1)}, bf16[2,144,384]{2,1,0:T(8,128)(2,1)S(1)}, u32[]{:S(2)}, u32[]{:S(2)}) %collective-permute-start.4) | collective-permute-done | bytes 221216 | tf_op jit(solution)/shard_map/ppermute | solution.py:429
  23.9 0.3 collective-permute-start.5
  24.2 1.2 %collective-permute-done.5.refs_2_ = bf16[2,32,384]{2,1,0:T(8,128)(2,1)S(1)} collective-permute-done((bf16[2,32,384]{2,1,0:T(8,128)(2,1)S(1)}, bf16[2,32,384]{2,1,0:T(8,128)(2,1)S(1)}, u32[]{:S(2)}, u32[]{:S(2)}) %collective-permute-start.5) | collective-permute-done | bytes 49184 | tf_op jit(solution)/shard_map/ppermute | solution.py:425
  25.4 4.0 %upsample_last.1 = (f32[2,176,768]{2,1,0:T(8,128)S(1)}, bf16[8,8,64,192]{3,2,1,0:T(8,128)(2,1)}) custom-call(f32[2,176,384]{2,1,0:T(8,128)S(1)} %get-tuple-element.38.refs_0_, bf16[2,144,384]{2,1,0:T(8,128)(2,1)S(1)} %collective-permute-done.4.refs_1_, bf16[2,32,384]{2,1,0:T(8,128)(2,1)S(1)} %collective-permute-done.5.refs_2_, ...), custom_call_target="tpu_custom_call" | custom-call | flops 2233466880 | bytes 6291456 | tf_op jit(solution)/shard_map/upsample_last/pallas_call | solution.py:561
  29.4 0.4 %collective-permute-done.3.refs_0_ = bf16[2,176,384]{2,1,0:T(8,128)(2,1)S(1)} collective-permute-done((bf16[2,176,384]{2,1,0:T(8,128)(2,1)S(1)}, bf16[2,176,384]{2,1,0:T(8,128)(2,1)S(1)}, u32[]{:S(2)}, u32[]{:S(2)}) %collective-permute-start.3) | collective-permute-done | bytes 270368 | tf_op jit(solution)/shard_map/ppermute | solution.py:429
  29.8 3.3 %upsample_first.1 = bf16[8,8,64,192]{3,2,1,0:T(8,128)(2,1)} custom-call(bf16[2,176,384]{2,1,0:T(8,128)(2,1)S(1)} %collective-permute-done.3.refs_0_, f32[2,176,768]{2,1,0:T(8,128)S(1)} %get-tuple-element.41.refs_1_, bf16[3,384,768]{2,1,0:T(8,128)(2,1)S(1)} %copy-done.3, ...), custom_call_target="tpu_custom_call", output_to_operand_aliasing={{}: (5, {})} | custom-call | flops 2233466880 | bytes 6291456 | tf_op jit(solution)/shard_map/upsample_first/pallas_call | solution.py:574
  (16 shorter events, 0.1 us)
Async XLA Ops:
  0.0 1.9 %collective-permute-start = (bf16[4,4,32,384]{3,2,1,0:T(8,128)(2,1)}, bf16[4,4,32,384]{3,2,1,0:T(8,128)(2,1)S(1)}, u32[]{:S(2)}, u32[]{:S(2)}) collective-permute-start(bf16[4,4,32,384]{3,2,1,0:T(8,128)(2,1)} %own.7), channel_id=1, source_target_pairs={{0,8},{8,0},{1,9},{9,1},{2,10},{10,2},{3,11},{11,3},{4,12},{12,4},... | collective-permute-start | bytes 1179656 | tf_op jit(solution)/shard_map/ppermute | solution.py:425
  0.0 1.0 %copy-start.1 = (bf16[4,4,32,384]{3,2,1,0:T(8,128)(2,1)S(1)}, bf16[4,4,32,384]{3,2,1,0:T(8,128)(2,1)}, u32[]{:S(2)}) copy-start(bf16[4,4,32,384]{3,2,1,0:T(8,128)(2,1)} %own.7) | copy-start | bytes 1179652
  1.1 3.4 %copy-start.2 = (bf16[4,4,32,384]{3,2,1,0:T(8,128)(2,1)S(1)}, bf16[4,4,32,384]{3,2,1,0:T(8,128)(2,1)}, u32[]{:S(2)}) copy-start(bf16[4,4,32,384]{3,2,1,0:T(8,128)(2,1)} %own.7) | copy-start | bytes 1179652
  1.1 3.4 %copy-start.6 = (f32[384]{0:T(512)S(1)}, f32[384]{0:T(512)}, u32[]{:S(2)}) copy-start(f32[384]{0:T(512)} %gain.3) | copy-start | bytes 4612
  1.9 3.3 %copy-start = (bf16[3,3,3,384,384]{4,3,2,1,0:T(8,128)(2,1)S(1)}, bf16[3,3,3,384,384]{4,3,2,1,0:T(8,128)(2,1)}, u32[]{:S(2)}) copy-start(bf16[3,3,3,384,384]{4,3,2,1,0:T(8,128)(2,1)} %weight.9) | copy-start | bytes 23887876
  2.0 7.6 %collective-permute-start.1 = (bf16[4,2,8,384]{3,2,1,0:T(8,128)(2,1)S(1)}, bf16[4,2,8,384]{3,2,1,0:T(8,128)(2,1)S(1)}, u32[]{:S(2)}, u32[]{:S(2)}) collective-permute-start(bf16[4,2,8,384]{3,2,1,0:T(8,128)(2,1)S(1)} %edge.1), channel_id=1, source_target_pairs={{1,0},{2,1},{3,2},{4,3},{5,4},{6,5},{7,6},{8,9},{9,10},{10,11},{11... | collective-permute-start | bytes 147464 | tf_op jit(solution)/shard_map/ppermute | solution.py:436
  9.6 1.6 %collective-permute-start.2 = (bf16[4,2,8,384]{3,2,1,0:T(8,128)(2,1)S(1)}, bf16[4,2,8,384]{3,2,1,0:T(8,128)(2,1)S(1)}, u32[]{:S(2)}, u32[]{:S(2)}) collective-permute-start(bf16[4,2,8,384]{3,2,1,0:T(8,128)(2,1)S(1)} %collective-permute-done.1.mine), channel_id=1, source_target_pairs={{0,8},{8,0},{1,9},{9,1},{2,10},{10,2},{3,11},{11,3},{4,12},{12,4},... | collective-permute-start | bytes 147464 | tf_op jit(solution)/shard_map/ppermute | solution.py:425
  11.2 4.6 %copy-start.5 = (f32[384]{0:T(512)S(1)}, f32[384]{0:T(512)}, u32[]{:S(2)}) copy-start(f32[384]{0:T(512)} %bias.3) | copy-start | bytes 4612
  12.4 11.5 %collective-permute-start.4 = (bf16[2,144,384]{2,1,0:T(8,128)(2,1)S(1)}, bf16[2,144,384]{2,1,0:T(8,128)(2,1)S(1)}, u32[]{:S(2)}, u32[]{:S(2)}) collective-permute-start(bf16[2,144,384]{2,1,0:T(8,128)(2,1)S(1)} %get-tuple-element.36), channel_id=1, source_target_pairs={{0,16},{16,32},{32,48},{48,64},{64,80},{80,96},{96,112},{112,128},... | collective-permute-start | bytes 663560 | tf_op jit(solution)/shard_map/ppermute | solution.py:429
  15.8 5.2 %copy-start.4 = (bf16[3,3,384,192]{2,3,1,0:T(8,128)(2,1)S(1)}, bf16[3,3,384,192]{2,3,1,0:T(8,128)(2,1)}, u32[]{:S(2)}) copy-start(bf16[3,3,384,192]{2,3,1,0:T(8,128)(2,1)} %param.14) | copy-start | bytes 3981316
  17.6 12.3 %collective-permute-start.3 = (bf16[2,176,384]{2,1,0:T(8,128)(2,1)S(1)}, bf16[2,176,384]{2,1,0:T(8,128)(2,1)S(1)}, u32[]{:S(2)}, u32[]{:S(2)}) collective-permute-start(bf16[2,176,384]{2,1,0:T(8,128)(2,1)S(1)} %mixed_last.1.refs_3_), channel_id=1, source_target_pairs={{0,16},{16,32},{32,48},{48,64},{64,80},{80,96},{96,112},{112,128},... | collective-permute-start | bytes 811016 | tf_op jit(solution)/shard_map/ppermute | solution.py:429
  21.0 4.4 %copy-start.3 = (bf16[3,384,768]{2,1,0:T(8,128)(2,1)S(1)}, bf16[3,384,768]{2,1,0:T(8,128)(2,1)}, u32[]{:S(2)}) copy-start(bf16[3,384,768]{2,1,0:T(8,128)(2,1)} %refs_2_.1) | copy-start | bytes 5308420
  21.0 4.4 %copy-start.7 = (f32[192]{0:T(256)S(1)}, f32[192]{0:T(256)}, u32[]{:S(2)}) copy-start(f32[192]{0:T(256)} %refs_4_.3) | copy-start | bytes 2308
  21.0 4.4 %copy-start.8 = (f32[768]{0:T(1024)S(1)}, f32[768]{0:T(1024)}, u32[]{:S(2)}) copy-start(f32[768]{0:T(1024)} %refs_5_.1) | copy-start | bytes 9220
  23.9 1.5 %collective-permute-start.5 = (bf16[2,32,384]{2,1,0:T(8,128)(2,1)S(1)}, bf16[2,32,384]{2,1,0:T(8,128)(2,1)S(1)}, u32[]{:S(2)}, u32[]{:S(2)}) collective-permute-start(bf16[2,32,384]{2,1,0:T(8,128)(2,1)S(1)} %slice_select_fusion), channel_id=1, source_target_pairs={{0,8},{8,0},{1,9},{9,1},{2,10},{10,2},{3,11},{11,3},{4,12},{12,4},... | collective-permute-start | bytes 147464 | tf_op jit(solution)/shard_map/ppermute | solution.py:425

commit v7 on v5

--- a/solution.py
+++ b/solution.py
@@ -232,6 +232,7 @@
 ):
     core = lax.axis_index("row")
     shift = bias[...].reshape(1, C)
+    early = dot(zero_patches[:, SPLIT:], step_weight(weight, 0)[SPLIT:])
     fill_patches(3, 0, activated, edges, outer, fourth_patches)
     late = dot(fourth_patches[...], step_weight(weight, 2))
     fill_patches(2, 0, activated, edges, outer, third_patches)
@@ -239,7 +240,6 @@
     mixed[1] = (fourth + late + crossing[1]).astype(BF16)
     late = dot(third_patches[...], step_weight(weight, 2))
     third = base_rows(2, own, other, mine, theirs, shift, core)
-    early = dot(zero_patches[:, SPLIT:], step_weight(weight, 0)[SPLIT:])
     early = jnp.concatenate([early, jnp.zeros((SIDE, C), F32)], axis=0)
     mixed[0] = (third + late + crossing[0] + early).astype(BF16)
 

time: 33.5 us -> 33.5 us (level)
  no operation moved by 1% of the time
where the time goes in v7:
time: 33.5 us; the launch traced here: 33.3 us
  Pallas kernels  16.8 us (50%)
  starting transfers between devices  9.84 us (29%)
  waiting for transfers between devices  4.55 us (14%)
  local copies, waits for them, and re-layouts  1.81 us (5%)
  between operations  0.35 us (1%)
    ppermute x2, starting transfers between devices, to_later_frames(): lax.ppermute(block, 'tm', [(i, i + 1) for i in range(lax.axis_size('tm')...  6.79 us
    pallas_call x1, Pallas kernels, on_device(): call(last_frames, 'upsample_last', late_cost, out_shape=(jax.ShapeDtypeSt...  4.04 us
    pallas_call x1, Pallas kernels, on_device(): call(first_frames, 'upsample_first', late_cost, out_shape=out_shape, in_s...  3.34 us
    pallas_call x1, Pallas kernels, on_device(): call(activate_kernel, 'activated', cost(4 * MROWS * W * 9 * C * C, 7 * 2...  2.64 us
    pallas_call x1, Pallas kernels, on_device(): call(first_part_kernel, 'mixed_first', cost(3 * BLOCK * 9 * C * C, 10 * 2...  2.47 us
    ppermute x1, starting transfers between devices, across_columns(): return lax.ppermute(block, ('row', 'col'), route)  2.41 us
    ppermute x3, waiting for transfers between devices, swap_rows(): return lax.ppermute(block, 'row', [(0, 1), (1, 0)])  2.06 us
    pallas_call x1, Pallas kernels, on_device(): call(own_kernel, 'mixed_last', cost(3 * BLOCK * 9 * C * C, 10 * 2 ** 20),...  1.89 us
  transfers between devices with their start and end apart: 6, of which 5 were waited for; matrix products, arithmetic and copies ran while one was open for 0% of the time, Pallas kernels for 36%

profile of v7, /device:TPU:104, one launch (start us, length us, event | category | flops | bytes accessed | tf_op | source)
XLA Modules:
  0.0 33.3 jit_solution(1579965559080385119)
XLA Ops:
  0.0 1.0 %copy-done.1 = bf16[4,4,32,384]{3,2,1,0:T(8,128)(2,1)S(1)} copy-done((bf16[4,4,32,384]{3,2,1,0:T(8,128)(2,1)S(1)}, bf16[4,4,32,384]{3,2,1,0:T(8,128)(2,1)}, u32[]{:S(2)}) %copy-start.1) | copy-done | bytes 393240
  1.0 0.1 own_edge.1.held
  1.1 0.0 copy-start.6
  1.1 0.8 %collective-permute-done.other = bf16[4,4,32,384]{3,2,1,0:T(8,128)(2,1)S(1)} collective-permute-done((bf16[4,4,32,384]{3,2,1,0:T(8,128)(2,1)}, bf16[4,4,32,384]{3,2,1,0:T(8,128)(2,1)S(1)}, u32[]{:S(2)}, u32[]{:S(2)}) %collective-permute-start) | collective-permute-done | bytes 393248 | tf_op jit(solution)/shard_map/ppermute | solution.py:425
  1.9 0.1 edge.1
  2.0 2.4 %collective-permute-start.1 = (bf16[4,2,8,384]{3,2,1,0:T(8,128)(2,1)S(1)}, bf16[4,2,8,384]{3,2,1,0:T(8,128)(2,1)S(1)}, u32[]{:S(2)}, u32[]{:S(2)}) collective-permute-start(bf16[4,2,8,384]{3,2,1,0:T(8,128)(2,1)S(1)} %edge.1), channel_id=1, source_target_pairs={{1,0},{2,1},{3,2},{4,3},{5,4},{6,5},{7,6},{8,9},{9,10},{10,11},{11... | collective-permute-start | bytes 147464 | tf_op jit(solution)/shard_map/ppermute | solution.py:436
  4.5 0.8 %copy-done = bf16[3,3,3,384,384]{4,3,2,1,0:T(8,128)(2,1)S(1)} copy-done((bf16[3,3,3,384,384]{4,3,2,1,0:T(8,128)(2,1)S(1)}, bf16[3,3,3,384,384]{4,3,2,1,0:T(8,128)(2,1)}, u32[]{:S(2)}) %copy-start) | copy-done | bytes 7962648
  5.2 2.6 %activated.1 = (bf16[4,7,32,384]{3,2,1,0:T(8,128)(2,1)S(1)}, f32[4,2,8,384]{3,2,1,0:T(8,128)S(1)}, f32[160,768]{1,0:T(8,128)S(1)}, f32[160,768]{1,0:T(8,128)S(1)...) custom-call(bf16[4,4,32,384]{3,2,1,0:T(8,128)(2,1)S(1)} %copy-done.2, ...), custom_call_target="tpu_custom_call" | custom-call | flops 1698693120 | bytes 7340032 | tf_op jit(solution)/shard_map/activated/pallas_call | solution.py:467
  7.9 1.7 %collective-permute-done.1.mine = bf16[4,2,8,384]{3,2,1,0:T(8,128)(2,1)S(1)} collective-permute-done((bf16[4,2,8,384]{3,2,1,0:T(8,128)(2,1)S(1)}, bf16[4,2,8,384]{3,2,1,0:T(8,128)(2,1)S(1)}, u32[]{:S(2)}, u32[]{:S(2)}) %collective-permute-start.1) | collective-permute-done | bytes 49184 | tf_op jit(solution)/shard_map/ppermute | solution.py:436
  9.6 0.4 %collective-permute-start.2 = (bf16[4,2,8,384]{3,2,1,0:T(8,128)(2,1)S(1)}, bf16[4,2,8,384]{3,2,1,0:T(8,128)(2,1)S(1)}, u32[]{:S(2)}, u32[]{:S(2)}) collective-permute-start(bf16[4,2,8,384]{3,2,1,0:T(8,128)(2,1)S(1)} %collective-permute-done.1.mine), channel_id=1, source_target_pairs={{0,8},{8,0},{1,9},{9,1},{2,10},{10,2},{3,11},{11,3},{4,12},{12,4},... | collective-permute-start | bytes 147464 | tf_op jit(solution)/shard_map/ppermute | solution.py:425
  10.0 1.1 %inner.1.inner2 = f32[160,768]{1,0:T(8,128)S(1)} custom-call(bf16[160,3456]{1,0:T(8,128)(2,1)S(1)} %get-tuple-element.32.patches, bf16[3,3,3,384,384]{4,3,2,1,0:T(8,128)(2,1)S(1)} %copy-done), custom_call_target="tpu_custom_call" | custom-call | flops 849346560 | bytes 7340032 | tf_op jit(solution)/shard_map/inner/pallas_call | solution.py:486
  11.0 1.2 %partial_for_next.1 = (bf16[2,144,384]{2,1,0:T(8,128)(2,1)S(1)}, f32[2,176,384]{2,1,0:T(8,128)S(1)}, f32[4,4,8,384]{3,2,1,0:T(8,128)S(1)}) custom-call(f32[4,2,8,384]{3,2,1,0:T(8,128)S(1)} %get-tuple-element.28.edges, bf16[4,2,8,384]{3,2,1,0:T(8,128)(2,1)S(1)} %collective-permute-done.1.mine, bf16[4,2,8,384]{3,2,1,0:T(8,128)(2,1)S(1)} %collective-permute-done.2.theirs, ...), custom_call_target="tpu_custom_call" | custom-call | flops 509607936 | bytes 10485760 | tf_op jit(solution)/shard_map/partial_for_next/pallas_call | solution.py:496
  12.3 3.4 %collective-permute-start.4 = (bf16[2,144,384]{2,1,0:T(8,128)(2,1)S(1)}, bf16[2,144,384]{2,1,0:T(8,128)(2,1)S(1)}, u32[]{:S(2)}, u32[]{:S(2)}) collective-permute-start(bf16[2,144,384]{2,1,0:T(8,128)(2,1)S(1)} %get-tuple-element.36), channel_id=1, source_target_pairs={{0,16},{16,32},{32,48},{48,64},{64,80},{80,96},{96,112},{112,128},... | collective-permute-start | bytes 663560 | tf_op jit(solution)/shard_map/ppermute | solution.py:429
  15.7 0.0 copy-start.4
  15.7 1.9 %mixed_last.1.refs_3_ = bf16[2,176,384]{2,1,0:T(8,128)(2,1)S(1)} custom-call(bf16[160,3456]{1,0:T(8,128)(2,1)S(1)} %get-tuple-element.24.zero_patches, bf16[4,7,32,384]{3,2,1,0:T(8,128)(2,1)S(1)} %get-tuple-element.27.activated, f32[4,2,8,384]{3,2,1,0:T(8,128)S(1)} %get-tuple-element.28.edges, f32[4,4,8,384]{3,2,1,0:T(8,128)S(1)} %get-tuple-element.34.outer, ...), custom_call_target="tpu_custom_call" | custom-call | flops 1401421824 | bytes 10485760 | tf_op jit(solution)/shard_map/mixed_last/pallas_call | solution.py:512
  17.6 3.4 %collective-permute-start.3 = (bf16[2,176,384]{2,1,0:T(8,128)(2,1)S(1)}, bf16[2,176,384]{2,1,0:T(8,128)(2,1)S(1)}, u32[]{:S(2)}, u32[]{:S(2)}) collective-permute-start(bf16[2,176,384]{2,1,0:T(8,128)(2,1)S(1)} %mixed_last.1.refs_3_), channel_id=1, source_target_pairs={{0,16},{16,32},{32,48},{48,64},{64,80},{80,96},{96,112},{112,128},... | collective-permute-start | bytes 811016 | tf_op jit(solution)/shard_map/ppermute | solution.py:429
  21.0 0.0 copy-start.3
  21.0 2.5 %mixed_first.1 = (f32[2,176,384]{2,1,0:T(8,128)S(1)}, bf16[4,2,768,256]{3,2,1,0:T(8,128)(2,1)S(1)}) custom-call(bf16[4,7,32,384]{3,2,1,0:T(8,128)(2,1)S(1)} %get-tuple-element.27.activated, f32[4,2,8,384]{3,2,1,0:T(8,128)S(1)} %get-tuple-element.28.edges, f32[4,4,8,384]{3,2,1,0:T(8,128)S(1)} %get-tuple-element.34.outer, ...), custom_call_target="tpu_custom_call" | custom-call | flops 1401421824 | bytes 10485760 | tf_op jit(solution)/shard_map/mixed_first/pallas_call | solution.py:536
  23.5 0.2 collective-permute-done.4.refs_1_
  23.8 0.3 collective-permute-start.5
  24.0 1.2 %collective-permute-done.5.refs_2_ = bf16[2,32,384]{2,1,0:T(8,128)(2,1)S(1)} collective-permute-done((bf16[2,32,384]{2,1,0:T(8,128)(2,1)S(1)}, bf16[2,32,384]{2,1,0:T(8,128)(2,1)S(1)}, u32[]{:S(2)}, u32[]{:S(2)}) %collective-permute-start.5) | collective-permute-done | bytes 49184 | tf_op jit(solution)/shard_map/ppermute | solution.py:425
  25.3 4.0 %upsample_last.1 = (f32[2,176,768]{2,1,0:T(8,128)S(1)}, bf16[8,8,64,192]{3,2,1,0:T(8,128)(2,1)}) custom-call(f32[2,176,384]{2,1,0:T(8,128)S(1)} %get-tuple-element.38.refs_0_, bf16[2,144,384]{2,1,0:T(8,128)(2,1)S(1)} %collective-permute-done.4.refs_1_, bf16[2,32,384]{2,1,0:T(8,128)(2,1)S(1)} %collective-permute-done.5.refs_2_, ...), custom_call_target="tpu_custom_call" | custom-call | flops 2233466880 | bytes 6291456 | tf_op jit(solution)/shard_map/upsample_last/pallas_call | solution.py:561
  29.3 0.5 %collective-permute-done.3.refs_0_ = bf16[2,176,384]{2,1,0:T(8,128)(2,1)S(1)} collective-permute-done((bf16[2,176,384]{2,1,0:T(8,128)(2,1)S(1)}, bf16[2,176,384]{2,1,0:T(8,128)(2,1)S(1)}, u32[]{:S(2)}, u32[]{:S(2)}) %collective-permute-start.3) | collective-permute-done | bytes 270368 | tf_op jit(solution)/shard_map/ppermute | solution.py:429
  29.8 3.3 %upsample_first.1 = bf16[8,8,64,192]{3,2,1,0:T(8,128)(2,1)} custom-call(bf16[2,176,384]{2,1,0:T(8,128)(2,1)S(1)} %collective-permute-done.3.refs_0_, f32[2,176,768]{2,1,0:T(8,128)S(1)} %get-tuple-element.41.refs_1_, bf16[3,384,768]{2,1,0:T(8,128)(2,1)S(1)} %copy-done.3, ...), custom_call_target="tpu_custom_call", output_to_operand_aliasing={{}: (5, {})} | custom-call | flops 2233466880 | bytes 6291456 | tf_op jit(solution)/shard_map/upsample_first/pallas_call | solution.py:574
  (16 shorter events, 0.1 us)
Async XLA Ops:
  0.0 1.9 %collective-permute-start = (bf16[4,4,32,384]{3,2,1,0:T(8,128)(2,1)}, bf16[4,4,32,384]{3,2,1,0:T(8,128)(2,1)S(1)}, u32[]{:S(2)}, u32[]{:S(2)}) collective-permute-start(bf16[4,4,32,384]{3,2,1,0:T(8,128)(2,1)} %own.7), channel_id=1, source_target_pairs={{0,8},{8,0},{1,9},{9,1},{2,10},{10,2},{3,11},{11,3},{4,12},{12,4},... | collective-permute-start | bytes 1179656 | tf_op jit(solution)/shard_map/ppermute | solution.py:425
  0.0 1.0 %copy-start.1 = (bf16[4,4,32,384]{3,2,1,0:T(8,128)(2,1)S(1)}, bf16[4,4,32,384]{3,2,1,0:T(8,128)(2,1)}, u32[]{:S(2)}) copy-start(bf16[4,4,32,384]{3,2,1,0:T(8,128)(2,1)} %own.7) | copy-start | bytes 1179652
  1.1 3.4 %copy-start.2 = (bf16[4,4,32,384]{3,2,1,0:T(8,128)(2,1)S(1)}, bf16[4,4,32,384]{3,2,1,0:T(8,128)(2,1)}, u32[]{:S(2)}) copy-start(bf16[4,4,32,384]{3,2,1,0:T(8,128)(2,1)} %own.7) | copy-start | bytes 1179652
  1.1 3.4 %copy-start.6 = (f32[384]{0:T(512)S(1)}, f32[384]{0:T(512)}, u32[]{:S(2)}) copy-start(f32[384]{0:T(512)} %gain.3) | copy-start | bytes 4612
  1.9 3.3 %copy-start = (bf16[3,3,3,384,384]{4,3,2,1,0:T(8,128)(2,1)S(1)}, bf16[3,3,3,384,384]{4,3,2,1,0:T(8,128)(2,1)}, u32[]{:S(2)}) copy-start(bf16[3,3,3,384,384]{4,3,2,1,0:T(8,128)(2,1)} %weight.9) | copy-start | bytes 23887876
  2.0 7.6 %collective-permute-start.1 = (bf16[4,2,8,384]{3,2,1,0:T(8,128)(2,1)S(1)}, bf16[4,2,8,384]{3,2,1,0:T(8,128)(2,1)S(1)}, u32[]{:S(2)}, u32[]{:S(2)}) collective-permute-start(bf16[4,2,8,384]{3,2,1,0:T(8,128)(2,1)S(1)} %edge.1), channel_id=1, source_target_pairs={{1,0},{2,1},{3,2},{4,3},{5,4},{6,5},{7,6},{8,9},{9,10},{10,11},{11... | collective-permute-start | bytes 147464 | tf_op jit(solution)/shard_map/ppermute | solution.py:436
  9.6 1.4 %collective-permute-start.2 = (bf16[4,2,8,384]{3,2,1,0:T(8,128)(2,1)S(1)}, bf16[4,2,8,384]{3,2,1,0:T(8,128)(2,1)S(1)}, u32[]{:S(2)}, u32[]{:S(2)}) collective-permute-start(bf16[4,2,8,384]{3,2,1,0:T(8,128)(2,1)S(1)} %collective-permute-done.1.mine), channel_id=1, source_target_pairs={{0,8},{8,0},{1,9},{9,1},{2,10},{10,2},{3,11},{11,3},{4,12},{12,4},... | collective-permute-start | bytes 147464 | tf_op jit(solution)/shard_map/ppermute | solution.py:425
  11.0 4.6 %copy-start.5 = (f32[384]{0:T(512)S(1)}, f32[384]{0:T(512)}, u32[]{:S(2)}) copy-start(f32[384]{0:T(512)} %bias.3) | copy-start | bytes 4612
  12.3 11.5 %collective-permute-start.4 = (bf16[2,144,384]{2,1,0:T(8,128)(2,1)S(1)}, bf16[2,144,384]{2,1,0:T(8,128)(2,1)S(1)}, u32[]{:S(2)}, u32[]{:S(2)}) collective-permute-start(bf16[2,144,384]{2,1,0:T(8,128)(2,1)S(1)} %get-tuple-element.36), channel_id=1, source_target_pairs={{0,16},{16,32},{32,48},{48,64},{64,80},{80,96},{96,112},{112,128},... | collective-permute-start | bytes 663560 | tf_op jit(solution)/shard_map/ppermute | solution.py:429
  15.7 5.3 %copy-start.4 = (bf16[3,3,384,192]{2,3,1,0:T(8,128)(2,1)S(1)}, bf16[3,3,384,192]{2,3,1,0:T(8,128)(2,1)}, u32[]{:S(2)}) copy-start(bf16[3,3,384,192]{2,3,1,0:T(8,128)(2,1)} %param.14) | copy-start | bytes 3981316
  17.6 12.3 %collective-permute-start.3 = (bf16[2,176,384]{2,1,0:T(8,128)(2,1)S(1)}, bf16[2,176,384]{2,1,0:T(8,128)(2,1)S(1)}, u32[]{:S(2)}, u32[]{:S(2)}) collective-permute-start(bf16[2,176,384]{2,1,0:T(8,128)(2,1)S(1)} %mixed_last.1.refs_3_), channel_id=1, source_target_pairs={{0,16},{16,32},{32,48},{48,64},{64,80},{80,96},{96,112},{112,128},... | collective-permute-start | bytes 811016 | tf_op jit(solution)/shard_map/ppermute | solution.py:429
  21.0 4.3 %copy-start.3 = (bf16[3,384,768]{2,1,0:T(8,128)(2,1)S(1)}, bf16[3,384,768]{2,1,0:T(8,128)(2,1)}, u32[]{:S(2)}) copy-start(bf16[3,384,768]{2,1,0:T(8,128)(2,1)} %refs_2_.1) | copy-start | bytes 5308420
  21.0 4.3 %copy-start.7 = (f32[192]{0:T(256)S(1)}, f32[192]{0:T(256)}, u32[]{:S(2)}) copy-start(f32[192]{0:T(256)} %refs_4_.3) | copy-start | bytes 2308
  21.0 4.2 %copy-start.8 = (f32[768]{0:T(1024)S(1)}, f32[768]{0:T(1024)}, u32[]{:S(2)}) copy-start(f32[768]{0:T(1024)} %refs_5_.1) | copy-start | bytes 9220
  23.8 1.5 %collective-permute-start.5 = (bf16[2,32,384]{2,1,0:T(8,128)(2,1)S(1)}, bf16[2,32,384]{2,1,0:T(8,128)(2,1)S(1)}, u32[]{:S(2)}, u32[]{:S(2)}) collective-permute-start(bf16[2,32,384]{2,1,0:T(8,128)(2,1)S(1)} %slice_select_fusion), channel_id=1, source_target_pairs={{0,8},{8,0},{1,9},{9,1},{2,10},{10,2},{3,11},{11,3},{4,12},{12,4},... | collective-permute-start | bytes 147464 | tf_op jit(solution)/shard_map/ppermute | solution.py:425
